TPU v7x, 256 devices: a whole 4x4x8 slice. The times are simulated.
256 devices in a mesh: ctx: 16 (over y, z_lo, core), head: 16 (over x, z_hi).
Axes of the slice: x: 4, y: 4, z: 8 (z_hi: 4, z_lo: 2; z = z_hi * 2 + z_lo), core: 2. Of those that a mesh axis runs over, the one named last changes fastest.
Arguments:
- queries: bfloat16 [2048, 24576], P('ctx', 'head'), may hold values from -400 to 400
- latent: bfloat16 [2048, 576], P('ctx'), may hold values from -6 to 6
- w_uk: bfloat16 [512, 16384], P(None, 'head'), may hold values from -0.25 to 0.25
- w_uv: bfloat16 [512, 16384], P(None, 'head'), may hold values from -0.25 to 0.25
- grad_out: bfloat16 [2048, 16384], P('ctx', 'head'), may hold values from -6 to 6
- positions: int32 [2048], P('ctx'), may hold values from 0 to 2047, as said below
- tool_result: int32 [2048], P('ctx'), may hold values from 0 to 1
Outputs:
- grad_queries: bfloat16 [2048, 24576], P('ctx', 'head')
- grad_latent: float32 [2048, 576], P('ctx')
- grad_w_uk: float32 [512, 16384], P('ctx', 'head')
- grad_w_uv: float32 [512, 16384], P('ctx', 'head')
Inputs may be any that keep to these rules, and one draw needn't show every extreme that they name: Every number from 0 to 2047 appears once; each aligned run of 128 slots holds consecutive positions in increasing order.
All inputs are finite; a program needn't handle non-finite values.
Results may differ from a plain program's by a relative error of at most 0.0064.
Values may be sent and summed in bfloat16 or wider, within the bound.
No kernel may reach another device: no remote copies, remote signals or barrier semaphores. Data moves between devices by JAX's collectives and lax.ppermute only.
A program may use at most 128 MiB of HBM per device.

v0:
```python
import jax
import jax.numpy as jnp
from jax import lax
from jax.sharding import PartitionSpec as P

DR = 64
DN = 128
DV = 128


big_negative = -1e30


def block_scores(q_nope, q_rope, key_nope, key_rope, score_scale):
    scores = jnp.einsum("qhd,khd->hqk", q_nope, key_nope, preferred_element_type=jnp.float32)
    scores = scores + jnp.einsum(
        "qhd,kd->hqk", q_rope, key_rope, preferred_element_type=jnp.float32
    )
    return scores * score_scale


def local(queries, latent, w_uk, w_uv, grad_out, positions, tool_result):
    tok_count = queries.shape[0]
    latent_width = w_uk.shape[0]
    head_count = w_uk.shape[1] // DN
    blocks = lax.axis_size("ctx")
    score_scale = (DN + DR) ** (-0.5)
    q_three = queries.reshape(tok_count, head_count, DN + DR)
    q_nope = q_three[:, :, :DN]
    q_rope = q_three[:, :, DN:]
    keep_rows = (1 - tool_result).astype(jnp.bfloat16)
    cotangent = (grad_out * keep_rows[:, None]).reshape(tok_count, head_count, DV)
    lat_nope = latent[:, :latent_width]
    own_keys = jnp.dot(lat_nope, w_uk, preferred_element_type=jnp.float32).astype(jnp.bfloat16)
    own_values = jnp.dot(lat_nope, w_uv, preferred_element_type=jnp.float32).astype(jnp.bfloat16)
    all_keys, all_rope, all_values, all_pos = (
        lax.all_gather(own_keys, "ctx", axis=0, tiled=True),
        lax.all_gather(latent[:, latent_width:], "ctx", axis=0, tiled=True),
        lax.all_gather(own_values, "ctx", axis=0, tiled=True),
        lax.all_gather(positions, "ctx", axis=0, tiled=True),
    )
    stacked = (
        all_keys.reshape(blocks, tok_count, head_count, DN),
        all_rope.reshape(blocks, tok_count, DR),
        all_values.reshape(blocks, tok_count, head_count, DV),
        all_pos.reshape(blocks, tok_count),
    )

    def forward_step(state_now, key_block):
        key_nope, key_rope, values, key_pos = key_block
        visible = key_pos[None, :] <= positions[:, None]
        row_top, row_total, weighted = state_now
        scores = block_scores(q_nope, q_rope, key_nope, key_rope, score_scale)
        masked = jnp.where(visible[None], scores, big_negative)
        new_top = jnp.maximum(row_top, jnp.max(masked, axis=-1))
        shifted = jnp.where(visible[None], jnp.exp(scores - new_top[..., None]), 0.0)
        factor = jnp.exp(row_top - new_top)
        row_total = row_total * factor + jnp.sum(shifted, axis=-1)
        weighted = weighted * factor[..., None] + jnp.einsum(
            "hqk,khd->hqd", shifted, values.astype(jnp.float32), precision=lax.Precision.HIGHEST
        )
        state_now = (new_top, row_total, weighted)
        return (state_now, None)

    start_state = (
        jnp.full((head_count, tok_count), big_negative, jnp.float32),
        jnp.zeros((head_count, tok_count), jnp.float32),
        jnp.zeros((head_count, tok_count, DV), jnp.float32),
    )
    (row_top, row_total, weighted), _ = lax.scan(forward_step, start_state, stacked)
    log_total = row_top + jnp.log(row_total)
    attended = weighted / row_total[..., None]
    row_delta = jnp.sum(cotangent.astype(jnp.float32).transpose(1, 0, 2) * attended, axis=-1)

    def backward_step(state_now, key_block):
        key_nope, key_rope, values, key_pos = key_block
        visible = key_pos[None, :] <= positions[:, None]
        grad_nope, grad_rope = state_now
        scores = block_scores(q_nope, q_rope, key_nope, key_rope, score_scale)
        softmax_w = jnp.where(visible[None], jnp.exp(scores - log_total[..., None]), 0.0)
        grad_prob = jnp.einsum(
            "qhd,khd->hqk", cotangent, values, preferred_element_type=jnp.float32
        )
        dscore = (softmax_w * (grad_prob - row_delta[..., None])).astype(jnp.bfloat16)
        grad_nope = grad_nope + jnp.einsum(
            "hqk,khd->qhd", dscore, key_nope, preferred_element_type=jnp.float32
        )
        grad_rope = grad_rope + jnp.einsum(
            "hqk,kd->qhd", dscore, key_rope, preferred_element_type=jnp.float32
        )
        key_grad = (
            jnp.einsum("hqk,qhd->khd", dscore, q_nope, preferred_element_type=jnp.float32)
            * score_scale
        )
        rope_grad = (
            jnp.einsum("hqk,qhd->kd", dscore, q_rope, preferred_element_type=jnp.float32)
            * score_scale
        )
        value_grad = jnp.einsum(
            "hqk,qhd->khd",
            softmax_w.astype(jnp.bfloat16),
            cotangent,
            preferred_element_type=jnp.float32,
        )
        state_now = (grad_nope, grad_rope)
        block_grads = (
            key_grad.reshape(tok_count, head_count * DN),
            rope_grad,
            value_grad.reshape(tok_count, head_count * DV),
        )
        return (state_now, block_grads)

    start_grads = (
        jnp.zeros((tok_count, head_count, DN), jnp.float32),
        jnp.zeros((tok_count, head_count, DR), jnp.float32),
    )
    (grad_nope, grad_rope), (key_terms, rope_terms, value_terms) = lax.scan(
        backward_step, start_grads, stacked
    )
    grad_queries = (jnp.concatenate([grad_nope, grad_rope], axis=2) * score_scale).astype(
        jnp.bfloat16
    )
    grad_queries = grad_queries.reshape(tok_count, head_count * (DN + DR))
    key_every = key_terms.reshape(blocks * tok_count, head_count * DN)
    rope_every = rope_terms.reshape(blocks * tok_count, DR)
    value_every = value_terms.reshape(blocks * tok_count, head_count * DV)
    w_uk_float = w_uk.astype(jnp.float32)
    w_uv_float = w_uv.astype(jnp.float32)
    key_grads, rope_grads, value_grads = (
        lax.psum_scatter(key_every, "ctx", scatter_dimension=0, tiled=True),
        lax.psum_scatter(rope_every, "ctx", scatter_dimension=0, tiled=True),
        lax.psum_scatter(value_every, "ctx", scatter_dimension=0, tiled=True),
    )
    grad_lat_nope = jnp.dot(key_grads, w_uk_float.T, precision=lax.Precision.HIGHEST)
    grad_lat_nope = grad_lat_nope + jnp.dot(
        value_grads, w_uv_float.T, precision=lax.Precision.HIGHEST
    )
    latent_part = jnp.concatenate([grad_lat_nope, rope_grads], axis=1)
    lat_float = lat_nope.astype(jnp.float32)
    weight_key = jnp.dot(lat_float.T, key_grads, precision=lax.Precision.HIGHEST)
    weight_value = jnp.dot(lat_float.T, value_grads, precision=lax.Precision.HIGHEST)
    grad_latent = lax.psum(latent_part, "head")
    grad_w_uk, grad_w_uv = (
        lax.psum_scatter(weight_key, "ctx", scatter_dimension=0, tiled=True),
        lax.psum_scatter(weight_value, "ctx", scatter_dimension=0, tiled=True),
    )
    return (grad_queries, grad_latent, grad_w_uk, grad_w_uv)


def solution(mesh):
    placed = (
        P("ctx", "head"),
        P("ctx", None),
        P(None, "head"),
        P(None, "head"),
        P("ctx", "head"),
        P("ctx"),
        P("ctx"),
    )
    return jax.shard_map(
        local,
        mesh=mesh,
        in_specs=placed,
        out_specs=(P("ctx", "head"), P("ctx", None), P("ctx", "head"), P("ctx", "head")),
        check_vma=False,
    )
```

profile of v0, /device:TPU:2, one launch (start us, length us, event | category | flops | bytes accessed | tf_op | source)
XLA Modules:
  0.0 952.5 jit_solution(11524760763761317401)
XLA Ops:
  8.5 1.9 convolution_convert_fusion.1
  10.5 2.3 convolution_convert_fusion
  14.7 21.0 %all-gather = s32[16,1,128]{2,1,0:T(1,128)} all-gather(s32[1,1,128]{2,1,0:T(1,128)} %bitcast), channel_id=1, replica_groups=mesh['ctx'=16,'head'=16] {'ctx'}, dimensions={0}, use_global_device_ids=true | all-gather | bytes 8704 | tf_op jit(solution)/shard_map/all_gather | solution.py:40
  35.7 18.7 %all_gather.14 = bf16[2048,64]{0,1:T(8,128)(2,1)S(1)} all-gather(bf16[128,64]{0,1:T(8,128)(2,1)S(1)} %slice-done), channel_id=1, replica_groups=mesh['ctx'=16,'head'=16] {'ctx'}, dimensions={0}, use_global_device_ids=true | all-gather | bytes 278528 | tf_op jit(solution)/shard_map/all_gather | solution.py:38
  55.2 3.3 copy.104
  58.5 3.2 copy.75
  61.7 34.8 %all-gather.6.cloned.1.call-done = bf16[2048,1024]{1,0:T(8,128)(2,1)} async-done(((bf16[128,1024]{1,0:T(8,128)(2,1)}), bf16[2048,1024]{1,0:T(8,128)(2,1)}) %all-gather.6.cloned.1.call-update) | async-done | bytes 4194320 | tf_op jit(solution)/shard_map/all_gather | solution.py:39
  96.5 3.3 copy.105
  99.8 3.2 copy.72
  103.0 89.0 %while.34 = (s32[]{:T(128)}, f32[8,128]{1,0:T(8,128)S(1)}, f32[8,128]{1,0:T(8,128)S(1)}, f32[8,128,128]{2,1,0:T(8,128)S(1)}, s32[16,128]{1,0:T(8,128)}, /*index=...) while((s32[]{:T(128)}, f32[8,128]{1,0:T(8,128)S(1)}, ...), condition=%wide.region_3.4_spmd.clone, body=%wide.region_0.3_spmd.clone.sunk | while | flops 253252608 | bytes 4737185 | solution.py:70
  106.8 1.7 convolution_add_fusion.3
  112.4 1.7 convolution_add_fusion.3
  129.1 1.7 convolution_add_fusion.3
  134.6 1.7 convolution_add_fusion.3
  156.9 1.7 convolution_add_fusion.3
  162.5 1.7 convolution_add_fusion.3
  184.7 1.7 convolution_add_fusion.3
  190.3 1.7 convolution_add_fusion.3
  192.3 188.1 %while.35 = (s32[]{:T(128)}, f32[128,8,128]{0,2,1:T(8,128)}, f32[128,8,64]{0,2,1:T(8,128)}, f32[16,128,1024]{2,1,0:T(8,128)}, f32[16,128,64]{1,2,0:T(8,128)}, /*...) while((s32[]{:T(128)}, f32[128,8,128]{0,2,1:T(8,128)}, ...), condition=%wide.region_6.7_spmd.clone, body=%wide.region_5.6_spmd.clone.sunk | while | flops 219701248 | bytes 12953816 | solution.py:117
  199.3 2.1 fusion.133
  209.1 1.9 fusion.134
  210.9 2.2 fusion.133
  220.8 1.9 fusion.134
  222.7 2.2 fusion.133
  232.6 1.9 fusion.134
  234.5 2.2 fusion.133
  244.4 1.9 fusion.134
  246.2 2.2 fusion.133
  256.2 1.9 fusion.134
  258.0 2.2 fusion.133
  268.0 1.9 fusion.134
  269.8 2.2 fusion.133
  279.7 1.9 fusion.134
  281.6 2.2 fusion.133
  291.5 1.9 fusion.134
  293.3 2.2 fusion.133
  303.3 1.9 fusion.134
  305.1 2.2 fusion.133
  315.1 1.9 fusion.134
  316.9 2.2 fusion.133
  326.8 1.9 fusion.134
  328.7 2.2 fusion.133
  338.6 1.9 fusion.134
  340.4 2.2 fusion.133
  350.4 1.9 fusion.134
  352.2 2.2 fusion.133
  362.1 1.9 fusion.134
  364.0 2.2 fusion.133
  373.9 1.9 fusion.134
  375.8 2.2 fusion.133
  381.1 2.4 copy.80
  383.6 97.4 %reduce-scatter.10.cloned.1.call-done = f32[128,1024]{1,0:T(8,128)} async-done(((f32[2048,1024]{1,0:T(8,128)}), f32[128,1024]{1,0:T(8,128)}) %reduce-scatter.10.cloned.1.call-update) | async-done | bytes 524304 | tf_op jit(solution)/shard_map/reduce_scatter | solution.py:130
  481.0 2.2 fusion.55
  483.2 99.1 %reduce-scatter.12.cloned.1.call-done = f32[128,1024]{1,0:T(8,128)} async-done(((f32[2048,1024]{1,0:T(8,128)}), f32[128,1024]{1,0:T(8,128)}) %reduce-scatter.12.cloned.1.call-update) | async-done | bytes 524304 | tf_op jit(solution)/shard_map/reduce_scatter | solution.py:132
  582.3 2.2 convolution_add_fusion.1
  584.5 62.7 %reduce-scatter.14.cloned.1.call-done = f32[128,64]{1,0:T(8,128)} async-done(((f32[2048,64]{1,0:T(8,128)}), f32[128,64]{1,0:T(8,128)}) %reduce-scatter.14.cloned.1.call-update) | async-done | bytes 32784 | tf_op jit(solution)/shard_map/reduce_scatter | solution.py:131
  648.8 2.1 convolution_bitcast_fusion.7
  650.9 1.9 copy.96
  652.9 2.1 convolution_bitcast_fusion.8
  654.9 1.8 copy.94
  658.9 150.1 %all-reduce.2.cloned.1.call-done = f32[128,576]{1,0:T(8,128)} async-done(((f32[128,576]{1,0:T(8,128)}), f32[128,576]{1,0:T(8,128)}) %all-reduce.2.cloned.1.call-update) | async-done | bytes 294928 | tf_op jit(solution)/shard_map/psum | solution.py:142
  809.1 1.8 copy.82
  810.9 66.4 %reduce-scatter.18.cloned.1.call-done = f32[32,1024]{1,0:T(8,128)} async-done(((f32[512,1024]{1,0:T(8,128)}), f32[32,1024]{1,0:T(8,128)}) %reduce-scatter.18.cloned.1.call-update) | async-done | bytes 131088
  877.3 68.3 %reduce-scatter.16.cloned.1.call-done = f32[32,1024]{1,0:T(8,128)} async-done(((f32[512,1024]{1,0:T(8,128)}), f32[32,1024]{1,0:T(8,128)}) %reduce-scatter.16.cloned.1.call-update) | async-done | bytes 131088
  (364 shorter events, 206.8 us)
Async XLA Ops:
  7.2 1.3 copy-start
  7.2 28.6 %slice-start = ((bf16[128,576]{0,1:T(8,128)(2,1)}), bf16[128,64]{0,1:T(8,128)(2,1)S(1)}, s32[]{:S(2)}) async-start(bf16[128,576]{0,1:T(8,128)(2,1)} %param.12), calls=%async_computation.13 | async-start | bytes 32768 | tf_op jit(solution)/shard_map/slice | solution.py:38
  7.2 7.1 copy-start.4
  7.2 7.1 copy-start.3
  7.2 48.0 %all-gather.4.cloned.1.call-start = ((), (), s32[]{:S(2)}) async-start(), calls=%async_computation.5 | async-start | bytes 4456448 | tf_op jit(solution)/shard_map/all_gather | solution.py:37
  10.5 86.0 %all-gather.6.cloned.1.call-start = ((), (), s32[]{:S(2)}) async-start(), calls=%async_computation.6 | async-start | bytes 4456448 | tf_op jit(solution)/shard_map/all_gather | solution.py:39
  12.9 468.1 %reduce-scatter.10.cloned.1.call-start = ((), (), s32[]{:S(2)}) async-start(), calls=%async_computation.7 | async-start | bytes 8912896 | tf_op jit(solution)/shard_map/reduce_scatter | solution.py:130
  380.4 201.9 %reduce-scatter.12.cloned.1.call-start = ((), (), s32[]{:S(2)}) async-start(), calls=%async_computation.8 | async-start | bytes 8912896 | tf_op jit(solution)/shard_map/reduce_scatter | solution.py:132
  381.0 201.3 %copy-start.1 = (bf16[512,1024]{1,0:T(8,128)(2,1)S(1)}, bf16[512,1024]{1,0:T(8,128)(2,1)}, u32[]{:S(2)}) copy-start(bf16[512,1024]{1,0:T(8,128)(2,1)} %param.14) | copy-start | bytes 3145732
  381.0 267.8 %copy-start.2 = (bf16[128,576]{0,1:T(8,128)(2,1)S(1)}, bf16[128,576]{0,1:T(8,128)(2,1)}, u32[]{:S(2)}) copy-start(bf16[128,576]{0,1:T(8,128)(2,1)} %param.12) | copy-start | bytes 442372
  381.0 266.2 %reduce-scatter.14.cloned.1.call-start = ((), (), s32[]{:S(2)}) async-start(), calls=%async_computation.9 | async-start | bytes 1114112 | tf_op jit(solution)/shard_map/reduce_scatter | solution.py:131
  383.5 425.6 %all-reduce.2.cloned.1.call-start = ((), (), s32[]{:S(2)}) async-start(), calls=%async_computation.10 | async-start | bytes 655360 | tf_op jit(solution)/shard_map/psum | solution.py:142
  648.8 228.5 %reduce-scatter.18.cloned.1.call-start = ((), (), s32[]{:S(2)}) async-start(), calls=%async_computation.12 | async-start | bytes 2228224
  652.8 292.8 %reduce-scatter.16.cloned.1.call-start = ((), (), s32[]{:S(2)}) async-start(), calls=%async_computation.11 | async-start | bytes 2228224
Sparse Core Ops, SparseCore 0:
  10.6 44.4 all-gather.3
  56.9 39.5 all-gather.5
  380.5 100.3 reduce-scatter.9
  483.4 98.8 reduce-scatter.11
  584.7 62.4 reduce-scatter.13
  649.9 159.1 all-reduce.1
  812.2 65.0 reduce-scatter.17
  880.4 65.1 reduce-scatter.15
where the time goes:
time: 959 us; the launch traced here: 952 us
  waiting for transfers between devices  580 us (60%)
  matrix products  217 us (23%)
  local copies, waits for them, and re-layouts  70.9 us (7%)
  blocking collectives  39.7 us (4%)
  other arithmetic  28.5 us (3%)
  between operations  14.4 us (2%)
    psum x1, waiting for transfers between devices, local(): grad_latent = lax.psum(latent_part, 'head')  150 us
    unnamed x10, waiting for transfers between devices  135 us
    reduce_scatter x1, waiting for transfers between devices, local(): lax.psum_scatter(value_every, 'ctx', scatter_dimension=0, tiled=True)  99.1 us
    reduce_scatter x1, waiting for transfers between devices, local(): lax.psum_scatter(key_every, 'ctx', scatter_dimension=0, tiled=True)  97.4 us
    reduce_scatter x1, waiting for transfers between devices, local(): lax.psum_scatter(rope_every, 'ctx', scatter_dimension=0, tiled=True)  62.7 us
    dot_general x32, matrix products, block_scores(): jnp.einsum('qhd,khd->hqk', q_nope, key_nope, preferred_element_type=jnp.f...  38.6 us
    dot_general x16, matrix products, backward_step(): jnp.einsum('hqk,khd->qhd', dscore, key_nope, preferred_element_type=jnp.f...  35.6 us
    all_gather x1, waiting for transfers between devices, local(): lax.all_gather(own_values, 'ctx', axis=0, tiled=True)  34.8 us
  transfers between devices with their start and end apart: 8, of which 7 were waited for; matrix products, arithmetic and copies ran while one was open for 3% of the time, Pallas kernels for 0%

commit v1 on v0

v1 whole, which is shorter than its diff:
```python
import functools
import math

import jax
import jax.numpy as jnp
from jax import lax
from jax.experimental import pallas as pl
from jax.experimental.pallas import tpu as pltpu
from jax.sharding import PartitionSpec as P

DL = 512
DR = 64
DN = 128
DV = 128
TOK = 128
HALF = TOK // 2
ROWS = 464
BACK = 320
CHUNK = 512
MASKED = -1e30
BF = jnp.bfloat16
F32 = jnp.float32


def dot(a, b):
    return lax.dot_general(a, b, (((1,), (0,)), ((), ())), preferred_element_type=F32)


def dot_nt(a, b):
    return lax.dot_general(a, b, (((1,), (1,)), ((), ())), preferred_element_type=F32)


def low_lanes(shape):
    return lax.broadcasted_iota(jnp.int32, shape, len(shape) - 1) < DR


def pack_kernel(q_ref, lat_ref, g_ref, pos_ref, tool_ref, out_ref, lat_s, rope_s, keep_s):
    @pl.when(pl.program_id(0) == 0)
    def _():
        lat_s[...] = lat_ref[:DL, :].astype(F32).T.astype(BF)
        rope = jnp.concatenate([jnp.zeros((DR, TOK), F32), lat_ref[DL:, :].astype(F32)], axis=0)
        rope_s[...] = rope.T
        keep = (1 - tool_ref[...]).astype(F32)
        keep_s[...] = jnp.broadcast_to(keep, (TOK, TOK)).T

    low = low_lanes((TOK, TOK))
    rope = rope_s[...]
    mid = pltpu.roll(q_ref[:, 128:256].astype(F32), DR, 1)
    end = pltpu.roll(q_ref[:, 256:384].astype(F32), DR, 1)
    nope = [q_ref[:, 0:128], jnp.where(low, mid, end).astype(BF)]
    ropes = [
        jnp.where(low, q_ref[:, 128:256].astype(F32), rope).astype(BF),
        jnp.where(low, end, rope).astype(BF),
    ]
    order = jnp.broadcast_to((pos_ref[...] // TOK).astype(F32), (16, TOK)).astype(BF)
    for h in range(2):
        cols = slice(h * 128, h * 128 + 128)
        cotangent = (g_ref[:, cols].astype(F32) * keep_s[...]).astype(BF)
        for c in range(2):
            rows = slice(c * HALF, c * HALF + HALF)
            to = 2 * h + c
            for t in range(4):
                out_ref[to, t * HALF : (t + 1) * HALF, :] = lat_s[rows, t * 128 : (t + 1) * 128]
            out_ref[to, 256:320, :] = ropes[h][rows]
            out_ref[to, 320:384, :] = nope[h][rows]
            out_ref[to, 384:448, :] = cotangent[rows]
            out_ref[to, 448:464, :] = order


def pack(queries, lat_t, grad_out, positions, tool_result):
    return pl.pallas_call(
        pack_kernel,
        grid=(4,),
        in_specs=[
            pl.BlockSpec((TOK, 384), lambda i: (0, i)),
            pl.BlockSpec((DL + DR, TOK), lambda i: (0, 0)),
            pl.BlockSpec((TOK, 256), lambda i: (0, i)),
            pl.BlockSpec((1, TOK), lambda i: (0, 0)),
            pl.BlockSpec((1, TOK), lambda i: (0, 0)),
        ],
        out_specs=pl.BlockSpec((4, ROWS, 128), lambda i: (i, 0, 0)),
        out_shape=jax.ShapeDtypeStruct((16, ROWS, 128), BF),
        scratch_shapes=[
            pltpu.VMEM((TOK, DL), BF),
            pltpu.VMEM((TOK, TOK), F32),
            pltpu.VMEM((TOK, TOK), F32),
        ],
        compiler_params=pltpu.CompilerParams(vmem_limit_bytes=60 << 20),
    )(queries, lat_t, grad_out, positions.reshape(1, TOK), tool_result.reshape(1, TOK))


def attend_kernel(ord_ref, own_ref, oth_ref, uk_ref, uv_ref, keep_out, give_out, dq_out, rope_out,
                  lat, met, weights, kv, ts, kt, qs, cs, s_sc, g_sc, ds_sc, kvg, dr, dqs, sems):
    scale = (DN + DR) ** -0.5
    me = lax.axis_index("ctx")
    core = lax.rem(me, 2)
    columns = pl.ds(pl.multiple_of((me // 2) * 128, 128), 128)

    def fetch(src, dst, sem):
        pltpu.make_async_copy(src, dst, sems.at[sem]).start()

    def arrive(ref, sem):
        pltpu.make_async_copy(ref, ref, sems.at[sem]).wait()

    fetch(uk_ref.at[:, columns], weights.at[:, 0:128], 0)
    fetch(uv_ref.at[:, columns], weights.at[:, 128:256], 1)
    for s in range(16):
        fetch(own_ref.at[s, 0:320, :], lat.at[ord_ref[s] * 2 + core], 2)
        fetch(oth_ref.at[s, 0:320, :], lat.at[ord_ref[s] * 2 + 1 - core], 2)
        fetch(own_ref.at[s, 320:448, :], met.at[ord_ref[s]], 3)
    arrive(weights.at[:, 0:128], 0)
    arrive(weights.at[:, 128:256], 1)
    arrive(lat, 2)
    arrive(met, 3)

    low = low_lanes((HALF, TOK))
    for b in range(16):
        rows = slice(b * HALF, (b + 1) * HALF)
        turned = pltpu.roll(lat[2 * b + core, 256:320, :].astype(F32), DR, 1)
        qs[rows, 0:128] = met[b, 0:64, :]
        qs[rows, 128:256] = jnp.where(low, 0.0, turned).astype(BF)
        cs[rows, :] = met[b, 64:128, :]
    for b in range(8):
        rows = slice(b * 256, b * 256 + 256)
        four = range(4 * b, 4 * b + 4)
        tokens = jnp.concatenate(
            [jnp.concatenate([lat[i, t * HALF : (t + 1) * HALF, :] for t in range(4)], axis=1) for i in four], axis=0
        )
        both = dot(tokens, weights[...])
        rope = jnp.concatenate([lat[i, 256:320, :] for i in four], axis=0)
        keys = both[:, 0:128].astype(BF)
        kv[0, rows, :] = keys
        kv[1, rows, :] = both[:, 128:256].astype(BF)
        ts[rows, :] = rope
        kt[0:128, rows] = keys.astype(F32).T.astype(BF)
        kt[128:256, rows] = rope.astype(F32).T.astype(BF)

    factor = scale * math.log2(math.e)
    lane = lax.broadcasted_iota(jnp.int32, (CHUNK, 256), 1)
    qpos = (lane // HALF) * TOK + core * HALF + lax.rem(lane, HALF)
    visible = lax.broadcasted_iota(jnp.int32, (CHUNK, 256), 0) <= qpos
    for p in range(4):
        rows = slice(p * 256, p * 256 + 256)
        chunks = [slice(c * CHUNK, (c + 1) * CHUNK) for c in range(p + 1)]
        top = jnp.full((8, 256), MASKED, F32)
        for c, at in enumerate(chunks):
            s = dot_nt(jnp.concatenate([kv[0, at, :], ts[at, :]], axis=1), qs[rows, :]) * factor
            if c == p:
                s = jnp.where(visible, s, MASKED)
            s_sc[at, :] = s
            g_sc[at, :] = dot_nt(kv[1, at, :], cs[rows, :])
            top = jnp.maximum(top, jnp.max(s.reshape(CHUNK // 8, 8, 256), axis=0))
        top = jnp.max(top, axis=0, keepdims=True)
        total = jnp.zeros((8, 256), F32)
        mixed = jnp.zeros((8, 256), F32)
        for at in chunks:
            e = jnp.exp2(s_sc[at, :] - top)
            s_sc[at, :] = e
            total = total + jnp.sum(e.reshape(CHUNK // 8, 8, 256), axis=0)
            mixed = mixed + jnp.sum((e * g_sc[at, :]).reshape(CHUNK // 8, 8, 256), axis=0)
        share = 1.0 / jnp.sum(total, axis=0, keepdims=True)
        delta = jnp.sum(mixed, axis=0, keepdims=True) * share
        for c, at in enumerate(chunks):
            prob = s_sc[at, :] * share
            ds = (prob * (g_sc[at, :] - delta)).astype(BF)
            ds_sc[at, :] = ds
            key_part = dot(ds, qs[rows, :])
            value_part = dot(prob.astype(BF), cs[rows, :])
            if c == p:
                kvg[0, at, :] = key_part[:, 0:128]
                dr[at, :] = key_part[:, 128:256]
                kvg[1, at, :] = value_part
            else:
                kvg[0, at, :] += key_part[:, 0:128]
                dr[at, :] += key_part[:, 128:256]
                kvg[1, at, :] += value_part
        upto = (p + 1) * CHUNK
        dqs[rows, :] = (dot(kt[:, 0:upto], ds_sc[0:upto, :]) * scale).T

    keep_scale = jnp.where(core == 0, scale, 1.0)
    give_scale = jnp.where(core == 0, 1.0, scale)
    for s in range(16):
        at = pl.ds(pl.multiple_of(ord_ref[s] * TOK, TOK), TOK)
        of = pl.ds(pl.multiple_of(ord_ref[s] * HALF, HALF), HALF)
        keep_out[s, :, :] = (kvg[core, at, :] * keep_scale).astype(BF)
        give_out[s, :, :] = (kvg[1 - core, at, :] * give_scale).astype(BF)
        dq_out[s, :, :] = dqs[of, 0:128].astype(BF)
        rope = dr[at, :] * scale
        turned = pltpu.roll(dqs[of, 128:256], DR, 1)
        rope_out[s, 0:64, :] = jnp.where(low, turned, rope[0:64]).astype(BF)
        rope_out[s, 64:128, :] = rope[64:128].astype(BF)


def attend(orders, own, other, w_uk, w_uv):
    whole = pl.BlockSpec(memory_space=pltpu.VMEM)
    anywhere = pl.BlockSpec(memory_space=pl.ANY)
    return pl.pallas_call(
        attend_kernel,
        in_specs=[pl.BlockSpec(memory_space=pltpu.SMEM), anywhere, anywhere, anywhere, anywhere],
        out_specs=[whole, whole, whole, whole],
        out_shape=[
            jax.ShapeDtypeStruct((16, TOK, 128), BF),
            jax.ShapeDtypeStruct((16, TOK, 128), BF),
            jax.ShapeDtypeStruct((16, HALF, 128), BF),
            jax.ShapeDtypeStruct((16, TOK, 128), BF),
        ],
        scratch_shapes=[
            pltpu.VMEM((32, 320, 128), BF),
            pltpu.VMEM((16, 128, 128), BF),
            pltpu.VMEM((DL, 256), BF),
            pltpu.VMEM((2, 2048, 128), BF),
            pltpu.VMEM((2048, 128), BF),
            pltpu.VMEM((256, 2048), BF),
            pltpu.VMEM((1024, 256), BF),
            pltpu.VMEM((1024, 128), BF),
            pltpu.VMEM((2048, 256), F32),
            pltpu.VMEM((2048, 256), F32),
            pltpu.VMEM((2048, 256), BF),
            pltpu.VMEM((2, 2048, 128), F32),
            pltpu.VMEM((2048, 128), F32),
            pltpu.VMEM((1024, 256), F32),
            pltpu.SemaphoreType.DMA((4,)),
        ],
        compiler_params=pltpu.CompilerParams(vmem_limit_bytes=32 << 20),
    )(orders, own, other, w_uk, w_uv)


def finish_kernel(keep_ref, met_ref, dq_ref, rope_ref, own_ref, oth_ref, out_ref):
    core = lax.rem(lax.axis_index("ctx"), 2)
    total = jnp.zeros((128, DL), F32)
    for i in range(0, 16, 2):
        pair = (keep_ref[i : i + 2].astype(F32) + met_ref[i : i + 2].astype(F32)).astype(BF)
        out_ref[i : i + 2, 0:128, :] = pair
        out_ref[i : i + 2, 128:192, :] = dq_ref[i : i + 2]
        pair = pair.astype(F32).reshape(4, HALF, 128)
        grads = [jnp.where(core == c, pair[j], pair[j + 1]) for c in range(2) for j in (0, 2)]
        grads = jnp.concatenate(grads, axis=0)
        lat = jnp.concatenate(
            [
                jnp.concatenate([ref[j, t * HALF : (t + 1) * HALF, :] for t in range(4)], axis=1)
                for ref in (own_ref, oth_ref)
                for j in (i, i + 1)
            ],
            axis=0,
        )
        total = total + dot(grads.T.astype(BF), lat)
    total = total.T
    turned = pltpu.roll(total, DR, 1)
    low = low_lanes((32, TOK))
    for i in range(16):
        out_ref[i, 192:256, :] = rope_ref[i, 0:64, :]
        for part, first in ((total, 64), (turned, 96)):
            rope = rope_ref[i, first : first + 32, :].astype(F32)
            mine = jnp.where(low, part[i * 32 : i * 32 + 32], rope)
            out_ref[i, 192 + first : 224 + first, :] = mine.astype(BF)


def finish(keep, met, dq, rope, own, other):
    whole = pl.BlockSpec(memory_space=pltpu.VMEM)
    return pl.pallas_call(
        finish_kernel,
        in_specs=[whole] * 6,
        out_specs=whole,
        out_shape=jax.ShapeDtypeStruct((16, BACK, 128), BF),
        compiler_params=pltpu.CompilerParams(vmem_limit_bytes=16 << 20),
    )(keep, met, dq, rope, own, other)


def latent_kernel(r_ref, uk_ref, uv_ref, out_ref):
    keys = jnp.concatenate([r_ref[i, 0:128, :] for i in range(0, 16, 2)], axis=1)
    values = jnp.concatenate([r_ref[i, 0:128, :] for i in range(1, 16, 2)], axis=1)
    out_ref[:DL, :] = (dot_nt(uk_ref[...], keys) + dot_nt(uv_ref[...], values)).astype(BF)
    rope = r_ref[0, 192:320, :].astype(F32)
    for i in range(1, 16):
        rope = rope + r_ref[i, 192:320, :].astype(F32)
    turned = rope.T
    out_ref[DL:, :] = jnp.concatenate([turned[DR:, :], jnp.zeros((DR, TOK), F32)], axis=0).astype(BF)


def latent_terms(received, w_uk, w_uv):
    whole = pl.BlockSpec(memory_space=pltpu.VMEM)
    return pl.pallas_call(
        latent_kernel,
        in_specs=[whole] * 3,
        out_specs=whole,
        out_shape=jax.ShapeDtypeStruct((DL + 2 * DR, TOK), BF),
        compiler_params=pltpu.CompilerParams(vmem_limit_bytes=16 << 20),
    )(received, w_uk, w_uv)


def unpack_kernel(r_ref, q_ref, uk_ref, uv_ref):
    low = low_lanes((HALF, TOK))
    for h in range(0, 8, 2):
        for c in range(2):
            rows = slice(c * HALF, c * HALF + HALF)
            i, j, at = 2 * h + c, 2 * h + 2 + c, h * 192
            q_ref[rows, at : at + 128] = r_ref[i, 128:192, :]
            first = r_ref[i, 192:256, :].astype(F32)
            second = pltpu.roll(r_ref[j, 192:256, :].astype(F32), DR, 1)
            turned = pltpu.roll(r_ref[j, 128:192, :].astype(F32), DR, 1)
            q_ref[rows, at + 128 : at + 256] = jnp.where(low, first, turned).astype(BF)
            q_ref[rows, at + 256 : at + 384] = jnp.where(low, turned, second).astype(BF)
    for i in range(16):
        left = r_ref[i, 256:288, :].astype(F32)
        right = pltpu.roll(r_ref[i, 288:320, :].astype(F32), DR, 1)
        ref = uv_ref if i % 2 else uk_ref
        ref[:, (i // 2) * 128 : (i // 2) * 128 + 128] = jnp.where(low[0:32], left, right)


def unpack(received):
    whole = pl.BlockSpec(memory_space=pltpu.VMEM)
    return pl.pallas_call(
        unpack_kernel,
        in_specs=[whole],
        out_specs=[whole] * 3,
        out_shape=[
            jax.ShapeDtypeStruct((TOK, 1536), BF),
            jax.ShapeDtypeStruct((32, 1024), F32),
            jax.ShapeDtypeStruct((32, 1024), F32),
        ],
        compiler_params=pltpu.CompilerParams(vmem_limit_bytes=16 << 20),
    )(received)


def local(queries, latent, w_uk, w_uv, grad_out, positions, tool_result):
    every = [list(range(16))]
    swap = [(i, i ^ 1) for i in range(16)]

    def exchange(x, axis):
        return lax.all_to_all(x, axis, 0, 0, tiled=True, axis_index_groups=every)

    lat_t = latent.T
    own = exchange(pack(queries, lat_t, grad_out, positions, tool_result), "ctx")
    other = lax.ppermute(own, "ctx", swap)
    orders = own[:, 448, 0].astype(jnp.int32)
    keep, give, dq, rope = attend(orders, own, other, w_uk, w_uv)
    met = lax.ppermute(give, "ctx", swap)
    received = exchange(finish(keep, met, dq, rope, own, other), "ctx")
    terms = latent_terms(received, w_uk, w_uv)
    met_terms = exchange(terms.reshape(16, 40, TOK), "head")
    summed = jnp.sum(met_terms.astype(F32), axis=0).astype(BF)
    spread = exchange(jnp.broadcast_to(summed[None], (16, 40, TOK)), "head")
    grad_latent = spread.reshape(640, TOK)[: DL + DR].astype(F32).T
    grad_queries, grad_w_uk, grad_w_uv = unpack(received)
    return (grad_queries, grad_latent, grad_w_uk, grad_w_uv)


def solution(mesh):
    placed = (
        P("ctx", "head"),
        P("ctx", None),
        P(None, "head"),
        P(None, "head"),
        P("ctx", "head"),
        P("ctx"),
        P("ctx"),
    )
    return jax.shard_map(
        local,
        mesh=mesh,
        in_specs=placed,
        out_specs=(P("ctx", "head"), P("ctx", None), P("ctx", "head"), P("ctx", "head")),
        check_vma=False,
    )
```

time: 959 us -> 114 us (0.12)
  waiting for transfers between devices: 580 us -> 13.2 us
  matrix products: 217 us -> 0 us
  local copies, waits for them, and re-layouts: 70.9 us -> 0.7 us
  blocking collectives: 39.7 us -> 72.9 us
  other arithmetic: 28.5 us -> 1.14 us
  Pallas kernels: 0 us -> 18.3 us
  between operations: 14.4 us -> 0.66 us
    reduce_scatter x3 -> x0, waiting for transfers between devices: 259 us -> none  [the longest x1 99.1 us: local(): lax.psum_scatter(value_every, 'ctx', scatter_dimension=0, tiled=True)]
    dot_general x182 -> x0, matrix products: 217 us -> none  [the longest x32 38.6 us: block_scores(): jnp.einsum('qhd,khd->hqk', q_nope, key_nope, preferred_element_type=jnp.f...]
    psum x1 -> x0, waiting for transfers between devices: 150 us -> none  [local(): grad_latent = lax.psum(latent_part, 'head')]
    unnamed x10 -> x0, waiting for transfers between devices: 135 us -> none
    all_to_all x0 -> x3, blocking collectives: none -> 72.9 us  [exchange(): return lax.all_to_all(x, axis, 0, 0, tiled=True, axis_index_groups=every)]
    all_gather x2 -> x0, blocking collectives: 39.7 us -> none  [the longest x1 21 us: local(): lax.all_gather(positions, 'ctx', axis=0, tiled=True)]
    all_gather x2 -> x0, waiting for transfers between devices: 34.8 us -> none  [the longest x1 34.8 us: local(): lax.all_gather(own_values, 'ctx', axis=0, tiled=True)]
    le x32 -> x0, other arithmetic: 23.6 us -> none  [the longest x16 11.8 us: forward_step(): visible = key_pos[None, :] <= positions[:, None]]
  transfers between devices with their start and end apart: 8 -> 3, of which waited for: 7 -> 3; matrix products, arithmetic and copies ran while one was open for 3% -> 0% of each run, Pallas kernels for 0% -> 1%
where the time goes in v1:
time: 114 us; the launch traced here: 113 us
  blocking collectives  72.9 us (64%)
  Pallas kernels  18.3 us (16%)
  waiting for transfers between devices  13.2 us (12%)
  starting transfers between devices  6 us (5%)
    all_to_all x3, blocking collectives, exchange(): return lax.all_to_all(x, axis, 0, 0, tiled=True, axis_index_groups=every)  72.9 us
    pallas_call x1, Pallas kernels, attend(): pl.pallas_call(attend_kernel, in_specs=[pl.BlockSpec(memory_space=pltpu.S...  12.1 us
    all_to_all x1, waiting for transfers between devices, exchange(): return lax.all_to_all(x, axis, 0, 0, tiled=True, axis_index_groups=every)  7.9 us
    all_to_all x1, starting transfers between devices, exchange(): return lax.all_to_all(x, axis, 0, 0, tiled=True, axis_index_groups=every)  5.78 us
    pallas_call x1, Pallas kernels, pack(): pl.pallas_call(pack_kernel, grid=(4,), in_specs=[pl.BlockSpec((TOK, 384),...  3.81 us
    ppermute x1, waiting for transfers between devices, local(): other = lax.ppermute(own, 'ctx', swap)  3.5 us
  transfers between devices with their start and end apart: 3, of which 3 were waited for; matrix products, arithmetic and copies ran while one was open for 0% of the time, Pallas kernels for 1%

profile of v1, /device:TPU:2, one launch (start us, length us, event | category | flops | bytes accessed | tf_op | source)
XLA Modules:
  0.0 112.8 jit_solution(7920398149610123744)
XLA Ops:
  0.6 3.8 %shard_map.102 = bf16[16,464,128]{2,1,0:T(8,128)(2,1)} custom-call(bf16[128,1536]{1,0:T(8,128)(2,1)} %q_ref.1, bf16[576,128]{1,0:T(8,128)(2,1)} %bitcast.9, bf16[128,1024]{1,0:T(8,128)(2,1)} %g_ref.1, s32[1,128]{1,0:T(1,128)} %bitcast.10, s32[1,128]{1,0:T(1,128)} %bitcast.11), custom_call_target="tpu_custom_call" | custom-call | tf_op jit(solution)/shard_map/pallas_call | solution.py:71
  4.4 0.0 copy-start
  4.4 0.0 copy-start.1
  4.5 31.7 %all_to_all.20.own_ref = bf16[16,464,128]{2,1,0:T(8,128)(2,1)S(1)} all-to-all(bf16[16,464,128]{2,1,0:T(8,128)(2,1)} %shard_map.102), channel_id=1, replica_groups={{0,16,32,48,64,80,96,112,128,144,160,176,192,208,224,240},{1,17,33,49,6..., dimensions={0} | all-to-all | bytes 3801088 | tf_op jit(solution)/shard_map/all_to_all | solution.py:330
  36.1 0.0 collective-permute-start
  36.1 0.4 fusion.ord_ref
  36.5 3.5 %collective-permute-done.oth_ref = bf16[16,464,128]{2,1,0:T(8,128)(2,1)S(1)} collective-permute-done((bf16[16,464,128]{2,1,0:T(8,128)(2,1)S(1)}, bf16[16,464,128]{2,1,0:T(8,128)(2,1)S(1)}, u32[]{:S(2)}, u32[]{:S(2)}) %collective-permute-start) | collective-permute-done | bytes 1900576 | tf_op jit(solution)/shard_map/ppermute | solution.py:334
  40.0 0.0 copy-done
  40.0 0.0 copy-done.1
  40.0 12.1 %shard_map.103 = (bf16[16,128,128]{2,1,0:T(8,128)(2,1)S(1)}, bf16[16,128,128]{2,1,0:T(8,128)(2,1)S(1)}, bf16[16,64,128]{2,1,0:T(8,128)(2,1)S(1)}, bf16[16,128,128]{2,1,0:T(8,128)(2,1)S(1)}) custom-call(s32[16]{0:T(128)S(1)} %fusion.ord_ref, bf16[16,464,128]{2,1,0:T(8,128)(2,1)S(1)} %all_to_all.20.own_ref, ...), custom_call_target="tpu_custom_call" | custom-call | tf_op jit(solution)/shard_map/pallas_call | solution.py:197
  52.1 0.2 collective-permute-start.1
  52.3 1.8 %collective-permute-done.1.met_ref = bf16[16,128,128]{2,1,0:T(8,128)(2,1)S(1)} collective-permute-done((bf16[16,128,128]{2,1,0:T(8,128)(2,1)S(1)}, bf16[16,128,128]{2,1,0:T(8,128)(2,1)S(1)}, u32[]{:S(2)}, u32[]{:S(2)}) %collective-permute-start.1) | collective-permute-done | bytes 524320 | tf_op jit(solution)/shard_map/ppermute | solution.py:337
  54.1 0.7 shard_map.104
  54.8 21.9 %all_to_all.21.r_ref = bf16[16,320,128]{2,1,0:T(8,128)(2,1)S(1)} all-to-all(bf16[16,320,128]{2,1,0:T(8,128)(2,1)S(1)} %shard_map.104), channel_id=1, replica_groups={{0,16,32,48,64,80,96,112,128,144,160,176,192,208,224,240},{1,17,33,49,6..., dimensions={0} | all-to-all | bytes 2621440 | tf_op jit(solution)/shard_map/all_to_all | solution.py:330
  76.7 0.7 shard_map.106
  77.4 19.3 %all_to_all.22 = bf16[16,40,128]{2,1,0:T(8,128)(2,1)S(1)} all-to-all(bf16[16,40,128]{2,1,0:T(8,128)(2,1)S(1)} %bitcast.7), channel_id=1, replica_groups={{0,1,2,3,4,5,6,7,8,9,10,11,12,13,14,15},{16,17,18,19,20,21,22,23,24,25,..., dimensions={0} | all-to-all | bytes 327680 | tf_op jit(solution)/shard_map/all_to_all | solution.py:330
  96.7 0.7 broadcast_in_dim.2
  97.4 5.8 %all-to-all-start.3 = ((bf16[16,40,128]{2,1,0:T(8,128)(2,1)}), bf16[16,40,128]{2,1,0:T(8,128)(2,1)S(1)}, u32[]{:S(2)}, u32[]{:S(2)}) async-start(bf16[16,40,128]{2,1,0:T(8,128)(2,1)} %broadcast_in_dim.2), calls=%async_computation.3 | async-start | bytes 327680 | tf_op jit(solution)/shard_map/all_to_all | solution.py:330
  103.2 1.0 shard_map.105
  104.2 7.9 %all-to-all-done.3 = bf16[16,40,128]{2,1,0:T(8,128)(2,1)S(1)} async-done(((bf16[16,40,128]{2,1,0:T(8,128)(2,1)}), bf16[16,40,128]{2,1,0:T(8,128)(2,1)S(1)}, u32[]{:S(2)}, u32[]{:S(2)}) %all-to-all-start.3) | async-done | bytes 163872 | tf_op jit(solution)/shard_map/all_to_all | solution.py:330
  112.1 0.7 convert_bitcast_fusion
  (1 shorter events, 0.0 us)
Async XLA Ops:
  4.4 35.6 %copy-start = (bf16[512,1024]{1,0:T(8,128)(2,1)S(1)}, bf16[512,1024]{1,0:T(8,128)(2,1)}, u32[]{:S(2)}) copy-start(bf16[512,1024]{1,0:T(8,128)(2,1)} %uk_ref.3) | copy-start | bytes 3145732
  4.4 35.6 %copy-start.1 = (bf16[512,1024]{1,0:T(8,128)(2,1)S(1)}, bf16[512,1024]{1,0:T(8,128)(2,1)}, u32[]{:S(2)}) copy-start(bf16[512,1024]{1,0:T(8,128)(2,1)} %uv_ref.3) | copy-start | bytes 3145732
  36.1 3.9 %collective-permute-start = (bf16[16,464,128]{2,1,0:T(8,128)(2,1)S(1)}, bf16[16,464,128]{2,1,0:T(8,128)(2,1)S(1)}, u32[]{:S(2)}, u32[]{:S(2)}) collective-permute-start(bf16[16,464,128]{2,1,0:T(8,128)(2,1)S(1)} %all_to_all.20.own_ref), channel_id=1, source_target_pairs={{0,16},{16,0},{32,48},{48,32},{64,80},{80,64},{96,112},{112,96},{1... | collective-permute-start | bytes 5701640 | tf_op jit(solution)/shard_map/ppermute | solution.py:334
  52.1 2.0 %collective-permute-start.1 = (bf16[16,128,128]{2,1,0:T(8,128)(2,1)S(1)}, bf16[16,128,128]{2,1,0:T(8,128)(2,1)S(1)}, u32[]{:S(2)}, u32[]{:S(2)}) collective-permute-start(bf16[16,128,128]{2,1,0:T(8,128)(2,1)S(1)} %get-tuple-element.12), channel_id=1, source_target_pairs={{0,16},{16,0},{32,48},{48,32},{64,80},{80,64},{96,112},{112,96},{1... | collective-permute-start | bytes 1572872 | tf_op jit(solution)/shard_map/ppermute | solution.py:337
  97.4 14.7 %all-to-all-start.3 = ((bf16[16,40,128]{2,1,0:T(8,128)(2,1)}), bf16[16,40,128]{2,1,0:T(8,128)(2,1)S(1)}, u32[]{:S(2)}, u32[]{:S(2)}) async-start(bf16[16,40,128]{2,1,0:T(8,128)(2,1)} %broadcast_in_dim.2), calls=%async_computation.3 | async-start | bytes 327680 | tf_op jit(solution)/shard_map/all_to_all | solution.py:330

commit v2 on v1

v2 whole, which is shorter than its diff:
```python
import functools
import math

import jax
import jax.numpy as jnp
from jax import lax
from jax.experimental import pallas as pl
from jax.experimental.pallas import tpu as pltpu
from jax.sharding import PartitionSpec as P

DL = 512
DR = 64
DN = 128
DV = 128
TOK = 128
HALF = TOK // 2
ROWS = 464
BACK = 320
PART = (DL + DR) // 4
CHUNK = 512
MASKED = -1e30
BF = jnp.bfloat16
F32 = jnp.float32


def dot(a, b):
    return lax.dot_general(a, b, (((1,), (0,)), ((), ())), preferred_element_type=F32)


def dot_nt(a, b):
    return lax.dot_general(a, b, (((1,), (1,)), ((), ())), preferred_element_type=F32)


def low_lanes(shape):
    return lax.broadcasted_iota(jnp.int32, shape, len(shape) - 1) < DR


def pack_kernel(q_hbm, lat_hbm, g_hbm, pos_hbm, tool_hbm, out_ref, q_ref, lat_ref, g_ref, pos_ref, tool_ref, sems):
    pairs = [(tool_hbm, tool_ref), (pos_hbm, pos_ref), (lat_hbm, lat_ref), (q_hbm, q_ref), (g_hbm, g_ref)]
    copies = [pltpu.make_async_copy(src, dst, sems.at[i]) for i, (src, dst) in enumerate(pairs)]
    for copy in copies:
        copy.start()
    for copy in copies[:3]:
        copy.wait()
    tokens = lat_ref[:DL, :].astype(F32).T.astype(BF)
    rope = jnp.concatenate([jnp.zeros((DR, TOK), F32), lat_ref[DL:, :].astype(F32)], axis=0).T
    keep = jnp.broadcast_to((1 - tool_ref[...]).astype(F32), (TOK, TOK)).T
    order = jnp.broadcast_to((pos_ref[...] // TOK).astype(F32), (16, TOK)).astype(BF)
    halves = [slice(c * HALF, c * HALF + HALF) for c in range(2)]
    for i in range(16):
        for t in range(4):
            out_ref[i, t * HALF : (t + 1) * HALF, :] = tokens[halves[i % 2], t * 128 : (t + 1) * 128]
        out_ref[i, 448:464, :] = order
    for copy in copies[3:]:
        copy.wait()
    low = low_lanes((TOK, TOK))
    for h in range(0, 8, 2):
        at = h * 192
        near = q_ref[:, at + 128 : at + 256].astype(F32)
        mid = pltpu.roll(near, DR, 1)
        end = pltpu.roll(q_ref[:, at + 256 : at + 384].astype(F32), DR, 1)
        nope = [q_ref[:, at : at + 128], jnp.where(low, mid, end).astype(BF)]
        ropes = [jnp.where(low, near, rope).astype(BF), jnp.where(low, end, rope).astype(BF)]
        for k in range(2):
            cotangent = (g_ref[:, (h + k) * 128 : (h + k) * 128 + 128].astype(F32) * keep).astype(BF)
            for c, rows in enumerate(halves):
                to = 2 * (h + k) + c
                out_ref[to, 256:320, :] = ropes[k][rows]
                out_ref[to, 320:384, :] = nope[k][rows]
                out_ref[to, 384:448, :] = cotangent[rows]


def pack(queries, lat_t, grad_out, positions, tool_result):
    return pl.pallas_call(
        pack_kernel,
        in_specs=[pl.BlockSpec(memory_space=pl.ANY)] * 5,
        out_specs=pl.BlockSpec(memory_space=pltpu.VMEM),
        out_shape=jax.ShapeDtypeStruct((16, ROWS, 128), BF),
        scratch_shapes=[
            pltpu.VMEM((TOK, 1536), BF),
            pltpu.VMEM((DL + DR, TOK), BF),
            pltpu.VMEM((TOK, 1024), BF),
            pltpu.VMEM((1, TOK), jnp.int32),
            pltpu.VMEM((1, TOK), jnp.int32),
            pltpu.SemaphoreType.DMA((5,)),
        ],
        compiler_params=pltpu.CompilerParams(vmem_limit_bytes=60 << 20),
    )(queries, lat_t, grad_out, positions.reshape(1, TOK), tool_result.reshape(1, TOK))


def attend_kernel(ord_ref, own_ref, oth_ref, uk_ref, uv_ref, keep_out, give_out, dq_out, rope_out,
                  weights, kv, ts, kt, qs, cs, s_sc, g_sc, ds_sc, kvg, dr, dqs, source, sems):
    scale = (DN + DR) ** -0.5
    me = lax.axis_index("ctx")
    core = lax.rem(me, 2)
    columns = pl.ds(pl.multiple_of((me // 2) * 128, 128), 128)
    copies = [
        pltpu.make_async_copy(ref.at[:, columns], weights.at[:, i * 128 : i * 128 + 128], sems.at[i])
        for i, ref in enumerate((uk_ref, uv_ref))
    ]
    for copy in copies:
        copy.start()
    for s in range(16):
        source[ord_ref[s]] = s

    low = low_lanes((HALF, TOK))
    for b in range(16):
        rows = slice(b * HALF, (b + 1) * HALF)
        turned = pltpu.roll(own_ref[source[b], 256:320, :].astype(F32), DR, 1)
        qs[rows, 0:128] = own_ref[source[b], 320:384, :]
        qs[rows, 128:256] = jnp.where(low, 0.0, turned).astype(BF)
        cs[rows, :] = own_ref[source[b], 384:448, :]
    for copy in copies:
        copy.wait()
    for b in range(8):
        rows = slice(b * 256, b * 256 + 256)
        four = [(ref, source[2 * b + k]) for k in range(2) for ref in (own_ref, oth_ref)]
        tokens = jnp.concatenate(
            [
                jnp.concatenate([ref[i, t * HALF : (t + 1) * HALF, :] for t in range(4)], axis=1)
                for ref, i in four
            ],
            axis=0,
        )
        both = dot(tokens, weights[...])
        rope = jnp.concatenate([ref[i, 256:320, :] for ref, i in four], axis=0)
        keys = both[:, 0:128].astype(BF)
        kv[0, rows, :] = keys
        kv[1, rows, :] = both[:, 128:256].astype(BF)
        ts[rows, :] = rope
        kt[0:128, rows] = keys.astype(F32).T.astype(BF)
        kt[128:256, rows] = rope.astype(F32).T.astype(BF)

    factor = scale * math.log2(math.e)
    lane = lax.broadcasted_iota(jnp.int32, (CHUNK, 256), 1)
    qpos = (lane // HALF) * TOK + core * HALF + lax.rem(lane, HALF)
    row = lax.broadcasted_iota(jnp.int32, (CHUNK, 256), 0)
    kpos = (row // TOK) * TOK + lax.rem(lax.rem(row, TOK) + core * HALF, TOK)
    visible = kpos <= qpos
    for p in range(4):
        rows = slice(p * 256, p * 256 + 256)
        chunks = [slice(c * CHUNK, (c + 1) * CHUNK) for c in range(p + 1)]
        top = jnp.full((8, 256), MASKED, F32)
        for c, at in enumerate(chunks):
            s = dot_nt(jnp.concatenate([kv[0, at, :], ts[at, :]], axis=1), qs[rows, :]) * factor
            if c == p:
                s = jnp.where(visible, s, MASKED)
            s_sc[at, :] = s
            g_sc[at, :] = dot_nt(kv[1, at, :], cs[rows, :])
            top = jnp.maximum(top, jnp.max(s.reshape(CHUNK // 8, 8, 256), axis=0))
        top = jnp.max(top, axis=0, keepdims=True)
        total = jnp.zeros((8, 256), F32)
        mixed = jnp.zeros((8, 256), F32)
        for at in chunks:
            e = jnp.exp2(s_sc[at, :] - top)
            s_sc[at, :] = e
            total = total + jnp.sum(e.reshape(CHUNK // 8, 8, 256), axis=0)
            mixed = mixed + jnp.sum((e * g_sc[at, :]).reshape(CHUNK // 8, 8, 256), axis=0)
        share = 1.0 / jnp.sum(total, axis=0, keepdims=True)
        delta = jnp.sum(mixed, axis=0, keepdims=True) * share
        for c, at in enumerate(chunks):
            prob = s_sc[at, :] * share
            ds = (prob * (g_sc[at, :] - delta)).astype(BF)
            ds_sc[at, :] = ds
            key_part = dot(ds, qs[rows, :])
            value_part = dot(prob.astype(BF), cs[rows, :])
            if c == p:
                kvg[0, at, :] = key_part[:, 0:128]
                dr[at, :] = key_part[:, 128:256]
                kvg[1, at, :] = value_part
            else:
                kvg[0, at, :] += key_part[:, 0:128]
                dr[at, :] += key_part[:, 128:256]
                kvg[1, at, :] += value_part
        upto = (p + 1) * CHUNK
        dqs[rows, :] = (dot(kt[:, 0:upto], ds_sc[0:upto, :]) * scale).T

    keep_scale = jnp.where(core == 0, scale, 1.0)
    give_scale = jnp.where(core == 0, 1.0, scale)
    for s in range(16):
        at = pl.multiple_of(ord_ref[s] * TOK, TOK)
        own_half, oth_half = pl.ds(at, HALF), pl.ds(at + HALF, HALF)
        of = pl.ds(pl.multiple_of(ord_ref[s] * HALF, HALF), HALF)
        keep_out[s, :, :] = (kvg[core, pl.ds(at, TOK), :] * keep_scale).astype(BF)
        give_out[s, 0:64, :] = (kvg[1 - core, oth_half, :] * give_scale).astype(BF)
        give_out[s, 64:128, :] = (kvg[1 - core, own_half, :] * give_scale).astype(BF)
        dq_out[s, 0:64, :] = dqs[of, 0:128].astype(BF)
        dq_out[s, 64:128, :] = pltpu.roll(dqs[of, 128:256], DR, 1).astype(BF)
        turned = pltpu.roll(dr[own_half, :], DR, 1)
        rope_out[s, :, :] = (jnp.where(low, turned, dr[oth_half, :]) * scale).astype(BF)


def attend(orders, own, other, w_uk, w_uv):
    whole = pl.BlockSpec(memory_space=pltpu.VMEM)
    anywhere = pl.BlockSpec(memory_space=pl.ANY)
    return pl.pallas_call(
        attend_kernel,
        in_specs=[pl.BlockSpec(memory_space=pltpu.SMEM), whole, whole, anywhere, anywhere],
        out_specs=[whole, whole, whole, whole],
        out_shape=[
            jax.ShapeDtypeStruct((16, TOK, 128), BF),
            jax.ShapeDtypeStruct((16, TOK, 128), BF),
            jax.ShapeDtypeStruct((16, TOK, 128), BF),
            jax.ShapeDtypeStruct((16, HALF, 128), BF),
        ],
        scratch_shapes=[
            pltpu.VMEM((DL, 256), BF),
            pltpu.VMEM((2, 2048, 128), BF),
            pltpu.VMEM((2048, 128), BF),
            pltpu.VMEM((256, 2048), BF),
            pltpu.VMEM((1024, 256), BF),
            pltpu.VMEM((1024, 128), BF),
            pltpu.VMEM((2048, 256), F32),
            pltpu.VMEM((2048, 256), F32),
            pltpu.VMEM((2048, 256), BF),
            pltpu.VMEM((2, 2048, 128), F32),
            pltpu.VMEM((2048, 128), F32),
            pltpu.VMEM((1024, 256), F32),
            pltpu.SMEM((16,), jnp.int32),
            pltpu.SemaphoreType.DMA((2,)),
        ],
        compiler_params=pltpu.CompilerParams(vmem_limit_bytes=20 << 20),
    )(orders, own, other, w_uk, w_uv)


def small(kernel, inputs, outputs):
    whole = pl.BlockSpec(memory_space=pltpu.VMEM)
    return pl.pallas_call(
        kernel,
        in_specs=[whole] * len(inputs),
        out_specs=[whole] * len(outputs),
        out_shape=[jax.ShapeDtypeStruct(shape, dtype) for shape, dtype in outputs],
        compiler_params=pltpu.CompilerParams(vmem_limit_bytes=16 << 20),
    )(*inputs)


def finish_kernel(keep_ref, met_ref, rope_ref, dq_ref, own_ref, oth_ref, out_ref):
    total = jnp.zeros((128, DL), F32)
    for i in range(0, 16, 2):
        pair = keep_ref[i : i + 2].astype(F32) + met_ref[i : i + 2].astype(F32)
        out_ref[i : i + 2, 0:128, :] = pair.astype(BF)
        out_ref[i : i + 2, 128:192, :] = rope_ref[i : i + 2]
        out_ref[i : i + 2, 192:256, :] = dq_ref[i : i + 2, 0:64, :]
        lat = jnp.concatenate(
            [
                jnp.concatenate([ref[j, t * HALF : (t + 1) * HALF, :] for t in range(4)], axis=1)
                for j in (i, i + 1)
                for ref in (own_ref, oth_ref)
            ],
            axis=0,
        )
        total = total + dot(pair.reshape(256, 128).T.astype(BF), lat)
    total = total.T
    turned = pltpu.roll(total, DR, 1)
    low = low_lanes((32, TOK))
    for i in range(16):
        for part, first in ((turned, 64), (total, 96)):
            dq = dq_ref[i, first : first + 32, :].astype(F32)
            out_ref[i, 192 + first : 224 + first, :] = jnp.where(low, dq, part[i * 32 : i * 32 + 32]).astype(BF)


def latent_kernel(r_ref, uk_ref, uv_ref, own_out, first_out, second_out, third_out, all_s):
    keys = jnp.concatenate([r_ref[i, 0:128, :] for i in range(0, 16, 2)], axis=1)
    values = jnp.concatenate(
        [jnp.concatenate([r_ref[i, 64:128, :], r_ref[i, 0:64, :]], axis=0) for i in range(1, 16, 2)], axis=1
    )
    all_s[:DL, :] = (dot_nt(uk_ref[...], keys) + dot_nt(uv_ref[...], values)).astype(BF)
    even = r_ref[0, 128:192, :].astype(F32)
    odd = r_ref[1, 128:192, :].astype(F32)
    for i in range(2, 16, 2):
        even = even + r_ref[i, 128:192, :].astype(F32)
        odd = odd + r_ref[i + 1, 128:192, :].astype(F32)
    rope = even + pltpu.roll(odd, DR, 1)
    rope = jnp.concatenate([rope, pltpu.roll(rope, DR, 1)], axis=0).T
    all_s[DL:, :] = rope[:DR, :].astype(BF)
    mine = lax.axis_index("head") // 4
    for k, out in enumerate((own_out, first_out, second_out, third_out)):
        out[...] = all_s[pl.ds(pl.multiple_of((mine ^ k) * PART, 16), PART), :]


def latent_terms(received, w_uk, w_uv):
    whole = pl.BlockSpec(memory_space=pltpu.VMEM)
    return pl.pallas_call(
        latent_kernel,
        in_specs=[whole] * 3,
        out_specs=[whole] * 4,
        out_shape=[jax.ShapeDtypeStruct((PART, TOK), BF)] * 4,
        scratch_shapes=[pltpu.VMEM((DL + DR, TOK), BF)],
        compiler_params=pltpu.CompilerParams(vmem_limit_bytes=16 << 20),
    )(received, w_uk, w_uv)


def four_kernel(a_ref, b_ref, c_ref, d_ref, out_ref):
    first = a_ref[...].astype(F32) + b_ref[...].astype(F32)
    out_ref[...] = (first + (c_ref[...].astype(F32) + d_ref[...].astype(F32))).astype(BF)


def place_kernel(a_ref, b_ref, c_ref, d_ref, out_ref):
    mine = lax.axis_index("head") // 4
    for k, ref in enumerate((a_ref, b_ref, c_ref, d_ref)):
        out_ref[pl.ds(pl.multiple_of((mine ^ k) * PART, 16), PART), :] = ref[...].astype(F32)


def unpack_kernel(r_ref, q_ref, uk_ref, uv_ref):
    low = low_lanes((HALF, TOK))
    for h in range(0, 8, 2):
        for c in range(2):
            rows = slice(c * HALF, c * HALF + HALF)
            i, j, at = 2 * h + c, 2 * h + 2 + c, h * 192
            q_ref[rows, at : at + 128] = r_ref[i, 192:256, :]
            first = r_ref[i, 256:320, :].astype(F32)
            second = pltpu.roll(r_ref[j, 256:320, :].astype(F32), DR, 1)
            turned = pltpu.roll(r_ref[j, 192:256, :].astype(F32), DR, 1)
            q_ref[rows, at + 128 : at + 256] = jnp.where(low, first, turned).astype(BF)
            q_ref[rows, at + 256 : at + 384] = jnp.where(low, turned, second).astype(BF)
    for i in range(16):
        left = pltpu.roll(r_ref[i, 256:288, :].astype(F32), DR, 1)
        right = r_ref[i, 288:320, :].astype(F32)
        ref = uv_ref if i % 2 else uk_ref
        ref[:, (i // 2) * 128 : (i // 2) * 128 + 128] = jnp.where(low[0:32], left, right)


def local(queries, latent, w_uk, w_uv, grad_out, positions, tool_result):
    every = [list(range(16))]
    swap = [(i, i ^ 1) for i in range(16)]

    def exchange(x):
        return lax.all_to_all(x, "ctx", 0, 0, tiled=True, axis_index_groups=every)

    def along_x(x, k):
        return lax.ppermute(x, "head", [(i, i ^ (4 * k)) for i in range(16)])

    def along_z(x, k):
        return lax.ppermute(x, "head", [(i, i ^ k) for i in range(16)])

    own = exchange(pack(queries, latent.T, grad_out, positions, tool_result))
    other = lax.ppermute(own, "ctx", swap)
    orders = own[:, 448, 0].astype(jnp.int32)
    keep, give, dq, rope = attend(orders, own, other, w_uk, w_uv)
    met = lax.ppermute(give, "ctx", swap)
    (back,) = small(finish_kernel, (keep, met, rope, dq, own, other), [((16, BACK, 128), BF)])
    received = exchange(back)
    parts = latent_terms(received, w_uk, w_uv)
    (part,) = small(four_kernel, [parts[0]] + [along_x(parts[k], k) for k in (1, 2, 3)], [((PART, TOK), BF)])
    (part,) = small(four_kernel, [part] + [along_z(part, k) for k in (1, 2, 3)], [((PART, TOK), BF)])
    (whole,) = small(place_kernel, [part] + [along_x(part, k) for k in (1, 2, 3)], [((DL + DR, TOK), F32)])

    grad_queries, grad_w_uk, grad_w_uv = small(
        unpack_kernel, (received,), [((TOK, 1536), BF), ((32, 1024), F32), ((32, 1024), F32)]
    )
    return (grad_queries, whole.T, grad_w_uk, grad_w_uv)


def solution(mesh):
    placed = (
        P("ctx", "head"),
        P("ctx", None),
        P(None, "head"),
        P(None, "head"),
        P("ctx", "head"),
        P("ctx"),
        P("ctx"),
    )
    return jax.shard_map(
        local,
        mesh=mesh,
        in_specs=placed,
        out_specs=(P("ctx", "head"), P("ctx", None), P("ctx", "head"), P("ctx", "head")),
        check_vma=False,
    )
```

time: 114 us -> 103 us (0.904)
  blocking collectives: 72.9 us -> 53.6 us
  starting transfers between devices: 6 us -> 16.9 us
  Pallas kernels: 18.3 us -> 13.8 us
  waiting for transfers between devices: 13.2 us -> 17.1 us
    all_to_all x3 -> x2, blocking collectives: 72.9 us -> 53.6 us  [exchange(): return lax.all_to_all(x, 'ctx', 0, 0, tiled=True, axis_index_groups=every)]
    ppermute x0 -> x9, starting transfers between devices: none -> 16.7 us  [the longest x6 8.76 us: along_x(): return lax.ppermute(x, 'head', [(i, i ^ 4 * k) for i in range(16)])]
    ppermute x0 -> x9, waiting for transfers between devices: none -> 11.8 us  [the longest x6 6.4 us: along_x(): return lax.ppermute(x, 'head', [(i, i ^ 4 * k) for i in range(16)])]
    all_to_all x1 -> x0, waiting for transfers between devices: 7.9 us -> none  [exchange(): return lax.all_to_all(x, axis, 0, 0, tiled=True, axis_index_groups=every)]
    all_to_all x1 -> x0, starting transfers between devices: 5.78 us -> none  [exchange(): return lax.all_to_all(x, axis, 0, 0, tiled=True, axis_index_groups=every)]
    pallas_call x1, Pallas kernels: 12.1 us -> 8.03 us  [attend(): pl.pallas_call(attend_kernel, in_specs=[pl.BlockSpec(memory_space=pltpu.S...]
    pallas_call x4 -> x7, Pallas kernels: 6.17 us -> 5.79 us  [the longest x1 2.66 us: pack(): pl.pallas_call(pack_kernel, in_specs=[pl.BlockSpec(memory_space=pl.ANY)]...]
  transfers between devices with their start and end apart: 3 -> 11, of which waited for: 3 -> 8; matrix products, arithmetic and copies ran while one was open for 0% -> 0% of each run, Pallas kernels for 1% -> 1%
where the time goes in v2:
time: 103 us
  blocking collectives  53.6 us (52%)
  waiting for transfers between devices  17.1 us (17%)
  starting transfers between devices  16.9 us (16%)
  Pallas kernels  13.8 us (13%)
    all_to_all x2, blocking collectives, exchange(): return lax.all_to_all(x, 'ctx', 0, 0, tiled=True, axis_index_groups=every)  53.6 us
    ppermute x6, starting transfers between devices, along_x(): return lax.ppermute(x, 'head', [(i, i ^ 4 * k) for i in range(16)])  8.76 us
    pallas_call x1, Pallas kernels, attend(): pl.pallas_call(attend_kernel, in_specs=[pl.BlockSpec(memory_space=pltpu.S...  8.03 us
    ppermute x3, starting transfers between devices, along_z(): return lax.ppermute(x, 'head', [(i, i ^ k) for i in range(16)])  7.95 us
    ppermute x6, waiting for transfers between devices, along_x(): return lax.ppermute(x, 'head', [(i, i ^ 4 * k) for i in range(16)])  6.4 us
    ppermute x3, waiting for transfers between devices, along_z(): return lax.ppermute(x, 'head', [(i, i ^ k) for i in range(16)])  5.41 us
    ppermute x1, waiting for transfers between devices, local(): other = lax.ppermute(own, 'ctx', swap)  3.5 us
    pallas_call x1, Pallas kernels, pack(): pl.pallas_call(pack_kernel, in_specs=[pl.BlockSpec(memory_space=pl.ANY)]...  2.66 us
  transfers between devices with their start and end apart: 11, of which 8 were waited for; matrix products, arithmetic and copies ran while one was open for 0% of the time, Pallas kernels for 1%

profile of v2, /device:TPU:2, one launch (start us, length us, event | category | flops | bytes accessed | tf_op | source)
XLA Modules:
  0.0 102.5 jit_solution(12967595514019751986)
XLA Ops:
  0.6 2.7 %shard_map.102 = bf16[16,464,128]{2,1,0:T(8,128)(2,1)} custom-call(bf16[128,1536]{1,0:T(8,128)(2,1)} %q_hbm.1, bf16[576,128]{1,0:T(8,128)(2,1)} %bitcast.5, bf16[128,1024]{1,0:T(8,128)(2,1)} %g_hbm.1, s32[1,128]{1,0:T(1,128)} %bitcast.6, s32[1,128]{1,0:T(1,128)} %bitcast.7), custom_call_target="tpu_custom_call" | custom-call | tf_op jit(solution)/shard_map/pallas_call | solution.py:74
  3.3 0.0 copy-start
  3.3 0.0 copy-start.1
  3.3 31.7 %all_to_all.10.own_ref = bf16[16,464,128]{2,1,0:T(8,128)(2,1)S(1)} all-to-all(bf16[16,464,128]{2,1,0:T(8,128)(2,1)} %shard_map.102), channel_id=1, replica_groups={{0,16,32,48,64,80,96,112,128,144,160,176,192,208,224,240},{1,17,33,49,6..., dimensions={0} | all-to-all | bytes 3801088 | tf_op jit(solution)/shard_map/all_to_all | solution.py:328
  35.0 0.0 collective-permute-start
  35.0 0.4 fusion.ord_ref
  35.4 3.5 %collective-permute-done.oth_ref = bf16[16,464,128]{2,1,0:T(8,128)(2,1)S(1)} collective-permute-done((bf16[16,464,128]{2,1,0:T(8,128)(2,1)S(1)}, bf16[16,464,128]{2,1,0:T(8,128)(2,1)S(1)}, u32[]{:S(2)}, u32[]{:S(2)}) %collective-permute-start) | collective-permute-done | bytes 1900576 | tf_op jit(solution)/shard_map/ppermute | solution.py:337
  38.9 0.0 copy-done
  38.9 0.0 copy-done.1
  38.9 8.0 %shard_map.103 = (bf16[16,128,128]{2,1,0:T(8,128)(2,1)S(1)}, bf16[16,128,128]{2,1,0:T(8,128)(2,1)S(1)}, bf16[16,128,128]{2,1,0:T(8,128)(2,1)S(1)}, bf16[16,64,128]{2,1,0:T(8,128)(2,1)S(1)}) custom-call(s32[16]{0:T(128)S(1)} %fusion.ord_ref, bf16[16,464,128]{2,1,0:T(8,128)(2,1)S(1)} %all_to_all.10.own_ref, ...), custom_call_target="tpu_custom_call" | custom-call | tf_op jit(solution)/shard_map/pallas_call | solution.py:196
  46.9 0.2 collective-permute-start.1
  47.2 1.8 %collective-permute-done.1.met_ref = bf16[16,128,128]{2,1,0:T(8,128)(2,1)S(1)} collective-permute-done((bf16[16,128,128]{2,1,0:T(8,128)(2,1)S(1)}, bf16[16,128,128]{2,1,0:T(8,128)(2,1)S(1)}, u32[]{:S(2)}, u32[]{:S(2)}) %collective-permute-start.1) | collective-permute-done | bytes 524320 | tf_op jit(solution)/shard_map/ppermute | solution.py:340
  48.9 0.6 shard_map.104
  49.6 21.9 %all_to_all.11.r_ref = bf16[16,320,128]{2,1,0:T(8,128)(2,1)S(1)} all-to-all(bf16[16,320,128]{2,1,0:T(8,128)(2,1)S(1)} %shard_map.104), channel_id=1, replica_groups={{0,16,32,48,64,80,96,112,128,144,160,176,192,208,224,240},{1,17,33,49,6..., dimensions={0} | all-to-all | bytes 2621440 | tf_op jit(solution)/shard_map/all_to_all | solution.py:328
  71.5 0.7 shard_map.106
  72.2 0.6 collective-permute-start.2
  72.8 2.4 %collective-permute-start.3 = (bf16[144,128]{1,0:T(8,128)(2,1)S(1)}, bf16[144,128]{1,0:T(8,128)(2,1)S(1)}, u32[]{:S(2)}, u32[]{:S(2)}) collective-permute-start(bf16[144,128]{1,0:T(8,128)(2,1)S(1)} %get-tuple-element.22), channel_id=1, source_target_pairs={{0,8},{1,9},{2,10},{3,11},{4,12},{5,13},{6,14},{7,15},{8,0},{9,1},... | collective-permute-start | bytes 110600 | tf_op jit(solution)/shard_map/ppermute | solution.py:331
  75.3 0.5 collective-permute-start.4
  75.8 0.5 collective-permute-done.2.b_ref
  76.3 2.0 %collective-permute-done.3.c_ref = bf16[144,128]{1,0:T(8,128)(2,1)S(1)} collective-permute-done((bf16[144,128]{1,0:T(8,128)(2,1)S(1)}, bf16[144,128]{1,0:T(8,128)(2,1)S(1)}, u32[]{:S(2)}, u32[]{:S(2)}) %collective-permute-start.3) | collective-permute-done | bytes 36896 | tf_op jit(solution)/shard_map/ppermute | solution.py:331
  78.3 0.9 collective-permute-done.4.d_ref
  79.2 5.5 %collective-permute-start.7 = (bf16[144,128]{1,0:T(8,128)(2,1)S(1)}, bf16[144,128]{1,0:T(8,128)(2,1)S(1)}, u32[]{:S(2)}, u32[]{:S(2)}) collective-permute-start(bf16[144,128]{1,0:T(8,128)(2,1)S(1)} %shard_map.107.a_ref), channel_id=1, source_target_pairs={{0,3},{1,2},{2,1},{3,0},{4,7},{5,6},{6,5},{7,4},{8,11},{9,10},{10,... | collective-permute-start | bytes 110600 | tf_op jit(solution)/shard_map/ppermute | solution.py:334
  84.7 1.4 %collective-permute-start.6 = (bf16[144,128]{1,0:T(8,128)(2,1)S(1)}, bf16[144,128]{1,0:T(8,128)(2,1)S(1)}, u32[]{:S(2)}, u32[]{:S(2)}) collective-permute-start(bf16[144,128]{1,0:T(8,128)(2,1)S(1)} %shard_map.107.a_ref), channel_id=1, source_target_pairs={{0,2},{1,3},{2,0},{3,1},{4,6},{5,7},{6,4},{7,5},{8,10},{9,11},{10,... | collective-permute-start | bytes 110600 | tf_op jit(solution)/shard_map/ppermute | solution.py:334
  86.2 1.0 %collective-permute-start.5 = (bf16[144,128]{1,0:T(8,128)(2,1)S(1)}, bf16[144,128]{1,0:T(8,128)(2,1)S(1)}, u32[]{:S(2)}, u32[]{:S(2)}) collective-permute-start(bf16[144,128]{1,0:T(8,128)(2,1)S(1)} %shard_map.107.a_ref), channel_id=1, source_target_pairs={{0,1},{1,0},{2,3},{3,2},{4,5},{5,4},{6,7},{7,6},{8,9},{9,8},{10,11... | collective-permute-start | bytes 110600 | tf_op jit(solution)/shard_map/ppermute | solution.py:334
  87.2 0.0 collective-permute-done.7.d_ref
  87.2 5.4 %collective-permute-done.6.c_ref = bf16[144,128]{1,0:T(8,128)(2,1)S(1)} collective-permute-done((bf16[144,128]{1,0:T(8,128)(2,1)S(1)}, bf16[144,128]{1,0:T(8,128)(2,1)S(1)}, u32[]{:S(2)}, u32[]{:S(2)}) %collective-permute-start.6) | collective-permute-done | bytes 36896 | tf_op jit(solution)/shard_map/ppermute | solution.py:334
  92.6 0.0 collective-permute-done.5.b_ref
  92.6 1.3 %collective-permute-start.10 = (bf16[144,128]{1,0:T(8,128)(2,1)S(1)}, bf16[144,128]{1,0:T(8,128)(2,1)S(1)}, u32[]{:S(2)}, u32[]{:S(2)}) collective-permute-start(bf16[144,128]{1,0:T(8,128)(2,1)S(1)} %shard_map.108.a_ref), channel_id=1, source_target_pairs={{0,12},{1,13},{2,14},{3,15},{4,8},{5,9},{6,10},{7,11},{8,4},{9,5},... | collective-permute-start | bytes 110600 | tf_op jit(solution)/shard_map/ppermute | solution.py:331
  94.0 3.8 %collective-permute-start.9 = (bf16[144,128]{1,0:T(8,128)(2,1)S(1)}, bf16[144,128]{1,0:T(8,128)(2,1)S(1)}, u32[]{:S(2)}, u32[]{:S(2)}) collective-permute-start(bf16[144,128]{1,0:T(8,128)(2,1)S(1)} %shard_map.108.a_ref), channel_id=1, source_target_pairs={{0,8},{1,9},{2,10},{3,11},{4,12},{5,13},{6,14},{7,15},{8,0},{9,1},... | collective-permute-start | bytes 110600 | tf_op jit(solution)/shard_map/ppermute | solution.py:331
  97.8 0.0 collective-permute-start.8
  97.8 1.0 shard_map.105
  98.8 0.0 collective-permute-done.10.d_ref
  98.8 0.9 collective-permute-done.9.c_ref
  99.7 2.0 %collective-permute-done.8.b_ref = bf16[144,128]{1,0:T(8,128)(2,1)S(1)} collective-permute-done((bf16[144,128]{1,0:T(8,128)(2,1)S(1)}, bf16[144,128]{1,0:T(8,128)(2,1)S(1)}, u32[]{:S(2)}, u32[]{:S(2)}) %collective-permute-start.8) | collective-permute-done | bytes 36896 | tf_op jit(solution)/shard_map/ppermute | solution.py:331
  101.8 0.7 shard_map.109
  (2 shorter events, 0.0 us)
Async XLA Ops:
  3.3 35.6 %copy-start = (bf16[512,1024]{1,0:T(8,128)(2,1)S(1)}, bf16[512,1024]{1,0:T(8,128)(2,1)}, u32[]{:S(2)}) copy-start(bf16[512,1024]{1,0:T(8,128)(2,1)} %uk_ref.3) | copy-start | bytes 3145732
  3.3 35.6 %copy-start.1 = (bf16[512,1024]{1,0:T(8,128)(2,1)S(1)}, bf16[512,1024]{1,0:T(8,128)(2,1)}, u32[]{:S(2)}) copy-start(bf16[512,1024]{1,0:T(8,128)(2,1)} %uv_ref.3) | copy-start | bytes 3145732
  35.0 3.9 %collective-permute-start = (bf16[16,464,128]{2,1,0:T(8,128)(2,1)S(1)}, bf16[16,464,128]{2,1,0:T(8,128)(2,1)S(1)}, u32[]{:S(2)}, u32[]{:S(2)}) collective-permute-start(bf16[16,464,128]{2,1,0:T(8,128)(2,1)S(1)} %all_to_all.10.own_ref), channel_id=1, source_target_pairs={{0,16},{16,0},{32,48},{48,32},{64,80},{80,64},{96,112},{112,96},{1... | collective-permute-start | bytes 5701640 | tf_op jit(solution)/shard_map/ppermute | solution.py:337
  46.9 2.0 %collective-permute-start.1 = (bf16[16,128,128]{2,1,0:T(8,128)(2,1)S(1)}, bf16[16,128,128]{2,1,0:T(8,128)(2,1)S(1)}, u32[]{:S(2)}, u32[]{:S(2)}) collective-permute-start(bf16[16,128,128]{2,1,0:T(8,128)(2,1)S(1)} %get-tuple-element.16), channel_id=1, source_target_pairs={{0,16},{16,0},{32,48},{48,32},{64,80},{80,64},{96,112},{112,96},{1... | collective-permute-start | bytes 1572872 | tf_op jit(solution)/shard_map/ppermute | solution.py:340
  72.2 4.0 %collective-permute-start.2 = (bf16[144,128]{1,0:T(8,128)(2,1)S(1)}, bf16[144,128]{1,0:T(8,128)(2,1)S(1)}, u32[]{:S(2)}, u32[]{:S(2)}) collective-permute-start(bf16[144,128]{1,0:T(8,128)(2,1)S(1)} %get-tuple-element.21), channel_id=1, source_target_pairs={{0,4},{1,5},{2,6},{3,7},{4,0},{5,1},{6,2},{7,3},{8,12},{9,13},{10,... | collective-permute-start | bytes 110600 | tf_op jit(solution)/shard_map/ppermute | solution.py:331
  72.8 5.5 %collective-permute-start.3 = (bf16[144,128]{1,0:T(8,128)(2,1)S(1)}, bf16[144,128]{1,0:T(8,128)(2,1)S(1)}, u32[]{:S(2)}, u32[]{:S(2)}) collective-permute-start(bf16[144,128]{1,0:T(8,128)(2,1)S(1)} %get-tuple-element.22), channel_id=1, source_target_pairs={{0,8},{1,9},{2,10},{3,11},{4,12},{5,13},{6,14},{7,15},{8,0},{9,1},... | collective-permute-start | bytes 110600 | tf_op jit(solution)/shard_map/ppermute | solution.py:331
  75.3 4.0 %collective-permute-start.4 = (bf16[144,128]{1,0:T(8,128)(2,1)S(1)}, bf16[144,128]{1,0:T(8,128)(2,1)S(1)}, u32[]{:S(2)}, u32[]{:S(2)}) collective-permute-start(bf16[144,128]{1,0:T(8,128)(2,1)S(1)} %get-tuple-element.23), channel_id=1, source_target_pairs={{0,12},{1,13},{2,14},{3,15},{4,8},{5,9},{6,10},{7,11},{8,4},{9,5},... | collective-permute-start | bytes 110600 | tf_op jit(solution)/shard_map/ppermute | solution.py:331
  79.2 8.0 %collective-permute-start.7 = (bf16[144,128]{1,0:T(8,128)(2,1)S(1)}, bf16[144,128]{1,0:T(8,128)(2,1)S(1)}, u32[]{:S(2)}, u32[]{:S(2)}) collective-permute-start(bf16[144,128]{1,0:T(8,128)(2,1)S(1)} %shard_map.107.a_ref), channel_id=1, source_target_pairs={{0,3},{1,2},{2,1},{3,0},{4,7},{5,6},{6,5},{7,4},{8,11},{9,10},{10,... | collective-permute-start | bytes 110600 | tf_op jit(solution)/shard_map/ppermute | solution.py:334
  84.7 7.9 %collective-permute-start.6 = (bf16[144,128]{1,0:T(8,128)(2,1)S(1)}, bf16[144,128]{1,0:T(8,128)(2,1)S(1)}, u32[]{:S(2)}, u32[]{:S(2)}) collective-permute-start(bf16[144,128]{1,0:T(8,128)(2,1)S(1)} %shard_map.107.a_ref), channel_id=1, source_target_pairs={{0,2},{1,3},{2,0},{3,1},{4,6},{5,7},{6,4},{7,5},{8,10},{9,11},{10,... | collective-permute-start | bytes 110600 | tf_op jit(solution)/shard_map/ppermute | solution.py:334
  86.2 6.4 %collective-permute-start.5 = (bf16[144,128]{1,0:T(8,128)(2,1)S(1)}, bf16[144,128]{1,0:T(8,128)(2,1)S(1)}, u32[]{:S(2)}, u32[]{:S(2)}) collective-permute-start(bf16[144,128]{1,0:T(8,128)(2,1)S(1)} %shard_map.107.a_ref), channel_id=1, source_target_pairs={{0,1},{1,0},{2,3},{3,2},{4,5},{5,4},{6,7},{7,6},{8,9},{9,8},{10,11... | collective-permute-start | bytes 110600 | tf_op jit(solution)/shard_map/ppermute | solution.py:334
  92.6 6.2 %collective-permute-start.10 = (bf16[144,128]{1,0:T(8,128)(2,1)S(1)}, bf16[144,128]{1,0:T(8,128)(2,1)S(1)}, u32[]{:S(2)}, u32[]{:S(2)}) collective-permute-start(bf16[144,128]{1,0:T(8,128)(2,1)S(1)} %shard_map.108.a_ref), channel_id=1, source_target_pairs={{0,12},{1,13},{2,14},{3,15},{4,8},{5,9},{6,10},{7,11},{8,4},{9,5},... | collective-permute-start | bytes 110600 | tf_op jit(solution)/shard_map/ppermute | solution.py:331
  94.0 5.8 %collective-permute-start.9 = (bf16[144,128]{1,0:T(8,128)(2,1)S(1)}, bf16[144,128]{1,0:T(8,128)(2,1)S(1)}, u32[]{:S(2)}, u32[]{:S(2)}) collective-permute-start(bf16[144,128]{1,0:T(8,128)(2,1)S(1)} %shard_map.108.a_ref), channel_id=1, source_target_pairs={{0,8},{1,9},{2,10},{3,11},{4,12},{5,13},{6,14},{7,15},{8,0},{9,1},... | collective-permute-start | bytes 110600 | tf_op jit(solution)/shard_map/ppermute | solution.py:331
  97.8 4.0 %collective-permute-start.8 = (bf16[144,128]{1,0:T(8,128)(2,1)S(1)}, bf16[144,128]{1,0:T(8,128)(2,1)S(1)}, u32[]{:S(2)}, u32[]{:S(2)}) collective-permute-start(bf16[144,128]{1,0:T(8,128)(2,1)S(1)} %shard_map.108.a_ref), channel_id=1, source_target_pairs={{0,4},{1,5},{2,6},{3,7},{4,0},{5,1},{6,2},{7,3},{8,12},{9,13},{10,... | collective-permute-start | bytes 110600 | tf_op jit(solution)/shard_map/ppermute | solution.py:331

commit v3 on v2

--- a/solution.py
+++ b/solution.py
@@ -15,7 +15,7 @@
 TOK = 128
 HALF = TOK // 2
 ROWS = 464
-BACK = 320
+BACK = 288
 PART = (DL + DR) // 4
 CHUNK = 512
 MASKED = -1e30
@@ -89,7 +89,7 @@
 
 
 def attend_kernel(ord_ref, own_ref, oth_ref, uk_ref, uv_ref, keep_out, give_out, dq_out, rope_out,
-                  weights, kv, ts, kt, qs, cs, s_sc, g_sc, ds_sc, kvg, dr, dqs, source, sems):
+                  weights, kv, ts, kt, qs, cs, s_sc, g_sc, ds_sc, p_sc, kvg, dr, dqs, source, sems):
     scale = (DN + DR) ** -0.5
     me = lax.axis_index("ctx")
     core = lax.rem(me, 2)
@@ -137,43 +137,50 @@
     row = lax.broadcasted_iota(jnp.int32, (CHUNK, 256), 0)
     kpos = (row // TOK) * TOK + lax.rem(lax.rem(row, TOK) + core * HALF, TOK)
     visible = kpos <= qpos
+    spans = [slice(c * CHUNK, (c + 1) * CHUNK) for c in range(4)]
+
+    def score(p, c):
+        rows, at = slice(p * 256, p * 256 + 256), spans[c]
+        s = dot_nt(jnp.concatenate([kv[0, at, :], ts[at, :]], axis=1), qs[rows, :]) * factor
+        if c == p:
+            s = jnp.where(visible, s, MASKED)
+        s_sc[p % 2, at, :] = s
+        g_sc[p % 2, at, :] = dot_nt(kv[1, at, :], cs[rows, :])
+        return jnp.max(s.reshape(CHUNK // 8, 8, 256), axis=0)
+
+    tops = [score(0, 0)]
     for p in range(4):
         rows = slice(p * 256, p * 256 + 256)
-        chunks = [slice(c * CHUNK, (c + 1) * CHUNK) for c in range(p + 1)]
-        top = jnp.full((8, 256), MASKED, F32)
-        for c, at in enumerate(chunks):
-            s = dot_nt(jnp.concatenate([kv[0, at, :], ts[at, :]], axis=1), qs[rows, :]) * factor
-            if c == p:
-                s = jnp.where(visible, s, MASKED)
-            s_sc[at, :] = s
-            g_sc[at, :] = dot_nt(kv[1, at, :], cs[rows, :])
-            top = jnp.maximum(top, jnp.max(s.reshape(CHUNK // 8, 8, 256), axis=0))
+        top = functools.reduce(jnp.maximum, tops)
+        tops = []
         top = jnp.max(top, axis=0, keepdims=True)
         total = jnp.zeros((8, 256), F32)
         mixed = jnp.zeros((8, 256), F32)
-        for at in chunks:
-            e = jnp.exp2(s_sc[at, :] - top)
-            s_sc[at, :] = e
+        for c in range(p + 1):
+            at = spans[c]
+            e = jnp.exp2(s_sc[p % 2, at, :] - top)
+            s_sc[p % 2, at, :] = e
             total = total + jnp.sum(e.reshape(CHUNK // 8, 8, 256), axis=0)
-            mixed = mixed + jnp.sum((e * g_sc[at, :]).reshape(CHUNK // 8, 8, 256), axis=0)
+            mixed = mixed + jnp.sum((e * g_sc[p % 2, at, :]).reshape(CHUNK // 8, 8, 256), axis=0)
+            if p < 3:
+                tops.append(score(p + 1, c))
         share = 1.0 / jnp.sum(total, axis=0, keepdims=True)
         delta = jnp.sum(mixed, axis=0, keepdims=True) * share
-        for c, at in enumerate(chunks):
-            prob = s_sc[at, :] * share
-            ds = (prob * (g_sc[at, :] - delta)).astype(BF)
-            ds_sc[at, :] = ds
-            key_part = dot(ds, qs[rows, :])
-            value_part = dot(prob.astype(BF), cs[rows, :])
-            if c == p:
-                kvg[0, at, :] = key_part[:, 0:128]
-                dr[at, :] = key_part[:, 128:256]
-                kvg[1, at, :] = value_part
-            else:
-                kvg[0, at, :] += key_part[:, 0:128]
-                dr[at, :] += key_part[:, 128:256]
-                kvg[1, at, :] += value_part
+        if p < 3:
+            tops.append(score(p + 1, p + 1))
+        for c in range(p + 1):
+            at = spans[c]
+            prob = s_sc[p % 2, at, :] * share
+            ds_sc[at, rows] = (prob * (g_sc[p % 2, at, :] - delta)).astype(BF)
+            p_sc[at, rows] = prob.astype(BF)
         upto = (p + 1) * CHUNK
-        dqs[rows, :] = (dot(kt[:, 0:upto], ds_sc[0:upto, :]) * scale).T
+        dqs[rows, :] = (dot(kt[:, 0:upto], ds_sc[0:upto, rows]) * scale).T
+    for c in range(4):
+        at = spans[c]
+        key_part = dot(ds_sc[at, c * 256 :], qs[c * 256 :, :])
+        kvg[0, at, :] = key_part[:, 0:128]
+        dr[at, :] = key_part[:, 128:256]
+        kvg[1, at, :] = dot(p_sc[at, c * 256 :], cs[c * 256 :, :])
 
     keep_scale = jnp.where(core == 0, scale, 1.0)
     give_scale = jnp.where(core == 0, 1.0, scale)
@@ -184,10 +191,10 @@
         keep_out[s, :, :] = (kvg[core, pl.ds(at, TOK), :] * keep_scale).astype(BF)
         give_out[s, 0:64, :] = (kvg[1 - core, oth_half, :] * give_scale).astype(BF)
         give_out[s, 64:128, :] = (kvg[1 - core, own_half, :] * give_scale).astype(BF)
-        dq_out[s, 0:64, :] = dqs[of, 0:128].astype(BF)
-        dq_out[s, 64:128, :] = pltpu.roll(dqs[of, 128:256], DR, 1).astype(BF)
-        turned = pltpu.roll(dr[own_half, :], DR, 1)
-        rope_out[s, :, :] = (jnp.where(low, turned, dr[oth_half, :]) * scale).astype(BF)
+        give_out[s, 128:192, :] = (dr[oth_half, :] * scale).astype(BF)
+        dq_out[s, :, :] = dqs[of, 0:128].astype(BF)
+        turned = pltpu.roll(dqs[of, 128:256], DR, 1)
+        rope_out[s, :, :] = jnp.where(low, turned, dr[own_half, :] * scale).astype(BF)
 
 
 def attend(orders, own, other, w_uk, w_uv):
@@ -199,8 +206,8 @@
         out_specs=[whole, whole, whole, whole],
         out_shape=[
             jax.ShapeDtypeStruct((16, TOK, 128), BF),
-            jax.ShapeDtypeStruct((16, TOK, 128), BF),
-            jax.ShapeDtypeStruct((16, TOK, 128), BF),
+            jax.ShapeDtypeStruct((16, TOK + HALF, 128), BF),
+            jax.ShapeDtypeStruct((16, HALF, 128), BF),
             jax.ShapeDtypeStruct((16, HALF, 128), BF),
         ],
         scratch_shapes=[
@@ -210,16 +217,17 @@
             pltpu.VMEM((256, 2048), BF),
             pltpu.VMEM((1024, 256), BF),
             pltpu.VMEM((1024, 128), BF),
-            pltpu.VMEM((2048, 256), F32),
-            pltpu.VMEM((2048, 256), F32),
-            pltpu.VMEM((2048, 256), BF),
+            pltpu.VMEM((2, 2048, 256), F32),
+            pltpu.VMEM((2, 2048, 256), F32),
+            pltpu.VMEM((2048, 1024), BF),
+            pltpu.VMEM((2048, 1024), BF),
             pltpu.VMEM((2, 2048, 128), F32),
             pltpu.VMEM((2048, 128), F32),
             pltpu.VMEM((1024, 256), F32),
             pltpu.SMEM((16,), jnp.int32),
             pltpu.SemaphoreType.DMA((2,)),
         ],
-        compiler_params=pltpu.CompilerParams(vmem_limit_bytes=20 << 20),
+        compiler_params=pltpu.CompilerParams(vmem_limit_bytes=32 << 20),
     )(orders, own, other, w_uk, w_uv)
 
 
@@ -237,10 +245,11 @@
 def finish_kernel(keep_ref, met_ref, rope_ref, dq_ref, own_ref, oth_ref, out_ref):
     total = jnp.zeros((128, DL), F32)
     for i in range(0, 16, 2):
-        pair = keep_ref[i : i + 2].astype(F32) + met_ref[i : i + 2].astype(F32)
+        pair = keep_ref[i : i + 2].astype(F32) + met_ref[i : i + 2, 0:128, :].astype(F32)
         out_ref[i : i + 2, 0:128, :] = pair.astype(BF)
-        out_ref[i : i + 2, 128:192, :] = rope_ref[i : i + 2]
-        out_ref[i : i + 2, 192:256, :] = dq_ref[i : i + 2, 0:64, :]
+        rope = rope_ref[i : i + 2].astype(F32) + met_ref[i : i + 2, 128:192, :].astype(F32)
+        out_ref[i : i + 2, 128:192, :] = dq_ref[i : i + 2]
+        out_ref[i : i + 2, 192:256, :] = rope.astype(BF)
         lat = jnp.concatenate(
             [
                 jnp.concatenate([ref[j, t * HALF : (t + 1) * HALF, :] for t in range(4)], axis=1)
@@ -250,13 +259,7 @@
             axis=0,
         )
         total = total + dot(pair.reshape(256, 128).T.astype(BF), lat)
-    total = total.T
-    turned = pltpu.roll(total, DR, 1)
-    low = low_lanes((32, TOK))
-    for i in range(16):
-        for part, first in ((turned, 64), (total, 96)):
-            dq = dq_ref[i, first : first + 32, :].astype(F32)
-            out_ref[i, 192 + first : 224 + first, :] = jnp.where(low, dq, part[i * 32 : i * 32 + 32]).astype(BF)
+    out_ref[:, 256:288, :] = total.T.reshape(16, 32, 128).astype(BF)
 
 
 def latent_kernel(r_ref, uk_ref, uv_ref, own_out, first_out, second_out, third_out, all_s):
@@ -265,14 +268,10 @@
         [jnp.concatenate([r_ref[i, 64:128, :], r_ref[i, 0:64, :]], axis=0) for i in range(1, 16, 2)], axis=1
     )
     all_s[:DL, :] = (dot_nt(uk_ref[...], keys) + dot_nt(uv_ref[...], values)).astype(BF)
-    even = r_ref[0, 128:192, :].astype(F32)
-    odd = r_ref[1, 128:192, :].astype(F32)
-    for i in range(2, 16, 2):
-        even = even + r_ref[i, 128:192, :].astype(F32)
-        odd = odd + r_ref[i + 1, 128:192, :].astype(F32)
-    rope = even + pltpu.roll(odd, DR, 1)
-    rope = jnp.concatenate([rope, pltpu.roll(rope, DR, 1)], axis=0).T
-    all_s[DL:, :] = rope[:DR, :].astype(BF)
+    halves = [r_ref[c, 192:256, :].astype(F32) for c in range(2)]
+    for i in range(2, 16):
+        halves[i % 2] = halves[i % 2] + r_ref[i, 192:256, :].astype(F32)
+    all_s[DL:, :] = jnp.concatenate(halves, axis=0).T[DR:, :].astype(BF)
     mine = lax.axis_index("head") // 4
     for k, out in enumerate((own_out, first_out, second_out, third_out)):
         out[...] = all_s[pl.ds(pl.multiple_of((mine ^ k) * PART, 16), PART), :]
@@ -307,17 +306,15 @@
         for c in range(2):
             rows = slice(c * HALF, c * HALF + HALF)
             i, j, at = 2 * h + c, 2 * h + 2 + c, h * 192
-            q_ref[rows, at : at + 128] = r_ref[i, 192:256, :]
-            first = r_ref[i, 256:320, :].astype(F32)
-            second = pltpu.roll(r_ref[j, 256:320, :].astype(F32), DR, 1)
-            turned = pltpu.roll(r_ref[j, 192:256, :].astype(F32), DR, 1)
+            q_ref[rows, at : at + 128] = r_ref[i, 128:192, :]
+            first = r_ref[i, 192:256, :].astype(F32)
+            second = pltpu.roll(r_ref[j, 192:256, :].astype(F32), DR, 1)
+            turned = pltpu.roll(r_ref[j, 128:192, :].astype(F32), DR, 1)
             q_ref[rows, at + 128 : at + 256] = jnp.where(low, first, turned).astype(BF)
             q_ref[rows, at + 256 : at + 384] = jnp.where(low, turned, second).astype(BF)
     for i in range(16):
-        left = pltpu.roll(r_ref[i, 256:288, :].astype(F32), DR, 1)
-        right = r_ref[i, 288:320, :].astype(F32)
         ref = uv_ref if i % 2 else uk_ref
-        ref[:, (i // 2) * 128 : (i // 2) * 128 + 128] = jnp.where(low[0:32], left, right)
+        ref[:, (i // 2) * 128 : (i // 2) * 128 + 128] = r_ref[i, 256:288, :].astype(F32)
 
 
 def local(queries, latent, w_uk, w_uv, grad_out, positions, tool_result):

time: 103 us -> 101 us (0.981)
  blocking collectives: 53.6 us -> 52.3 us
    all_to_all x2, blocking collectives: 53.6 us -> 52.3 us  [exchange(): return lax.all_to_all(x, 'ctx', 0, 0, tiled=True, axis_index_groups=every)]
where the time goes in v3:
time: 101 us
  blocking collectives  52.3 us (52%)
  waiting for transfers between devices  17.5 us (17%)
  starting transfers between devices  16.9 us (17%)
  Pallas kernels  12.8 us (13%)
    all_to_all x2, blocking collectives, exchange(): return lax.all_to_all(x, 'ctx', 0, 0, tiled=True, axis_index_groups=every)  52.3 us
    ppermute x6, starting transfers between devices, along_x(): return lax.ppermute(x, 'head', [(i, i ^ 4 * k) for i in range(16)])  8.74 us
    ppermute x3, starting transfers between devices, along_z(): return lax.ppermute(x, 'head', [(i, i ^ k) for i in range(16)])  7.95 us
    pallas_call x1, Pallas kernels, attend(): pl.pallas_call(attend_kernel, in_specs=[pl.BlockSpec(memory_space=pltpu.S...  7.13 us
    ppermute x6, waiting for transfers between devices, along_x(): return lax.ppermute(x, 'head', [(i, i ^ 4 * k) for i in range(16)])  6.47 us
    ppermute x3, waiting for transfers between devices, along_z(): return lax.ppermute(x, 'head', [(i, i ^ k) for i in range(16)])  5.41 us
    ppermute x1, waiting for transfers between devices, local(): other = lax.ppermute(own, 'ctx', swap)  3.5 us
    pallas_call x1, Pallas kernels, pack(): pl.pallas_call(pack_kernel, in_specs=[pl.BlockSpec(memory_space=pl.ANY)]...  2.66 us
  transfers between devices with their start and end apart: 11, of which 8 were waited for; matrix products, arithmetic and copies ran while one was open for 0% of the time, Pallas kernels for 1%

profile of v3, /device:TPU:2, one launch (start us, length us, event | category | flops | bytes accessed | tf_op | source)
XLA Modules:
  0.0 100.6 jit_solution(2989179222473012058)
XLA Ops:
  0.6 2.7 %shard_map.102 = bf16[16,464,128]{2,1,0:T(8,128)(2,1)} custom-call(bf16[128,1536]{1,0:T(8,128)(2,1)} %q_hbm.1, bf16[576,128]{1,0:T(8,128)(2,1)} %bitcast.5, bf16[128,1024]{1,0:T(8,128)(2,1)} %g_hbm.1, s32[1,128]{1,0:T(1,128)} %bitcast.6, s32[1,128]{1,0:T(1,128)} %bitcast.7), custom_call_target="tpu_custom_call" | custom-call | tf_op jit(solution)/shard_map/pallas_call | solution.py:74
  3.3 0.0 copy-start
  3.3 0.0 copy-start.1
  3.3 31.7 %all_to_all.10.own_ref = bf16[16,464,128]{2,1,0:T(8,128)(2,1)S(1)} all-to-all(bf16[16,464,128]{2,1,0:T(8,128)(2,1)} %shard_map.102), channel_id=1, replica_groups={{0,16,32,48,64,80,96,112,128,144,160,176,192,208,224,240},{1,17,33,49,6..., dimensions={0} | all-to-all | bytes 3801088 | tf_op jit(solution)/shard_map/all_to_all | solution.py:325
  35.0 0.0 collective-permute-start
  35.0 0.4 fusion.ord_ref
  35.4 3.5 %collective-permute-done.oth_ref = bf16[16,464,128]{2,1,0:T(8,128)(2,1)S(1)} collective-permute-done((bf16[16,464,128]{2,1,0:T(8,128)(2,1)S(1)}, bf16[16,464,128]{2,1,0:T(8,128)(2,1)S(1)}, u32[]{:S(2)}, u32[]{:S(2)}) %collective-permute-start) | collective-permute-done | bytes 1900576 | tf_op jit(solution)/shard_map/ppermute | solution.py:334
  38.9 0.0 copy-done
  38.9 0.0 copy-done.1
  38.9 7.1 %shard_map.103 = (bf16[16,128,128]{2,1,0:T(8,128)(2,1)S(1)}, bf16[16,192,128]{2,1,0:T(8,128)(2,1)S(1)}, bf16[16,64,128]{2,1,0:T(8,128)(2,1)S(1)}, bf16[16,64,128]{2,1,0:T(8,128)(2,1)S(1)}) custom-call(s32[16]{0:T(128)S(1)} %fusion.ord_ref, bf16[16,464,128]{2,1,0:T(8,128)(2,1)S(1)} %all_to_all.10.own_ref, ...), custom_call_target="tpu_custom_call" | custom-call | tf_op jit(solution)/shard_map/pallas_call | solution.py:203
  46.0 0.2 collective-permute-start.1
  46.3 2.1 %collective-permute-done.1.met_ref = bf16[16,192,128]{2,1,0:T(8,128)(2,1)S(1)} collective-permute-done((bf16[16,192,128]{2,1,0:T(8,128)(2,1)S(1)}, bf16[16,192,128]{2,1,0:T(8,128)(2,1)S(1)}, u32[]{:S(2)}, u32[]{:S(2)}) %collective-permute-start.1) | collective-permute-done | bytes 786464 | tf_op jit(solution)/shard_map/ppermute | solution.py:337
  48.4 0.6 shard_map.104
  49.0 20.6 %all_to_all.11.r_ref = bf16[16,288,128]{2,1,0:T(8,128)(2,1)S(1)} all-to-all(bf16[16,288,128]{2,1,0:T(8,128)(2,1)S(1)} %shard_map.104), channel_id=1, replica_groups={{0,16,32,48,64,80,96,112,128,144,160,176,192,208,224,240},{1,17,33,49,6..., dimensions={0} | all-to-all | bytes 2359296 | tf_op jit(solution)/shard_map/all_to_all | solution.py:325
  69.6 0.7 shard_map.106
  70.3 0.6 collective-permute-start.2
  70.9 2.4 %collective-permute-start.3 = (bf16[144,128]{1,0:T(8,128)(2,1)S(1)}, bf16[144,128]{1,0:T(8,128)(2,1)S(1)}, u32[]{:S(2)}, u32[]{:S(2)}) collective-permute-start(bf16[144,128]{1,0:T(8,128)(2,1)S(1)} %get-tuple-element.22), channel_id=1, source_target_pairs={{0,8},{1,9},{2,10},{3,11},{4,12},{5,13},{6,14},{7,15},{8,0},{9,1},... | collective-permute-start | bytes 110600 | tf_op jit(solution)/shard_map/ppermute | solution.py:328
  73.3 0.5 collective-permute-start.4
  73.9 0.5 collective-permute-done.2.b_ref
  74.3 2.0 %collective-permute-done.3.c_ref = bf16[144,128]{1,0:T(8,128)(2,1)S(1)} collective-permute-done((bf16[144,128]{1,0:T(8,128)(2,1)S(1)}, bf16[144,128]{1,0:T(8,128)(2,1)S(1)}, u32[]{:S(2)}, u32[]{:S(2)}) %collective-permute-start.3) | collective-permute-done | bytes 36896 | tf_op jit(solution)/shard_map/ppermute | solution.py:328
  76.4 0.9 collective-permute-done.4.d_ref
  77.3 5.5 %collective-permute-start.7 = (bf16[144,128]{1,0:T(8,128)(2,1)S(1)}, bf16[144,128]{1,0:T(8,128)(2,1)S(1)}, u32[]{:S(2)}, u32[]{:S(2)}) collective-permute-start(bf16[144,128]{1,0:T(8,128)(2,1)S(1)} %shard_map.107.a_ref), channel_id=1, source_target_pairs={{0,3},{1,2},{2,1},{3,0},{4,7},{5,6},{6,5},{7,4},{8,11},{9,10},{10,... | collective-permute-start | bytes 110600 | tf_op jit(solution)/shard_map/ppermute | solution.py:331
  82.8 1.4 %collective-permute-start.6 = (bf16[144,128]{1,0:T(8,128)(2,1)S(1)}, bf16[144,128]{1,0:T(8,128)(2,1)S(1)}, u32[]{:S(2)}, u32[]{:S(2)}) collective-permute-start(bf16[144,128]{1,0:T(8,128)(2,1)S(1)} %shard_map.107.a_ref), channel_id=1, source_target_pairs={{0,2},{1,3},{2,0},{3,1},{4,6},{5,7},{6,4},{7,5},{8,10},{9,11},{10,... | collective-permute-start | bytes 110600 | tf_op jit(solution)/shard_map/ppermute | solution.py:331
  84.2 1.0 %collective-permute-start.5 = (bf16[144,128]{1,0:T(8,128)(2,1)S(1)}, bf16[144,128]{1,0:T(8,128)(2,1)S(1)}, u32[]{:S(2)}, u32[]{:S(2)}) collective-permute-start(bf16[144,128]{1,0:T(8,128)(2,1)S(1)} %shard_map.107.a_ref), channel_id=1, source_target_pairs={{0,1},{1,0},{2,3},{3,2},{4,5},{5,4},{6,7},{7,6},{8,9},{9,8},{10,11... | collective-permute-start | bytes 110600 | tf_op jit(solution)/shard_map/ppermute | solution.py:331
  85.3 0.0 collective-permute-done.7.d_ref
  85.3 5.4 %collective-permute-done.6.c_ref = bf16[144,128]{1,0:T(8,128)(2,1)S(1)} collective-permute-done((bf16[144,128]{1,0:T(8,128)(2,1)S(1)}, bf16[144,128]{1,0:T(8,128)(2,1)S(1)}, u32[]{:S(2)}, u32[]{:S(2)}) %collective-permute-start.6) | collective-permute-done | bytes 36896 | tf_op jit(solution)/shard_map/ppermute | solution.py:331
  90.7 0.0 collective-permute-done.5.b_ref
  90.7 1.3 %collective-permute-start.10 = (bf16[144,128]{1,0:T(8,128)(2,1)S(1)}, bf16[144,128]{1,0:T(8,128)(2,1)S(1)}, u32[]{:S(2)}, u32[]{:S(2)}) collective-permute-start(bf16[144,128]{1,0:T(8,128)(2,1)S(1)} %shard_map.108.a_ref), channel_id=1, source_target_pairs={{0,12},{1,13},{2,14},{3,15},{4,8},{5,9},{6,10},{7,11},{8,4},{9,5},... | collective-permute-start | bytes 110600 | tf_op jit(solution)/shard_map/ppermute | solution.py:328
  92.0 3.8 %collective-permute-start.9 = (bf16[144,128]{1,0:T(8,128)(2,1)S(1)}, bf16[144,128]{1,0:T(8,128)(2,1)S(1)}, u32[]{:S(2)}, u32[]{:S(2)}) collective-permute-start(bf16[144,128]{1,0:T(8,128)(2,1)S(1)} %shard_map.108.a_ref), channel_id=1, source_target_pairs={{0,8},{1,9},{2,10},{3,11},{4,12},{5,13},{6,14},{7,15},{8,0},{9,1},... | collective-permute-start | bytes 110600 | tf_op jit(solution)/shard_map/ppermute | solution.py:328
  95.9 0.0 collective-permute-start.8
  95.9 0.9 shard_map.105
  96.8 0.0 collective-permute-done.10.d_ref
  96.8 1.0 collective-permute-done.9.c_ref
  97.8 2.0 %collective-permute-done.8.b_ref = bf16[144,128]{1,0:T(8,128)(2,1)S(1)} collective-permute-done((bf16[144,128]{1,0:T(8,128)(2,1)S(1)}, bf16[144,128]{1,0:T(8,128)(2,1)S(1)}, u32[]{:S(2)}, u32[]{:S(2)}) %collective-permute-start.8) | collective-permute-done | bytes 36896 | tf_op jit(solution)/shard_map/ppermute | solution.py:328
  99.8 0.7 shard_map.109
  (2 shorter events, 0.0 us)
Async XLA Ops:
  3.3 35.6 %copy-start = (bf16[512,1024]{1,0:T(8,128)(2,1)S(1)}, bf16[512,1024]{1,0:T(8,128)(2,1)}, u32[]{:S(2)}) copy-start(bf16[512,1024]{1,0:T(8,128)(2,1)} %uk_ref.3) | copy-start | bytes 3145732
  3.3 35.6 %copy-start.1 = (bf16[512,1024]{1,0:T(8,128)(2,1)S(1)}, bf16[512,1024]{1,0:T(8,128)(2,1)}, u32[]{:S(2)}) copy-start(bf16[512,1024]{1,0:T(8,128)(2,1)} %uv_ref.3) | copy-start | bytes 3145732
  35.0 3.9 %collective-permute-start = (bf16[16,464,128]{2,1,0:T(8,128)(2,1)S(1)}, bf16[16,464,128]{2,1,0:T(8,128)(2,1)S(1)}, u32[]{:S(2)}, u32[]{:S(2)}) collective-permute-start(bf16[16,464,128]{2,1,0:T(8,128)(2,1)S(1)} %all_to_all.10.own_ref), channel_id=1, source_target_pairs={{0,16},{16,0},{32,48},{48,32},{64,80},{80,64},{96,112},{112,96},{1... | collective-permute-start | bytes 5701640 | tf_op jit(solution)/shard_map/ppermute | solution.py:334
  46.0 2.4 %collective-permute-start.1 = (bf16[16,192,128]{2,1,0:T(8,128)(2,1)S(1)}, bf16[16,192,128]{2,1,0:T(8,128)(2,1)S(1)}, u32[]{:S(2)}, u32[]{:S(2)}) collective-permute-start(bf16[16,192,128]{2,1,0:T(8,128)(2,1)S(1)} %get-tuple-element.16), channel_id=1, source_target_pairs={{0,16},{16,0},{32,48},{48,32},{64,80},{80,64},{96,112},{112,96},{1... | collective-permute-start | bytes 2359304 | tf_op jit(solution)/shard_map/ppermute | solution.py:337
  70.3 4.0 %collective-permute-start.2 = (bf16[144,128]{1,0:T(8,128)(2,1)S(1)}, bf16[144,128]{1,0:T(8,128)(2,1)S(1)}, u32[]{:S(2)}, u32[]{:S(2)}) collective-permute-start(bf16[144,128]{1,0:T(8,128)(2,1)S(1)} %get-tuple-element.21), channel_id=1, source_target_pairs={{0,4},{1,5},{2,6},{3,7},{4,0},{5,1},{6,2},{7,3},{8,12},{9,13},{10,... | collective-permute-start | bytes 110600 | tf_op jit(solution)/shard_map/ppermute | solution.py:328
  70.9 5.5 %collective-permute-start.3 = (bf16[144,128]{1,0:T(8,128)(2,1)S(1)}, bf16[144,128]{1,0:T(8,128)(2,1)S(1)}, u32[]{:S(2)}, u32[]{:S(2)}) collective-permute-start(bf16[144,128]{1,0:T(8,128)(2,1)S(1)} %get-tuple-element.22), channel_id=1, source_target_pairs={{0,8},{1,9},{2,10},{3,11},{4,12},{5,13},{6,14},{7,15},{8,0},{9,1},... | collective-permute-start | bytes 110600 | tf_op jit(solution)/shard_map/ppermute | solution.py:328
  73.3 4.0 %collective-permute-start.4 = (bf16[144,128]{1,0:T(8,128)(2,1)S(1)}, bf16[144,128]{1,0:T(8,128)(2,1)S(1)}, u32[]{:S(2)}, u32[]{:S(2)}) collective-permute-start(bf16[144,128]{1,0:T(8,128)(2,1)S(1)} %get-tuple-element.23), channel_id=1, source_target_pairs={{0,12},{1,13},{2,14},{3,15},{4,8},{5,9},{6,10},{7,11},{8,4},{9,5},... | collective-permute-start | bytes 110600 | tf_op jit(solution)/shard_map/ppermute | solution.py:328
  77.3 7.9 %collective-permute-start.7 = (bf16[144,128]{1,0:T(8,128)(2,1)S(1)}, bf16[144,128]{1,0:T(8,128)(2,1)S(1)}, u32[]{:S(2)}, u32[]{:S(2)}) collective-permute-start(bf16[144,128]{1,0:T(8,128)(2,1)S(1)} %shard_map.107.a_ref), channel_id=1, source_target_pairs={{0,3},{1,2},{2,1},{3,0},{4,7},{5,6},{6,5},{7,4},{8,11},{9,10},{10,... | collective-permute-start | bytes 110600 | tf_op jit(solution)/shard_map/ppermute | solution.py:331
  82.8 7.9 %collective-permute-start.6 = (bf16[144,128]{1,0:T(8,128)(2,1)S(1)}, bf16[144,128]{1,0:T(8,128)(2,1)S(1)}, u32[]{:S(2)}, u32[]{:S(2)}) collective-permute-start(bf16[144,128]{1,0:T(8,128)(2,1)S(1)} %shard_map.107.a_ref), channel_id=1, source_target_pairs={{0,2},{1,3},{2,0},{3,1},{4,6},{5,7},{6,4},{7,5},{8,10},{9,11},{10,... | collective-permute-start | bytes 110600 | tf_op jit(solution)/shard_map/ppermute | solution.py:331
  84.2 6.4 %collective-permute-start.5 = (bf16[144,128]{1,0:T(8,128)(2,1)S(1)}, bf16[144,128]{1,0:T(8,128)(2,1)S(1)}, u32[]{:S(2)}, u32[]{:S(2)}) collective-permute-start(bf16[144,128]{1,0:T(8,128)(2,1)S(1)} %shard_map.107.a_ref), channel_id=1, source_target_pairs={{0,1},{1,0},{2,3},{3,2},{4,5},{5,4},{6,7},{7,6},{8,9},{9,8},{10,11... | collective-permute-start | bytes 110600 | tf_op jit(solution)/shard_map/ppermute | solution.py:331
  90.7 6.1 %collective-permute-start.10 = (bf16[144,128]{1,0:T(8,128)(2,1)S(1)}, bf16[144,128]{1,0:T(8,128)(2,1)S(1)}, u32[]{:S(2)}, u32[]{:S(2)}) collective-permute-start(bf16[144,128]{1,0:T(8,128)(2,1)S(1)} %shard_map.108.a_ref), channel_id=1, source_target_pairs={{0,12},{1,13},{2,14},{3,15},{4,8},{5,9},{6,10},{7,11},{8,4},{9,5},... | collective-permute-start | bytes 110600 | tf_op jit(solution)/shard_map/ppermute | solution.py:328
  92.0 5.8 %collective-permute-start.9 = (bf16[144,128]{1,0:T(8,128)(2,1)S(1)}, bf16[144,128]{1,0:T(8,128)(2,1)S(1)}, u32[]{:S(2)}, u32[]{:S(2)}) collective-permute-start(bf16[144,128]{1,0:T(8,128)(2,1)S(1)} %shard_map.108.a_ref), channel_id=1, source_target_pairs={{0,8},{1,9},{2,10},{3,11},{4,12},{5,13},{6,14},{7,15},{8,0},{9,1},... | collective-permute-start | bytes 110600 | tf_op jit(solution)/shard_map/ppermute | solution.py:328
  95.9 4.0 %collective-permute-start.8 = (bf16[144,128]{1,0:T(8,128)(2,1)S(1)}, bf16[144,128]{1,0:T(8,128)(2,1)S(1)}, u32[]{:S(2)}, u32[]{:S(2)}) collective-permute-start(bf16[144,128]{1,0:T(8,128)(2,1)S(1)} %shard_map.108.a_ref), channel_id=1, source_target_pairs={{0,4},{1,5},{2,6},{3,7},{4,0},{5,1},{6,2},{7,3},{8,12},{9,13},{10,... | collective-permute-start | bytes 110600 | tf_op jit(solution)/shard_map/ppermute | solution.py:328

commit v4 on v3

--- a/solution.py
+++ b/solution.py
@@ -17,7 +17,6 @@
 ROWS = 464
 BACK = 288
 PART = (DL + DR) // 4
-CHUNK = 512
 MASKED = -1e30
 BF = jnp.bfloat16
 F32 = jnp.float32
@@ -88,80 +87,123 @@
     )(queries, lat_t, grad_out, positions.reshape(1, TOK), tool_result.reshape(1, TOK))
 
 
-def attend_kernel(ord_ref, own_ref, oth_ref, uk_ref, uv_ref, keep_out, give_out, dq_out, rope_out,
-                  weights, kv, ts, kt, qs, cs, s_sc, g_sc, ds_sc, p_sc, kvg, dr, dqs, source, sems):
-    scale = (DN + DR) ** -0.5
-    me = lax.axis_index("ctx")
-    core = lax.rem(me, 2)
-    columns = pl.ds(pl.multiple_of((me // 2) * 128, 128), 128)
+FACTOR = (DN + DR) ** -0.5 * math.log2(math.e)
+
+
+def project(ref, source, weights, keys, values, ropes, turned):
+    for b in range(4):
+        rows = slice(b * 256, b * 256 + 256)
+        four = [source[4 * b + k] for k in range(4)]
+        tokens = jnp.concatenate(
+            [jnp.concatenate([ref[i, t * HALF : (t + 1) * HALF, :] for t in range(4)], axis=1) for i in four], axis=0
+        )
+        both = dot(tokens, weights[...])
+        rope = jnp.concatenate([ref[i, 256:320, :] for i in four], axis=0)
+        key = both[:, 0:128].astype(BF)
+        keys[rows, :] = key
+        values[rows, :] = both[:, 128:256].astype(BF)
+        ropes[rows, :] = rope
+        turned[0:128, rows] = key.astype(F32).T.astype(BF)
+        turned[128:256, rows] = rope.astype(F32).T.astype(BF)
+
+
+def fetch_weights(uk_ref, uv_ref, weights, sems):
+    columns = pl.ds(pl.multiple_of((lax.axis_index("ctx") // 2) * 128, 128), 128)
     copies = [
         pltpu.make_async_copy(ref.at[:, columns], weights.at[:, i * 128 : i * 128 + 128], sems.at[i])
         for i, ref in enumerate((uk_ref, uv_ref))
     ]
     for copy in copies:
         copy.start()
+    return copies
+
+
+def own_kernel(ord_ref, own_ref, uk_ref, uv_ref, qs, cs, keys, values, ropes, turned, s_out, g_out, top_out,
+               weights, source, sems):
+    copies = fetch_weights(uk_ref, uv_ref, weights, sems)
     for s in range(16):
         source[ord_ref[s]] = s
-
     low = low_lanes((HALF, TOK))
     for b in range(16):
         rows = slice(b * HALF, (b + 1) * HALF)
-        turned = pltpu.roll(own_ref[source[b], 256:320, :].astype(F32), DR, 1)
+        rope = pltpu.roll(own_ref[source[b], 256:320, :].astype(F32), DR, 1)
         qs[rows, 0:128] = own_ref[source[b], 320:384, :]
-        qs[rows, 128:256] = jnp.where(low, 0.0, turned).astype(BF)
+        qs[rows, 128:256] = jnp.where(low, 0.0, rope).astype(BF)
         cs[rows, :] = own_ref[source[b], 384:448, :]
     for copy in copies:
         copy.wait()
-    for b in range(8):
-        rows = slice(b * 256, b * 256 + 256)
-        four = [(ref, source[2 * b + k]) for k in range(2) for ref in (own_ref, oth_ref)]
-        tokens = jnp.concatenate(
-            [
-                jnp.concatenate([ref[i, t * HALF : (t + 1) * HALF, :] for t in range(4)], axis=1)
-                for ref, i in four
-            ],
-            axis=0,
-        )
-        both = dot(tokens, weights[...])
-        rope = jnp.concatenate([ref[i, 256:320, :] for ref, i in four], axis=0)
-        keys = both[:, 0:128].astype(BF)
-        kv[0, rows, :] = keys
-        kv[1, rows, :] = both[:, 128:256].astype(BF)
-        ts[rows, :] = rope
-        kt[0:128, rows] = keys.astype(F32).T.astype(BF)
-        kt[128:256, rows] = rope.astype(F32).T.astype(BF)
-
-    factor = scale * math.log2(math.e)
-    lane = lax.broadcasted_iota(jnp.int32, (CHUNK, 256), 1)
-    qpos = (lane // HALF) * TOK + core * HALF + lax.rem(lane, HALF)
-    row = lax.broadcasted_iota(jnp.int32, (CHUNK, 256), 0)
-    kpos = (row // TOK) * TOK + lax.rem(lax.rem(row, TOK) + core * HALF, TOK)
-    visible = kpos <= qpos
-    spans = [slice(c * CHUNK, (c + 1) * CHUNK) for c in range(4)]
+    project(own_ref, source, weights, keys, values, ropes, turned)
+    visible = lax.broadcasted_iota(jnp.int32, (256, 256), 0) <= lax.broadcasted_iota(jnp.int32, (256, 256), 1)
+    for p in range(4):
+        rows, first = slice(p * 256, p * 256 + 256), 128 * p * (p + 1)
+        top = jnp.full((8, 256), MASKED, F32)
+        for c in range(p + 1):
+            at, to = slice(c * 256, c * 256 + 256), slice(first + c * 256, first + c * 256 + 256)
+            sc = dot_nt(jnp.concatenate([keys[at, :], ropes[at, :]], axis=1), qs[rows, :]) * FACTOR
+            if c == p:
+                sc = jnp.where(visible, sc, MASKED)
+            s_out[to, :] = sc
+            g_out[to, :] = dot_nt(values[at, :], cs[rows, :])
+            top = jnp.maximum(top, jnp.max(sc.reshape(32, 8, 256), axis=0))
+        top_out[p, :, :] = top
+
+
+def own_side(orders, own, w_uk, w_uv):
+    whole = pl.BlockSpec(memory_space=pltpu.VMEM)
+    anywhere = pl.BlockSpec(memory_space=pl.ANY)
+    shapes = [(1024, 256), (1024, 128), (1024, 128), (1024, 128), (1024, 128), (256, 1024)]
+    return pl.pallas_call(
+        own_kernel,
+        in_specs=[pl.BlockSpec(memory_space=pltpu.SMEM), whole, anywhere, anywhere],
+        out_specs=[whole] * 9,
+        out_shape=[jax.ShapeDtypeStruct(shape, BF) for shape in shapes]
+        + [jax.ShapeDtypeStruct(shape, F32) for shape in ((2560, 256), (2560, 256), (4, 8, 256))],
+        scratch_shapes=[pltpu.VMEM((DL, 256), BF), pltpu.SMEM((16,), jnp.int32), pltpu.SemaphoreType.DMA((2,))],
+        compiler_params=pltpu.CompilerParams(vmem_limit_bytes=12 << 20),
+    )(orders, own, w_uk, w_uv)
+
+
+def attend_kernel(ord_ref, oth_ref, uk_ref, uv_ref, qs, cs, own_keys, own_values, own_ropes, own_turned, s_own, g_own,
+                  top_own, keep_out, give_out, dq_out, rope_out,
+                  weights, keys, values, ropes, turned, s_sc, g_sc, ds_sc, p_sc, kvg, dr, dqs, source, sems):
+    scale = (DN + DR) ** -0.5
+    core = lax.rem(lax.axis_index("ctx"), 2)
+    copies = fetch_weights(uk_ref, uv_ref, weights, sems)
+    for s in range(16):
+        source[ord_ref[s]] = s
+    for copy in copies:
+        copy.wait()
+    project(oth_ref, source, weights, keys, values, ropes, turned)
+    row = lax.broadcasted_iota(jnp.int32, (256, 256), 0) // HALF
+    lane = lax.broadcasted_iota(jnp.int32, (256, 256), 1) // HALF
+    visible = row < lane + core
+    spans = [slice(c * 256, (c + 1) * 256) for c in range(4)]
 
     def score(p, c):
-        rows, at = slice(p * 256, p * 256 + 256), spans[c]
-        s = dot_nt(jnp.concatenate([kv[0, at, :], ts[at, :]], axis=1), qs[rows, :]) * factor
+        at = spans[c]
+        sc = dot_nt(jnp.concatenate([keys[at, :], ropes[at, :]], axis=1), qs[spans[p], :]) * FACTOR
         if c == p:
-            s = jnp.where(visible, s, MASKED)
-        s_sc[p % 2, at, :] = s
-        g_sc[p % 2, at, :] = dot_nt(kv[1, at, :], cs[rows, :])
-        return jnp.max(s.reshape(CHUNK // 8, 8, 256), axis=0)
+            sc = jnp.where(visible, sc, MASKED)
+        s_sc[p % 2, 1, at, :] = sc
+        g_sc[p % 2, at, :] = dot_nt(values[at, :], cs[spans[p], :])
+        return jnp.max(sc.reshape(32, 8, 256), axis=0)
 
     tops = [score(0, 0)]
     for p in range(4):
-        rows = slice(p * 256, p * 256 + 256)
-        top = functools.reduce(jnp.maximum, tops)
+        rows, first = spans[p], 128 * p * (p + 1)
+        top = functools.reduce(jnp.maximum, tops, top_own[p])
         tops = []
         top = jnp.max(top, axis=0, keepdims=True)
         total = jnp.zeros((8, 256), F32)
         mixed = jnp.zeros((8, 256), F32)
         for c in range(p + 1):
-            at = spans[c]
-            e = jnp.exp2(s_sc[p % 2, at, :] - top)
-            s_sc[p % 2, at, :] = e
-            total = total + jnp.sum(e.reshape(CHUNK // 8, 8, 256), axis=0)
-            mixed = mixed + jnp.sum((e * g_sc[p % 2, at, :]).reshape(CHUNK // 8, 8, 256), axis=0)
+            at, of = spans[c], slice(first + c * 256, first + c * 256 + 256)
+            for side in range(2):
+                e = jnp.exp2((s_sc[p % 2, 1, at, :] if side else s_own[of, :]) - top)
+                g = g_sc[p % 2, at, :] if side else g_own[of, :]
+                s_sc[p % 2, side, at, :] = e
+                total = total + jnp.sum(e.reshape(32, 8, 256), axis=0)
+                mixed = mixed + jnp.sum((e * g).reshape(32, 8, 256), axis=0)
             if p < 3:
                 tops.append(score(p + 1, c))
         share = 1.0 / jnp.sum(total, axis=0, keepdims=True)
@@ -169,40 +211,44 @@
         if p < 3:
             tops.append(score(p + 1, p + 1))
         for c in range(p + 1):
-            at = spans[c]
-            prob = s_sc[p % 2, at, :] * share
-            ds_sc[at, rows] = (prob * (g_sc[p % 2, at, :] - delta)).astype(BF)
-            p_sc[at, rows] = prob.astype(BF)
-        upto = (p + 1) * CHUNK
-        dqs[rows, :] = (dot(kt[:, 0:upto], ds_sc[0:upto, rows]) * scale).T
+            at, of = spans[c], slice(first + c * 256, first + c * 256 + 256)
+            for side in range(2):
+                prob = s_sc[p % 2, side, at, :] * share
+                g = g_sc[p % 2, at, :] if side else g_own[of, :]
+                ds_sc[side, at, rows] = (prob * (g - delta)).astype(BF)
+                p_sc[side, at, rows] = prob.astype(BF)
+        upto = (p + 1) * 256
+        dq = dot(own_turned[:, 0:upto], ds_sc[0, 0:upto, rows]) + dot(turned[:, 0:upto], ds_sc[1, 0:upto, rows])
+        dqs[rows, :] = (dq * scale).T
     for c in range(4):
         at = spans[c]
-        key_part = dot(ds_sc[at, c * 256 :], qs[c * 256 :, :])
-        kvg[0, at, :] = key_part[:, 0:128]
-        dr[at, :] = key_part[:, 128:256]
-        kvg[1, at, :] = dot(p_sc[at, c * 256 :], cs[c * 256 :, :])
-
+        for side in range(2):
+            key_part = dot(ds_sc[side, at, c * 256 :], qs[c * 256 :, :])
+            kvg[0, side, at, :] = key_part[:, 0:128]
+            dr[side, at, :] = key_part[:, 128:256]
+            kvg[1, side, at, :] = dot(p_sc[side, at, c * 256 :], cs[c * 256 :, :])
+
+    low = low_lanes((HALF, TOK))
     keep_scale = jnp.where(core == 0, scale, 1.0)
     give_scale = jnp.where(core == 0, 1.0, scale)
     for s in range(16):
-        at = pl.multiple_of(ord_ref[s] * TOK, TOK)
-        own_half, oth_half = pl.ds(at, HALF), pl.ds(at + HALF, HALF)
-        of = pl.ds(pl.multiple_of(ord_ref[s] * HALF, HALF), HALF)
-        keep_out[s, :, :] = (kvg[core, pl.ds(at, TOK), :] * keep_scale).astype(BF)
-        give_out[s, 0:64, :] = (kvg[1 - core, oth_half, :] * give_scale).astype(BF)
-        give_out[s, 64:128, :] = (kvg[1 - core, own_half, :] * give_scale).astype(BF)
-        give_out[s, 128:192, :] = (dr[oth_half, :] * scale).astype(BF)
-        dq_out[s, :, :] = dqs[of, 0:128].astype(BF)
-        turned = pltpu.roll(dqs[of, 128:256], DR, 1)
-        rope_out[s, :, :] = jnp.where(low, turned, dr[own_half, :] * scale).astype(BF)
-
-
-def attend(orders, own, other, w_uk, w_uv):
+        at = pl.ds(pl.multiple_of(ord_ref[s] * HALF, HALF), HALF)
+        for side in range(2):
+            half = slice(side * HALF, side * HALF + HALF)
+            keep_out[s, half, :] = (kvg[core, side, at, :] * keep_scale).astype(BF)
+            give_out[s, half, :] = (kvg[1 - core, 1 - side, at, :] * give_scale).astype(BF)
+        give_out[s, 128:192, :] = (dr[1, at, :] * scale).astype(BF)
+        dq_out[s, :, :] = dqs[at, 0:128].astype(BF)
+        moved = pltpu.roll(dqs[at, 128:256], DR, 1)
+        rope_out[s, :, :] = jnp.where(low, moved, dr[0, at, :] * scale).astype(BF)
+
+
+def attend(orders, other, w_uk, w_uv, mine):
     whole = pl.BlockSpec(memory_space=pltpu.VMEM)
     anywhere = pl.BlockSpec(memory_space=pl.ANY)
     return pl.pallas_call(
         attend_kernel,
-        in_specs=[pl.BlockSpec(memory_space=pltpu.SMEM), whole, whole, anywhere, anywhere],
+        in_specs=[pl.BlockSpec(memory_space=pltpu.SMEM), whole, anywhere, anywhere] + [whole] * 9,
         out_specs=[whole, whole, whole, whole],
         out_shape=[
             jax.ShapeDtypeStruct((16, TOK, 128), BF),
@@ -212,23 +258,22 @@
         ],
         scratch_shapes=[
             pltpu.VMEM((DL, 256), BF),
-            pltpu.VMEM((2, 2048, 128), BF),
-            pltpu.VMEM((2048, 128), BF),
-            pltpu.VMEM((256, 2048), BF),
-            pltpu.VMEM((1024, 256), BF),
             pltpu.VMEM((1024, 128), BF),
-            pltpu.VMEM((2, 2048, 256), F32),
-            pltpu.VMEM((2, 2048, 256), F32),
-            pltpu.VMEM((2048, 1024), BF),
-            pltpu.VMEM((2048, 1024), BF),
-            pltpu.VMEM((2, 2048, 128), F32),
-            pltpu.VMEM((2048, 128), F32),
+            pltpu.VMEM((1024, 128), BF),
+            pltpu.VMEM((1024, 128), BF),
+            pltpu.VMEM((256, 1024), BF),
+            pltpu.VMEM((2, 2, 1024, 256), F32),
+            pltpu.VMEM((2, 1024, 256), F32),
+            pltpu.VMEM((2, 1024, 1024), BF),
+            pltpu.VMEM((2, 1024, 1024), BF),
+            pltpu.VMEM((2, 2, 1024, 128), F32),
+            pltpu.VMEM((2, 1024, 128), F32),
             pltpu.VMEM((1024, 256), F32),
             pltpu.SMEM((16,), jnp.int32),
             pltpu.SemaphoreType.DMA((2,)),
         ],
-        compiler_params=pltpu.CompilerParams(vmem_limit_bytes=32 << 20),
-    )(orders, own, other, w_uk, w_uv)
+        compiler_params=pltpu.CompilerParams(vmem_limit_bytes=28 << 20),
+    )(orders, other, w_uk, w_uv, *mine)
 
 
 def small(kernel, inputs, outputs):
@@ -333,7 +378,8 @@
     own = exchange(pack(queries, latent.T, grad_out, positions, tool_result))
     other = lax.ppermute(own, "ctx", swap)
     orders = own[:, 448, 0].astype(jnp.int32)
-    keep, give, dq, rope = attend(orders, own, other, w_uk, w_uv)
+    mine = own_side(orders, own, w_uk, w_uv)
+    keep, give, dq, rope = attend(orders, other, w_uk, w_uv, mine)
     met = lax.ppermute(give, "ctx", swap)
     (back,) = small(finish_kernel, (keep, met, rope, dq, own, other), [((16, BACK, 128), BF)])
     received = exchange(back)

time: 101 us -> 99.6 us (0.986)
  waiting for transfers between devices: 17.5 us -> 15.5 us
    ppermute x1, waiting for transfers between devices: 3.5 us -> 1.48 us  [local(): other = lax.ppermute(own, 'ctx', swap)]
    pallas_call x0 -> x1, Pallas kernels: none -> 1.99 us  [own_side(): pl.pallas_call(own_kernel, in_specs=[pl.BlockSpec(memory_space=pltpu.SMEM...]
    pallas_call x1, Pallas kernels: 7.13 us -> 5.96 us  [attend(): pl.pallas_call(attend_kernel, in_specs=[pl.BlockSpec(memory_space=pltpu.S...]
  transfers between devices with their start and end apart: 11 -> 11, of which waited for: 8 -> 8; matrix products, arithmetic and copies ran while one was open for 0% -> 0% of each run, Pallas kernels for 1% -> 3%
where the time goes in v4:
time: 99.6 us; the launch traced here: 99.4 us
  blocking collectives  52.3 us (53%)
  starting transfers between devices  16.9 us (17%)
  waiting for transfers between devices  15.5 us (16%)
  Pallas kernels  13.6 us (14%)
    all_to_all x2, blocking collectives, exchange(): return lax.all_to_all(x, 'ctx', 0, 0, tiled=True, axis_index_groups=every)  52.3 us
    ppermute x6, starting transfers between devices, along_x(): return lax.ppermute(x, 'head', [(i, i ^ 4 * k) for i in range(16)])  8.76 us
    ppermute x3, starting transfers between devices, along_z(): return lax.ppermute(x, 'head', [(i, i ^ k) for i in range(16)])  7.94 us
    ppermute x6, waiting for transfers between devices, along_x(): return lax.ppermute(x, 'head', [(i, i ^ 4 * k) for i in range(16)])  6.46 us
    pallas_call x1, Pallas kernels, attend(): pl.pallas_call(attend_kernel, in_specs=[pl.BlockSpec(memory_space=pltpu.S...  5.96 us
    ppermute x3, waiting for transfers between devices, along_z(): return lax.ppermute(x, 'head', [(i, i ^ k) for i in range(16)])  5.41 us
    pallas_call x1, Pallas kernels, pack(): pl.pallas_call(pack_kernel, in_specs=[pl.BlockSpec(memory_space=pl.ANY)]...  2.66 us
    pallas_call x5, Pallas kernels, small(): pl.pallas_call(kernel, in_specs=[whole] * len(inputs), out_specs=[whole]...  2.31 us
  transfers between devices with their start and end apart: 11, of which 8 were waited for; matrix products, arithmetic and copies ran while one was open for 0% of the time, Pallas kernels for 3%

profile of v4, /device:TPU:2, one launch (start us, length us, event | category | flops | bytes accessed | tf_op | source)
XLA Modules:
  0.0 99.4 jit_solution(6871167278826710398)
XLA Ops:
  0.6 2.7 %shard_map.102 = bf16[16,464,128]{2,1,0:T(8,128)(2,1)} custom-call(bf16[128,1536]{1,0:T(8,128)(2,1)} %q_hbm.1, bf16[576,128]{1,0:T(8,128)(2,1)} %bitcast.5, bf16[128,1024]{1,0:T(8,128)(2,1)} %g_hbm.1, s32[1,128]{1,0:T(1,128)} %bitcast.6, s32[1,128]{1,0:T(1,128)} %bitcast.7), custom_call_target="tpu_custom_call" | custom-call | tf_op jit(solution)/shard_map/pallas_call | solution.py:73
  3.3 0.0 copy-start
  3.3 0.0 copy-start.1
  3.3 31.7 %all_to_all.10.own_ref = bf16[16,464,128]{2,1,0:T(8,128)(2,1)S(1)} all-to-all(bf16[16,464,128]{2,1,0:T(8,128)(2,1)} %shard_map.102), channel_id=1, replica_groups={{0,16,32,48,64,80,96,112,128,144,160,176,192,208,224,240},{1,17,33,49,6..., dimensions={0} | all-to-all | bytes 3801088 | tf_op jit(solution)/shard_map/all_to_all | solution.py:370
  35.0 0.0 collective-permute-start
  35.0 0.4 fusion.ord_ref
  35.4 0.0 copy-done
  35.4 0.0 copy-done.1
  35.4 2.0 %shard_map.103 = (bf16[1024,256]{1,0:T(8,128)(2,1)S(1)}, bf16[1024,128]{1,0:T(8,128)(2,1)S(1)}, bf16[1024,128]{1,0:T(8,128)(2,1)S(1)}, bf16[1024,128]{1,0:T(8,12...) custom-call(s32[16]{0:T(128)S(1)} %fusion.ord_ref, ...), custom_call_target="tpu_custom_call" | custom-call | tf_op jit(solution)/shard_map/pallas_call | solution.py:155
  37.4 1.5 %collective-permute-done.oth_ref = bf16[16,464,128]{2,1,0:T(8,128)(2,1)S(1)} collective-permute-done((bf16[16,464,128]{2,1,0:T(8,128)(2,1)S(1)}, bf16[16,464,128]{2,1,0:T(8,128)(2,1)S(1)}, u32[]{:S(2)}, u32[]{:S(2)}) %collective-permute-start) | collective-permute-done | bytes 1900576 | tf_op jit(solution)/shard_map/ppermute | solution.py:379
  38.9 6.0 %shard_map.104 = (bf16[16,128,128]{2,1,0:T(8,128)(2,1)S(1)}, bf16[16,192,128]{2,1,0:T(8,128)(2,1)S(1)}, bf16[16,64,128]{2,1,0:T(8,128)(2,1)S(1)}, bf16[16,64,128]{2,1,0:T(8,128)(2,1)S(1)}) custom-call(s32[16]{0:T(128)S(1)} %fusion.ord_ref, bf16[16,464,128]{2,1,0:T(8,128)(2,1)S(1)} %collective-permute-done.oth_ref, bf16[512,1024]{1,0:T(8,128)(2,1)S(1)} %copy-done, ...), custom_call_target="tpu_custom_call" | custom-call | tf_op jit(solution)/shard_map/pallas_call | solution.py:249
  44.9 0.2 collective-permute-start.1
  45.1 2.1 %collective-permute-done.1.met_ref = bf16[16,192,128]{2,1,0:T(8,128)(2,1)S(1)} collective-permute-done((bf16[16,192,128]{2,1,0:T(8,128)(2,1)S(1)}, bf16[16,192,128]{2,1,0:T(8,128)(2,1)S(1)}, u32[]{:S(2)}, u32[]{:S(2)}) %collective-permute-start.1) | collective-permute-done | bytes 786464 | tf_op jit(solution)/shard_map/ppermute | solution.py:383
  47.2 0.6 shard_map.105
  47.8 20.6 %all_to_all.11.r_ref = bf16[16,288,128]{2,1,0:T(8,128)(2,1)S(1)} all-to-all(bf16[16,288,128]{2,1,0:T(8,128)(2,1)S(1)} %shard_map.105), channel_id=1, replica_groups={{0,16,32,48,64,80,96,112,128,144,160,176,192,208,224,240},{1,17,33,49,6..., dimensions={0} | all-to-all | bytes 2359296 | tf_op jit(solution)/shard_map/all_to_all | solution.py:370
  68.4 0.7 shard_map.107
  69.1 0.6 collective-permute-start.2
  69.7 2.4 %collective-permute-start.3 = (bf16[144,128]{1,0:T(8,128)(2,1)S(1)}, bf16[144,128]{1,0:T(8,128)(2,1)S(1)}, u32[]{:S(2)}, u32[]{:S(2)}) collective-permute-start(bf16[144,128]{1,0:T(8,128)(2,1)S(1)} %get-tuple-element.40), channel_id=1, source_target_pairs={{0,8},{1,9},{2,10},{3,11},{4,12},{5,13},{6,14},{7,15},{8,0},{9,1},... | collective-permute-start | bytes 110600 | tf_op jit(solution)/shard_map/ppermute | solution.py:373
  72.2 0.5 collective-permute-start.4
  72.7 0.5 collective-permute-done.2.b_ref
  73.2 2.0 %collective-permute-done.3.c_ref = bf16[144,128]{1,0:T(8,128)(2,1)S(1)} collective-permute-done((bf16[144,128]{1,0:T(8,128)(2,1)S(1)}, bf16[144,128]{1,0:T(8,128)(2,1)S(1)}, u32[]{:S(2)}, u32[]{:S(2)}) %collective-permute-start.3) | collective-permute-done | bytes 36896 | tf_op jit(solution)/shard_map/ppermute | solution.py:373
  75.2 0.9 collective-permute-done.4.d_ref
  76.2 5.5 %collective-permute-start.7 = (bf16[144,128]{1,0:T(8,128)(2,1)S(1)}, bf16[144,128]{1,0:T(8,128)(2,1)S(1)}, u32[]{:S(2)}, u32[]{:S(2)}) collective-permute-start(bf16[144,128]{1,0:T(8,128)(2,1)S(1)} %shard_map.108.a_ref), channel_id=1, source_target_pairs={{0,3},{1,2},{2,1},{3,0},{4,7},{5,6},{6,5},{7,4},{8,11},{9,10},{10,... | collective-permute-start | bytes 110600 | tf_op jit(solution)/shard_map/ppermute | solution.py:376
  81.6 1.4 %collective-permute-start.6 = (bf16[144,128]{1,0:T(8,128)(2,1)S(1)}, bf16[144,128]{1,0:T(8,128)(2,1)S(1)}, u32[]{:S(2)}, u32[]{:S(2)}) collective-permute-start(bf16[144,128]{1,0:T(8,128)(2,1)S(1)} %shard_map.108.a_ref), channel_id=1, source_target_pairs={{0,2},{1,3},{2,0},{3,1},{4,6},{5,7},{6,4},{7,5},{8,10},{9,11},{10,... | collective-permute-start | bytes 110600 | tf_op jit(solution)/shard_map/ppermute | solution.py:376
  83.1 1.0 %collective-permute-start.5 = (bf16[144,128]{1,0:T(8,128)(2,1)S(1)}, bf16[144,128]{1,0:T(8,128)(2,1)S(1)}, u32[]{:S(2)}, u32[]{:S(2)}) collective-permute-start(bf16[144,128]{1,0:T(8,128)(2,1)S(1)} %shard_map.108.a_ref), channel_id=1, source_target_pairs={{0,1},{1,0},{2,3},{3,2},{4,5},{5,4},{6,7},{7,6},{8,9},{9,8},{10,11... | collective-permute-start | bytes 110600 | tf_op jit(solution)/shard_map/ppermute | solution.py:376
  84.1 0.0 collective-permute-done.7.d_ref
  84.1 5.4 %collective-permute-done.6.c_ref = bf16[144,128]{1,0:T(8,128)(2,1)S(1)} collective-permute-done((bf16[144,128]{1,0:T(8,128)(2,1)S(1)}, bf16[144,128]{1,0:T(8,128)(2,1)S(1)}, u32[]{:S(2)}, u32[]{:S(2)}) %collective-permute-start.6) | collective-permute-done | bytes 36896 | tf_op jit(solution)/shard_map/ppermute | solution.py:376
  89.5 0.0 collective-permute-done.5.b_ref
  89.5 1.3 %collective-permute-start.10 = (bf16[144,128]{1,0:T(8,128)(2,1)S(1)}, bf16[144,128]{1,0:T(8,128)(2,1)S(1)}, u32[]{:S(2)}, u32[]{:S(2)}) collective-permute-start(bf16[144,128]{1,0:T(8,128)(2,1)S(1)} %shard_map.109.a_ref), channel_id=1, source_target_pairs={{0,12},{1,13},{2,14},{3,15},{4,8},{5,9},{6,10},{7,11},{8,4},{9,5},... | collective-permute-start | bytes 110600 | tf_op jit(solution)/shard_map/ppermute | solution.py:373
  90.9 3.8 %collective-permute-start.9 = (bf16[144,128]{1,0:T(8,128)(2,1)S(1)}, bf16[144,128]{1,0:T(8,128)(2,1)S(1)}, u32[]{:S(2)}, u32[]{:S(2)}) collective-permute-start(bf16[144,128]{1,0:T(8,128)(2,1)S(1)} %shard_map.109.a_ref), channel_id=1, source_target_pairs={{0,8},{1,9},{2,10},{3,11},{4,12},{5,13},{6,14},{7,15},{8,0},{9,1},... | collective-permute-start | bytes 110600 | tf_op jit(solution)/shard_map/ppermute | solution.py:373
  94.7 0.0 collective-permute-start.8
  94.7 0.9 shard_map.106
  95.6 0.0 collective-permute-done.10.d_ref
  95.7 1.0 %collective-permute-done.9.c_ref = bf16[144,128]{1,0:T(8,128)(2,1)S(1)} collective-permute-done((bf16[144,128]{1,0:T(8,128)(2,1)S(1)}, bf16[144,128]{1,0:T(8,128)(2,1)S(1)}, u32[]{:S(2)}, u32[]{:S(2)}) %collective-permute-start.9) | collective-permute-done | bytes 36896 | tf_op jit(solution)/shard_map/ppermute | solution.py:373
  96.7 2.0 %collective-permute-done.8.b_ref = bf16[144,128]{1,0:T(8,128)(2,1)S(1)} collective-permute-done((bf16[144,128]{1,0:T(8,128)(2,1)S(1)}, bf16[144,128]{1,0:T(8,128)(2,1)S(1)}, u32[]{:S(2)}, u32[]{:S(2)}) %collective-permute-start.8) | collective-permute-done | bytes 36896 | tf_op jit(solution)/shard_map/ppermute | solution.py:373
  98.7 0.7 shard_map.110
  (2 shorter events, 0.0 us)
Async XLA Ops:
  3.3 32.1 %copy-start = (bf16[512,1024]{1,0:T(8,128)(2,1)S(1)}, bf16[512,1024]{1,0:T(8,128)(2,1)}, u32[]{:S(2)}) copy-start(bf16[512,1024]{1,0:T(8,128)(2,1)} %uk_ref.5) | copy-start | bytes 3145732
  3.3 32.1 %copy-start.1 = (bf16[512,1024]{1,0:T(8,128)(2,1)S(1)}, bf16[512,1024]{1,0:T(8,128)(2,1)}, u32[]{:S(2)}) copy-start(bf16[512,1024]{1,0:T(8,128)(2,1)} %uv_ref.5) | copy-start | bytes 3145732
  35.0 3.9 %collective-permute-start = (bf16[16,464,128]{2,1,0:T(8,128)(2,1)S(1)}, bf16[16,464,128]{2,1,0:T(8,128)(2,1)S(1)}, u32[]{:S(2)}, u32[]{:S(2)}) collective-permute-start(bf16[16,464,128]{2,1,0:T(8,128)(2,1)S(1)} %all_to_all.10.own_ref), channel_id=1, source_target_pairs={{0,16},{16,0},{32,48},{48,32},{64,80},{80,64},{96,112},{112,96},{1... | collective-permute-start | bytes 5701640 | tf_op jit(solution)/shard_map/ppermute | solution.py:379
  44.9 2.4 %collective-permute-start.1 = (bf16[16,192,128]{2,1,0:T(8,128)(2,1)S(1)}, bf16[16,192,128]{2,1,0:T(8,128)(2,1)S(1)}, u32[]{:S(2)}, u32[]{:S(2)}) collective-permute-start(bf16[16,192,128]{2,1,0:T(8,128)(2,1)S(1)} %get-tuple-element.34), channel_id=1, source_target_pairs={{0,16},{16,0},{32,48},{48,32},{64,80},{80,64},{96,112},{112,96},{1... | collective-permute-start | bytes 2359304 | tf_op jit(solution)/shard_map/ppermute | solution.py:383
  69.1 4.0 %collective-permute-start.2 = (bf16[144,128]{1,0:T(8,128)(2,1)S(1)}, bf16[144,128]{1,0:T(8,128)(2,1)S(1)}, u32[]{:S(2)}, u32[]{:S(2)}) collective-permute-start(bf16[144,128]{1,0:T(8,128)(2,1)S(1)} %get-tuple-element.39), channel_id=1, source_target_pairs={{0,4},{1,5},{2,6},{3,7},{4,0},{5,1},{6,2},{7,3},{8,12},{9,13},{10,... | collective-permute-start | bytes 110600 | tf_op jit(solution)/shard_map/ppermute | solution.py:373
  69.7 5.5 %collective-permute-start.3 = (bf16[144,128]{1,0:T(8,128)(2,1)S(1)}, bf16[144,128]{1,0:T(8,128)(2,1)S(1)}, u32[]{:S(2)}, u32[]{:S(2)}) collective-permute-start(bf16[144,128]{1,0:T(8,128)(2,1)S(1)} %get-tuple-element.40), channel_id=1, source_target_pairs={{0,8},{1,9},{2,10},{3,11},{4,12},{5,13},{6,14},{7,15},{8,0},{9,1},... | collective-permute-start | bytes 110600 | tf_op jit(solution)/shard_map/ppermute | solution.py:373
  72.2 4.0 %collective-permute-start.4 = (bf16[144,128]{1,0:T(8,128)(2,1)S(1)}, bf16[144,128]{1,0:T(8,128)(2,1)S(1)}, u32[]{:S(2)}, u32[]{:S(2)}) collective-permute-start(bf16[144,128]{1,0:T(8,128)(2,1)S(1)} %get-tuple-element.41), channel_id=1, source_target_pairs={{0,12},{1,13},{2,14},{3,15},{4,8},{5,9},{6,10},{7,11},{8,4},{9,5},... | collective-permute-start | bytes 110600 | tf_op jit(solution)/shard_map/ppermute | solution.py:373
  76.2 7.9 %collective-permute-start.7 = (bf16[144,128]{1,0:T(8,128)(2,1)S(1)}, bf16[144,128]{1,0:T(8,128)(2,1)S(1)}, u32[]{:S(2)}, u32[]{:S(2)}) collective-permute-start(bf16[144,128]{1,0:T(8,128)(2,1)S(1)} %shard_map.108.a_ref), channel_id=1, source_target_pairs={{0,3},{1,2},{2,1},{3,0},{4,7},{5,6},{6,5},{7,4},{8,11},{9,10},{10,... | collective-permute-start | bytes 110600 | tf_op jit(solution)/shard_map/ppermute | solution.py:376
  81.6 7.9 %collective-permute-start.6 = (bf16[144,128]{1,0:T(8,128)(2,1)S(1)}, bf16[144,128]{1,0:T(8,128)(2,1)S(1)}, u32[]{:S(2)}, u32[]{:S(2)}) collective-permute-start(bf16[144,128]{1,0:T(8,128)(2,1)S(1)} %shard_map.108.a_ref), channel_id=1, source_target_pairs={{0,2},{1,3},{2,0},{3,1},{4,6},{5,7},{6,4},{7,5},{8,10},{9,11},{10,... | collective-permute-start | bytes 110600 | tf_op jit(solution)/shard_map/ppermute | solution.py:376
  83.1 6.4 %collective-permute-start.5 = (bf16[144,128]{1,0:T(8,128)(2,1)S(1)}, bf16[144,128]{1,0:T(8,128)(2,1)S(1)}, u32[]{:S(2)}, u32[]{:S(2)}) collective-permute-start(bf16[144,128]{1,0:T(8,128)(2,1)S(1)} %shard_map.108.a_ref), channel_id=1, source_target_pairs={{0,1},{1,0},{2,3},{3,2},{4,5},{5,4},{6,7},{7,6},{8,9},{9,8},{10,11... | collective-permute-start | bytes 110600 | tf_op jit(solution)/shard_map/ppermute | solution.py:376
  89.5 6.1 %collective-permute-start.10 = (bf16[144,128]{1,0:T(8,128)(2,1)S(1)}, bf16[144,128]{1,0:T(8,128)(2,1)S(1)}, u32[]{:S(2)}, u32[]{:S(2)}) collective-permute-start(bf16[144,128]{1,0:T(8,128)(2,1)S(1)} %shard_map.109.a_ref), channel_id=1, source_target_pairs={{0,12},{1,13},{2,14},{3,15},{4,8},{5,9},{6,10},{7,11},{8,4},{9,5},... | collective-permute-start | bytes 110600 | tf_op jit(solution)/shard_map/ppermute | solution.py:373
  90.9 5.8 %collective-permute-start.9 = (bf16[144,128]{1,0:T(8,128)(2,1)S(1)}, bf16[144,128]{1,0:T(8,128)(2,1)S(1)}, u32[]{:S(2)}, u32[]{:S(2)}) collective-permute-start(bf16[144,128]{1,0:T(8,128)(2,1)S(1)} %shard_map.109.a_ref), channel_id=1, source_target_pairs={{0,8},{1,9},{2,10},{3,11},{4,12},{5,13},{6,14},{7,15},{8,0},{9,1},... | collective-permute-start | bytes 110600 | tf_op jit(solution)/shard_map/ppermute | solution.py:373
  94.7 4.0 %collective-permute-start.8 = (bf16[144,128]{1,0:T(8,128)(2,1)S(1)}, bf16[144,128]{1,0:T(8,128)(2,1)S(1)}, u32[]{:S(2)}, u32[]{:S(2)}) collective-permute-start(bf16[144,128]{1,0:T(8,128)(2,1)S(1)} %shard_map.109.a_ref), channel_id=1, source_target_pairs={{0,4},{1,5},{2,6},{3,7},{4,0},{5,1},{6,2},{7,3},{8,12},{9,13},{10,... | collective-permute-start | bytes 110600 | tf_op jit(solution)/shard_map/ppermute | solution.py:373

commit v5 on v4

--- a/solution.py
+++ b/solution.py
@@ -118,8 +118,8 @@
     return copies
 
 
-def own_kernel(ord_ref, own_ref, uk_ref, uv_ref, qs, cs, keys, values, ropes, turned, s_out, g_out, top_out,
-               weights, source, sems):
+def own_kernel(ord_ref, own_ref, uk_ref, uv_ref, qs, cs, keys, values, ropes, turned, s_out, g_out, top_out, total_out,
+               mixed_out, weights, source, sems):
     copies = fetch_weights(uk_ref, uv_ref, weights, sems)
     for s in range(16):
         source[ord_ref[s]] = s
@@ -145,7 +145,18 @@
             s_out[to, :] = sc
             g_out[to, :] = dot_nt(values[at, :], cs[rows, :])
             top = jnp.maximum(top, jnp.max(sc.reshape(32, 8, 256), axis=0))
-        top_out[p, :, :] = top
+        top = jnp.max(top, axis=0, keepdims=True)
+        total = jnp.zeros((8, 256), F32)
+        mixed = jnp.zeros((8, 256), F32)
+        for c in range(p + 1):
+            of = slice(first + c * 256, first + c * 256 + 256)
+            e = jnp.exp2(s_out[of, :] - top)
+            s_out[of, :] = e
+            total = total + jnp.sum(e.reshape(32, 8, 256), axis=0)
+            mixed = mixed + jnp.sum((e * g_out[of, :]).reshape(32, 8, 256), axis=0)
+        top_out[p, :, :] = jnp.broadcast_to(top, (8, 256))
+        total_out[p, :, :] = total
+        mixed_out[p, :, :] = mixed
 
 
 def own_side(orders, own, w_uk, w_uv):
@@ -155,16 +166,16 @@
     return pl.pallas_call(
         own_kernel,
         in_specs=[pl.BlockSpec(memory_space=pltpu.SMEM), whole, anywhere, anywhere],
-        out_specs=[whole] * 9,
+        out_specs=[whole] * 11,
         out_shape=[jax.ShapeDtypeStruct(shape, BF) for shape in shapes]
-        + [jax.ShapeDtypeStruct(shape, F32) for shape in ((2560, 256), (2560, 256), (4, 8, 256))],
+        + [jax.ShapeDtypeStruct(shape, F32) for shape in ((2560, 256), (2560, 256)) + ((4, 8, 256),) * 3],
         scratch_shapes=[pltpu.VMEM((DL, 256), BF), pltpu.SMEM((16,), jnp.int32), pltpu.SemaphoreType.DMA((2,))],
         compiler_params=pltpu.CompilerParams(vmem_limit_bytes=12 << 20),
     )(orders, own, w_uk, w_uv)
 
 
-def attend_kernel(ord_ref, oth_ref, uk_ref, uv_ref, qs, cs, own_keys, own_values, own_ropes, own_turned, s_own, g_own,
-                  top_own, keep_out, give_out, dq_out, rope_out,
+def attend_kernel(ord_ref, oth_ref, uk_ref, uv_ref, qs, cs, own_keys, own_values, own_ropes, own_turned, e_own, g_own,
+                  top_own, total_own, mixed_own, keep_out, give_out, dq_out, rope_out,
                   weights, keys, values, ropes, turned, s_sc, g_sc, ds_sc, p_sc, kvg, dr, dqs, source, sems):
     scale = (DN + DR) ** -0.5
     core = lax.rem(lax.axis_index("ctx"), 2)
@@ -184,7 +195,7 @@
         sc = dot_nt(jnp.concatenate([keys[at, :], ropes[at, :]], axis=1), qs[spans[p], :]) * FACTOR
         if c == p:
             sc = jnp.where(visible, sc, MASKED)
-        s_sc[p % 2, 1, at, :] = sc
+        s_sc[p % 2, at, :] = sc
         g_sc[p % 2, at, :] = dot_nt(values[at, :], cs[spans[p], :])
         return jnp.max(sc.reshape(32, 8, 256), axis=0)
 
@@ -194,26 +205,26 @@
         top = functools.reduce(jnp.maximum, tops, top_own[p])
         tops = []
         top = jnp.max(top, axis=0, keepdims=True)
-        total = jnp.zeros((8, 256), F32)
-        mixed = jnp.zeros((8, 256), F32)
+        shrink = jnp.exp2(top_own[p] - top)
+        total = total_own[p] * shrink
+        mixed = mixed_own[p] * shrink
         for c in range(p + 1):
-            at, of = spans[c], slice(first + c * 256, first + c * 256 + 256)
-            for side in range(2):
-                e = jnp.exp2((s_sc[p % 2, 1, at, :] if side else s_own[of, :]) - top)
-                g = g_sc[p % 2, at, :] if side else g_own[of, :]
-                s_sc[p % 2, side, at, :] = e
-                total = total + jnp.sum(e.reshape(32, 8, 256), axis=0)
-                mixed = mixed + jnp.sum((e * g).reshape(32, 8, 256), axis=0)
+            at = spans[c]
+            e = jnp.exp2(s_sc[p % 2, at, :] - top)
+            s_sc[p % 2, at, :] = e
+            total = total + jnp.sum(e.reshape(32, 8, 256), axis=0)
+            mixed = mixed + jnp.sum((e * g_sc[p % 2, at, :]).reshape(32, 8, 256), axis=0)
             if p < 3:
                 tops.append(score(p + 1, c))
         share = 1.0 / jnp.sum(total, axis=0, keepdims=True)
         delta = jnp.sum(mixed, axis=0, keepdims=True) * share
+        own_share = shrink[0:1] * share
         if p < 3:
             tops.append(score(p + 1, p + 1))
         for c in range(p + 1):
             at, of = spans[c], slice(first + c * 256, first + c * 256 + 256)
             for side in range(2):
-                prob = s_sc[p % 2, side, at, :] * share
+                prob = s_sc[p % 2, at, :] * share if side else e_own[of, :] * own_share
                 g = g_sc[p % 2, at, :] if side else g_own[of, :]
                 ds_sc[side, at, rows] = (prob * (g - delta)).astype(BF)
                 p_sc[side, at, rows] = prob.astype(BF)
@@ -248,7 +259,7 @@
     anywhere = pl.BlockSpec(memory_space=pl.ANY)
     return pl.pallas_call(
         attend_kernel,
-        in_specs=[pl.BlockSpec(memory_space=pltpu.SMEM), whole, anywhere, anywhere] + [whole] * 9,
+        in_specs=[pl.BlockSpec(memory_space=pltpu.SMEM), whole, anywhere, anywhere] + [whole] * 11,
         out_specs=[whole, whole, whole, whole],
         out_shape=[
             jax.ShapeDtypeStruct((16, TOK, 128), BF),
@@ -262,7 +273,7 @@
             pltpu.VMEM((1024, 128), BF),
             pltpu.VMEM((1024, 128), BF),
             pltpu.VMEM((256, 1024), BF),
-            pltpu.VMEM((2, 2, 1024, 256), F32),
+            pltpu.VMEM((2, 1024, 256), F32),
             pltpu.VMEM((2, 1024, 256), F32),
             pltpu.VMEM((2, 1024, 1024), BF),
             pltpu.VMEM((2, 1024, 1024), BF),

time: 99.6 us -> 99 us (level)
  no operation moved by 1% of the time
where the time goes in v5:
time: 99 us; the launch traced here: 98.8 us
  blocking collectives  52.3 us (53%)
  starting transfers between devices  16.9 us (17%)
  waiting for transfers between devices  15 us (15%)
  Pallas kernels  13.5 us (14%)
    all_to_all x2, blocking collectives, exchange(): return lax.all_to_all(x, 'ctx', 0, 0, tiled=True, axis_index_groups=every)  52.3 us
    ppermute x6, starting transfers between devices, along_x(): return lax.ppermute(x, 'head', [(i, i ^ 4 * k) for i in range(16)])  8.75 us
    ppermute x3, starting transfers between devices, along_z(): return lax.ppermute(x, 'head', [(i, i ^ k) for i in range(16)])  7.95 us
    ppermute x6, waiting for transfers between devices, along_x(): return lax.ppermute(x, 'head', [(i, i ^ 4 * k) for i in range(16)])  6.45 us
    ppermute x3, waiting for transfers between devices, along_z(): return lax.ppermute(x, 'head', [(i, i ^ k) for i in range(16)])  5.41 us
    pallas_call x1, Pallas kernels, attend(): pl.pallas_call(attend_kernel, in_specs=[pl.BlockSpec(memory_space=pltpu.S...  5.38 us
    pallas_call x1, Pallas kernels, pack(): pl.pallas_call(pack_kernel, in_specs=[pl.BlockSpec(memory_space=pl.ANY)]...  2.66 us
    pallas_call x1, Pallas kernels, own_side(): pl.pallas_call(own_kernel, in_specs=[pl.BlockSpec(memory_space=pltpu.SMEM...  2.48 us
  transfers between devices with their start and end apart: 11, of which 8 were waited for; matrix products, arithmetic and copies ran while one was open for 0% of the time, Pallas kernels for 3%

profile of v5, /device:TPU:2, one launch (start us, length us, event | category | flops | bytes accessed | tf_op | source)
XLA Modules:
  0.0 98.8 jit_solution(16878883328270032422)
XLA Ops:
  0.6 2.7 %shard_map.102 = bf16[16,464,128]{2,1,0:T(8,128)(2,1)} custom-call(bf16[128,1536]{1,0:T(8,128)(2,1)} %q_hbm.1, bf16[576,128]{1,0:T(8,128)(2,1)} %bitcast.5, bf16[128,1024]{1,0:T(8,128)(2,1)} %g_hbm.1, s32[1,128]{1,0:T(1,128)} %bitcast.6, s32[1,128]{1,0:T(1,128)} %bitcast.7), custom_call_target="tpu_custom_call" | custom-call | tf_op jit(solution)/shard_map/pallas_call | solution.py:73
  3.3 0.0 copy-start
  3.3 0.0 copy-start.1
  3.3 31.7 %all_to_all.10.own_ref = bf16[16,464,128]{2,1,0:T(8,128)(2,1)S(1)} all-to-all(bf16[16,464,128]{2,1,0:T(8,128)(2,1)} %shard_map.102), channel_id=1, replica_groups={{0,16,32,48,64,80,96,112,128,144,160,176,192,208,224,240},{1,17,33,49,6..., dimensions={0} | all-to-all | bytes 3801088 | tf_op jit(solution)/shard_map/all_to_all | solution.py:381
  35.0 0.0 collective-permute-start
  35.0 0.4 fusion.ord_ref
  35.4 0.0 copy-done
  35.4 0.0 copy-done.1
  35.4 2.5 %shard_map.103 = (bf16[1024,256]{1,0:T(8,128)(2,1)S(1)}, bf16[1024,128]{1,0:T(8,128)(2,1)S(1)}, bf16[1024,128]{1,0:T(8,128)(2,1)S(1)}, bf16[1024,128]{1,0:T(8,12...) custom-call(s32[16]{0:T(128)S(1)} %fusion.ord_ref, ...), custom_call_target="tpu_custom_call" | custom-call | tf_op jit(solution)/shard_map/pallas_call | solution.py:166
  37.9 1.0 %collective-permute-done.oth_ref = bf16[16,464,128]{2,1,0:T(8,128)(2,1)S(1)} collective-permute-done((bf16[16,464,128]{2,1,0:T(8,128)(2,1)S(1)}, bf16[16,464,128]{2,1,0:T(8,128)(2,1)S(1)}, u32[]{:S(2)}, u32[]{:S(2)}) %collective-permute-start) | collective-permute-done | bytes 1900576 | tf_op jit(solution)/shard_map/ppermute | solution.py:390
  38.9 5.4 %shard_map.104 = (bf16[16,128,128]{2,1,0:T(8,128)(2,1)S(1)}, bf16[16,192,128]{2,1,0:T(8,128)(2,1)S(1)}, bf16[16,64,128]{2,1,0:T(8,128)(2,1)S(1)}, bf16[16,64,128]{2,1,0:T(8,128)(2,1)S(1)}) custom-call(s32[16]{0:T(128)S(1)} %fusion.ord_ref, bf16[16,464,128]{2,1,0:T(8,128)(2,1)S(1)} %collective-permute-done.oth_ref, bf16[512,1024]{1,0:T(8,128)(2,1)S(1)} %copy-done, ...), custom_call_target="tpu_custom_call" | custom-call | tf_op jit(solution)/shard_map/pallas_call | solution.py:260
  44.3 0.2 collective-permute-start.1
  44.5 2.2 %collective-permute-done.1.met_ref = bf16[16,192,128]{2,1,0:T(8,128)(2,1)S(1)} collective-permute-done((bf16[16,192,128]{2,1,0:T(8,128)(2,1)S(1)}, bf16[16,192,128]{2,1,0:T(8,128)(2,1)S(1)}, u32[]{:S(2)}, u32[]{:S(2)}) %collective-permute-start.1) | collective-permute-done | bytes 786464 | tf_op jit(solution)/shard_map/ppermute | solution.py:394
  46.6 0.6 shard_map.105
  47.3 20.6 %all_to_all.11.r_ref = bf16[16,288,128]{2,1,0:T(8,128)(2,1)S(1)} all-to-all(bf16[16,288,128]{2,1,0:T(8,128)(2,1)S(1)} %shard_map.105), channel_id=1, replica_groups={{0,16,32,48,64,80,96,112,128,144,160,176,192,208,224,240},{1,17,33,49,6..., dimensions={0} | all-to-all | bytes 2359296 | tf_op jit(solution)/shard_map/all_to_all | solution.py:381
  67.8 0.7 shard_map.107
  68.5 0.6 collective-permute-start.2
  69.2 2.4 %collective-permute-start.3 = (bf16[144,128]{1,0:T(8,128)(2,1)S(1)}, bf16[144,128]{1,0:T(8,128)(2,1)S(1)}, u32[]{:S(2)}, u32[]{:S(2)}) collective-permute-start(bf16[144,128]{1,0:T(8,128)(2,1)S(1)} %get-tuple-element.44), channel_id=1, source_target_pairs={{0,8},{1,9},{2,10},{3,11},{4,12},{5,13},{6,14},{7,15},{8,0},{9,1},... | collective-permute-start | bytes 110600 | tf_op jit(solution)/shard_map/ppermute | solution.py:384
  71.6 0.5 collective-permute-start.4
  72.1 0.5 collective-permute-done.2.b_ref
  72.6 2.0 %collective-permute-done.3.c_ref = bf16[144,128]{1,0:T(8,128)(2,1)S(1)} collective-permute-done((bf16[144,128]{1,0:T(8,128)(2,1)S(1)}, bf16[144,128]{1,0:T(8,128)(2,1)S(1)}, u32[]{:S(2)}, u32[]{:S(2)}) %collective-permute-start.3) | collective-permute-done | bytes 36896 | tf_op jit(solution)/shard_map/ppermute | solution.py:384
  74.6 0.9 collective-permute-done.4.d_ref
  75.6 5.5 %collective-permute-start.7 = (bf16[144,128]{1,0:T(8,128)(2,1)S(1)}, bf16[144,128]{1,0:T(8,128)(2,1)S(1)}, u32[]{:S(2)}, u32[]{:S(2)}) collective-permute-start(bf16[144,128]{1,0:T(8,128)(2,1)S(1)} %shard_map.108.a_ref), channel_id=1, source_target_pairs={{0,3},{1,2},{2,1},{3,0},{4,7},{5,6},{6,5},{7,4},{8,11},{9,10},{10,... | collective-permute-start | bytes 110600 | tf_op jit(solution)/shard_map/ppermute | solution.py:387
  81.1 1.4 %collective-permute-start.6 = (bf16[144,128]{1,0:T(8,128)(2,1)S(1)}, bf16[144,128]{1,0:T(8,128)(2,1)S(1)}, u32[]{:S(2)}, u32[]{:S(2)}) collective-permute-start(bf16[144,128]{1,0:T(8,128)(2,1)S(1)} %shard_map.108.a_ref), channel_id=1, source_target_pairs={{0,2},{1,3},{2,0},{3,1},{4,6},{5,7},{6,4},{7,5},{8,10},{9,11},{10,... | collective-permute-start | bytes 110600 | tf_op jit(solution)/shard_map/ppermute | solution.py:387
  82.5 1.0 %collective-permute-start.5 = (bf16[144,128]{1,0:T(8,128)(2,1)S(1)}, bf16[144,128]{1,0:T(8,128)(2,1)S(1)}, u32[]{:S(2)}, u32[]{:S(2)}) collective-permute-start(bf16[144,128]{1,0:T(8,128)(2,1)S(1)} %shard_map.108.a_ref), channel_id=1, source_target_pairs={{0,1},{1,0},{2,3},{3,2},{4,5},{5,4},{6,7},{7,6},{8,9},{9,8},{10,11... | collective-permute-start | bytes 110600 | tf_op jit(solution)/shard_map/ppermute | solution.py:387
  83.5 0.0 collective-permute-done.7.d_ref
  83.5 5.4 %collective-permute-done.6.c_ref = bf16[144,128]{1,0:T(8,128)(2,1)S(1)} collective-permute-done((bf16[144,128]{1,0:T(8,128)(2,1)S(1)}, bf16[144,128]{1,0:T(8,128)(2,1)S(1)}, u32[]{:S(2)}, u32[]{:S(2)}) %collective-permute-start.6) | collective-permute-done | bytes 36896 | tf_op jit(solution)/shard_map/ppermute | solution.py:387
  88.9 0.0 collective-permute-done.5.b_ref
  89.0 1.3 %collective-permute-start.10 = (bf16[144,128]{1,0:T(8,128)(2,1)S(1)}, bf16[144,128]{1,0:T(8,128)(2,1)S(1)}, u32[]{:S(2)}, u32[]{:S(2)}) collective-permute-start(bf16[144,128]{1,0:T(8,128)(2,1)S(1)} %shard_map.109.a_ref), channel_id=1, source_target_pairs={{0,12},{1,13},{2,14},{3,15},{4,8},{5,9},{6,10},{7,11},{8,4},{9,5},... | collective-permute-start | bytes 110600 | tf_op jit(solution)/shard_map/ppermute | solution.py:384
  90.3 3.8 %collective-permute-start.9 = (bf16[144,128]{1,0:T(8,128)(2,1)S(1)}, bf16[144,128]{1,0:T(8,128)(2,1)S(1)}, u32[]{:S(2)}, u32[]{:S(2)}) collective-permute-start(bf16[144,128]{1,0:T(8,128)(2,1)S(1)} %shard_map.109.a_ref), channel_id=1, source_target_pairs={{0,8},{1,9},{2,10},{3,11},{4,12},{5,13},{6,14},{7,15},{8,0},{9,1},... | collective-permute-start | bytes 110600 | tf_op jit(solution)/shard_map/ppermute | solution.py:384
  94.1 0.0 collective-permute-start.8
  94.1 0.9 shard_map.106
  95.0 0.0 collective-permute-done.10.d_ref
  95.1 1.0 %collective-permute-done.9.c_ref = bf16[144,128]{1,0:T(8,128)(2,1)S(1)} collective-permute-done((bf16[144,128]{1,0:T(8,128)(2,1)S(1)}, bf16[144,128]{1,0:T(8,128)(2,1)S(1)}, u32[]{:S(2)}, u32[]{:S(2)}) %collective-permute-start.9) | collective-permute-done | bytes 36896 | tf_op jit(solution)/shard_map/ppermute | solution.py:384
  96.1 2.0 %collective-permute-done.8.b_ref = bf16[144,128]{1,0:T(8,128)(2,1)S(1)} collective-permute-done((bf16[144,128]{1,0:T(8,128)(2,1)S(1)}, bf16[144,128]{1,0:T(8,128)(2,1)S(1)}, u32[]{:S(2)}, u32[]{:S(2)}) %collective-permute-start.8) | collective-permute-done | bytes 36896 | tf_op jit(solution)/shard_map/ppermute | solution.py:384
  98.1 0.7 shard_map.110
  (2 shorter events, 0.0 us)
Async XLA Ops:
  3.3 32.1 %copy-start = (bf16[512,1024]{1,0:T(8,128)(2,1)S(1)}, bf16[512,1024]{1,0:T(8,128)(2,1)}, u32[]{:S(2)}) copy-start(bf16[512,1024]{1,0:T(8,128)(2,1)} %uk_ref.5) | copy-start | bytes 3145732
  3.3 32.1 %copy-start.1 = (bf16[512,1024]{1,0:T(8,128)(2,1)S(1)}, bf16[512,1024]{1,0:T(8,128)(2,1)}, u32[]{:S(2)}) copy-start(bf16[512,1024]{1,0:T(8,128)(2,1)} %uv_ref.5) | copy-start | bytes 3145732
  35.0 3.9 %collective-permute-start = (bf16[16,464,128]{2,1,0:T(8,128)(2,1)S(1)}, bf16[16,464,128]{2,1,0:T(8,128)(2,1)S(1)}, u32[]{:S(2)}, u32[]{:S(2)}) collective-permute-start(bf16[16,464,128]{2,1,0:T(8,128)(2,1)S(1)} %all_to_all.10.own_ref), channel_id=1, source_target_pairs={{0,16},{16,0},{32,48},{48,32},{64,80},{80,64},{96,112},{112,96},{1... | collective-permute-start | bytes 5701640 | tf_op jit(solution)/shard_map/ppermute | solution.py:390
  44.3 2.4 %collective-permute-start.1 = (bf16[16,192,128]{2,1,0:T(8,128)(2,1)S(1)}, bf16[16,192,128]{2,1,0:T(8,128)(2,1)S(1)}, u32[]{:S(2)}, u32[]{:S(2)}) collective-permute-start(bf16[16,192,128]{2,1,0:T(8,128)(2,1)S(1)} %get-tuple-element.38), channel_id=1, source_target_pairs={{0,16},{16,0},{32,48},{48,32},{64,80},{80,64},{96,112},{112,96},{1... | collective-permute-start | bytes 2359304 | tf_op jit(solution)/shard_map/ppermute | solution.py:394
  68.5 4.0 %collective-permute-start.2 = (bf16[144,128]{1,0:T(8,128)(2,1)S(1)}, bf16[144,128]{1,0:T(8,128)(2,1)S(1)}, u32[]{:S(2)}, u32[]{:S(2)}) collective-permute-start(bf16[144,128]{1,0:T(8,128)(2,1)S(1)} %get-tuple-element.43), channel_id=1, source_target_pairs={{0,4},{1,5},{2,6},{3,7},{4,0},{5,1},{6,2},{7,3},{8,12},{9,13},{10,... | collective-permute-start | bytes 110600 | tf_op jit(solution)/shard_map/ppermute | solution.py:384
  69.2 5.5 %collective-permute-start.3 = (bf16[144,128]{1,0:T(8,128)(2,1)S(1)}, bf16[144,128]{1,0:T(8,128)(2,1)S(1)}, u32[]{:S(2)}, u32[]{:S(2)}) collective-permute-start(bf16[144,128]{1,0:T(8,128)(2,1)S(1)} %get-tuple-element.44), channel_id=1, source_target_pairs={{0,8},{1,9},{2,10},{3,11},{4,12},{5,13},{6,14},{7,15},{8,0},{9,1},... | collective-permute-start | bytes 110600 | tf_op jit(solution)/shard_map/ppermute | solution.py:384
  71.6 4.0 %collective-permute-start.4 = (bf16[144,128]{1,0:T(8,128)(2,1)S(1)}, bf16[144,128]{1,0:T(8,128)(2,1)S(1)}, u32[]{:S(2)}, u32[]{:S(2)}) collective-permute-start(bf16[144,128]{1,0:T(8,128)(2,1)S(1)} %get-tuple-element.45), channel_id=1, source_target_pairs={{0,12},{1,13},{2,14},{3,15},{4,8},{5,9},{6,10},{7,11},{8,4},{9,5},... | collective-permute-start | bytes 110600 | tf_op jit(solution)/shard_map/ppermute | solution.py:384
  75.6 8.0 %collective-permute-start.7 = (bf16[144,128]{1,0:T(8,128)(2,1)S(1)}, bf16[144,128]{1,0:T(8,128)(2,1)S(1)}, u32[]{:S(2)}, u32[]{:S(2)}) collective-permute-start(bf16[144,128]{1,0:T(8,128)(2,1)S(1)} %shard_map.108.a_ref), channel_id=1, source_target_pairs={{0,3},{1,2},{2,1},{3,0},{4,7},{5,6},{6,5},{7,4},{8,11},{9,10},{10,... | collective-permute-start | bytes 110600 | tf_op jit(solution)/shard_map/ppermute | solution.py:387
  81.1 7.9 %collective-permute-start.6 = (bf16[144,128]{1,0:T(8,128)(2,1)S(1)}, bf16[144,128]{1,0:T(8,128)(2,1)S(1)}, u32[]{:S(2)}, u32[]{:S(2)}) collective-permute-start(bf16[144,128]{1,0:T(8,128)(2,1)S(1)} %shard_map.108.a_ref), channel_id=1, source_target_pairs={{0,2},{1,3},{2,0},{3,1},{4,6},{5,7},{6,4},{7,5},{8,10},{9,11},{10,... | collective-permute-start | bytes 110600 | tf_op jit(solution)/shard_map/ppermute | solution.py:387
  82.5 6.4 %collective-permute-start.5 = (bf16[144,128]{1,0:T(8,128)(2,1)S(1)}, bf16[144,128]{1,0:T(8,128)(2,1)S(1)}, u32[]{:S(2)}, u32[]{:S(2)}) collective-permute-start(bf16[144,128]{1,0:T(8,128)(2,1)S(1)} %shard_map.108.a_ref), channel_id=1, source_target_pairs={{0,1},{1,0},{2,3},{3,2},{4,5},{5,4},{6,7},{7,6},{8,9},{9,8},{10,11... | collective-permute-start | bytes 110600 | tf_op jit(solution)/shard_map/ppermute | solution.py:387
  89.0 6.1 %collective-permute-start.10 = (bf16[144,128]{1,0:T(8,128)(2,1)S(1)}, bf16[144,128]{1,0:T(8,128)(2,1)S(1)}, u32[]{:S(2)}, u32[]{:S(2)}) collective-permute-start(bf16[144,128]{1,0:T(8,128)(2,1)S(1)} %shard_map.109.a_ref), channel_id=1, source_target_pairs={{0,12},{1,13},{2,14},{3,15},{4,8},{5,9},{6,10},{7,11},{8,4},{9,5},... | collective-permute-start | bytes 110600 | tf_op jit(solution)/shard_map/ppermute | solution.py:384
  90.3 5.8 %collective-permute-start.9 = (bf16[144,128]{1,0:T(8,128)(2,1)S(1)}, bf16[144,128]{1,0:T(8,128)(2,1)S(1)}, u32[]{:S(2)}, u32[]{:S(2)}) collective-permute-start(bf16[144,128]{1,0:T(8,128)(2,1)S(1)} %shard_map.109.a_ref), channel_id=1, source_target_pairs={{0,8},{1,9},{2,10},{3,11},{4,12},{5,13},{6,14},{7,15},{8,0},{9,1},... | collective-permute-start | bytes 110600 | tf_op jit(solution)/shard_map/ppermute | solution.py:384
  94.1 4.0 %collective-permute-start.8 = (bf16[144,128]{1,0:T(8,128)(2,1)S(1)}, bf16[144,128]{1,0:T(8,128)(2,1)S(1)}, u32[]{:S(2)}, u32[]{:S(2)}) collective-permute-start(bf16[144,128]{1,0:T(8,128)(2,1)S(1)} %shard_map.109.a_ref), channel_id=1, source_target_pairs={{0,4},{1,5},{2,6},{3,7},{4,0},{5,1},{6,2},{7,3},{8,12},{9,13},{10,... | collective-permute-start | bytes 110600 | tf_op jit(solution)/shard_map/ppermute | solution.py:384

commit v6 on v5

--- a/solution.py
+++ b/solution.py
@@ -298,6 +298,10 @@
     )(*inputs)
 
 
+def share_kernel(own_ref, out_ref):
+    out_ref[...] = own_ref[:, 0:320, :]
+
+
 def finish_kernel(keep_ref, met_ref, rope_ref, dq_ref, own_ref, oth_ref, out_ref):
     total = jnp.zeros((128, DL), F32)
     for i in range(0, 16, 2):
@@ -387,7 +391,8 @@
         return lax.ppermute(x, "head", [(i, i ^ k) for i in range(16)])
 
     own = exchange(pack(queries, latent.T, grad_out, positions, tool_result))
-    other = lax.ppermute(own, "ctx", swap)
+    (shared,) = small(share_kernel, (own,), [((16, 320, 128), BF)])
+    other = lax.ppermute(shared, "ctx", swap)
     orders = own[:, 448, 0].astype(jnp.int32)
     mine = own_side(orders, own, w_uk, w_uv)
     keep, give, dq, rope = attend(orders, other, w_uk, w_uv, mine)

time: 99 us -> 99 us (level)
    ppermute x1, waiting for transfers between devices: 0.99 us -> 0.01 us  [local(): other = lax.ppermute(shared, 'ctx', swap)]
    pallas_call x5 -> x6, Pallas kernels: 2.31 us -> 2.37 us  [small(): pl.pallas_call(kernel, in_specs=[whole] * len(inputs), out_specs=[whole]...]
  transfers between devices with their start and end apart: 11 -> 11, of which waited for: 8 -> 7; matrix products, arithmetic and copies ran while one was open for 0% -> 0% of each run, Pallas kernels for 3% -> 3%
where the time goes in v6:
time: 99 us; the launch traced here: 98.8 us
  blocking collectives  52.1 us (53%)
  starting transfers between devices  16.9 us (17%)
  waiting for transfers between devices  14.1 us (14%)
  Pallas kernels  13.6 us (14%)
    all_to_all x2, blocking collectives, exchange(): return lax.all_to_all(x, 'ctx', 0, 0, tiled=True, axis_index_groups=every)  52.1 us
    ppermute x6, starting transfers between devices, along_x(): return lax.ppermute(x, 'head', [(i, i ^ 4 * k) for i in range(16)])  8.75 us
    ppermute x3, starting transfers between devices, along_z(): return lax.ppermute(x, 'head', [(i, i ^ k) for i in range(16)])  7.95 us
    ppermute x6, waiting for transfers between devices, along_x(): return lax.ppermute(x, 'head', [(i, i ^ 4 * k) for i in range(16)])  6.45 us
    ppermute x3, waiting for transfers between devices, along_z(): return lax.ppermute(x, 'head', [(i, i ^ k) for i in range(16)])  5.41 us
    pallas_call x1, Pallas kernels, attend(): pl.pallas_call(attend_kernel, in_specs=[pl.BlockSpec(memory_space=pltpu.S...  5.39 us
    pallas_call x1, Pallas kernels, pack(): pl.pallas_call(pack_kernel, in_specs=[pl.BlockSpec(memory_space=pl.ANY)]...  2.66 us
    pallas_call x1, Pallas kernels, own_side(): pl.pallas_call(own_kernel, in_specs=[pl.BlockSpec(memory_space=pltpu.SMEM...  2.47 us
  transfers between devices with their start and end apart: 11, of which 7 were waited for; matrix products, arithmetic and copies ran while one was open for 0% of the time, Pallas kernels for 3%

profile of v6, /device:TPU:2, one launch (start us, length us, event | category | flops | bytes accessed | tf_op | source)
XLA Modules:
  0.0 98.8 jit_solution(11657232570023384052)
XLA Ops:
  0.6 2.7 %shard_map.102 = bf16[16,464,128]{2,1,0:T(8,128)(2,1)} custom-call(bf16[128,1536]{1,0:T(8,128)(2,1)} %q_hbm.1, bf16[576,128]{1,0:T(8,128)(2,1)} %bitcast.5, bf16[128,1024]{1,0:T(8,128)(2,1)} %g_hbm.1, s32[1,128]{1,0:T(1,128)} %bitcast.6, s32[1,128]{1,0:T(1,128)} %bitcast.7), custom_call_target="tpu_custom_call" | custom-call | tf_op jit(solution)/shard_map/pallas_call | solution.py:73
  3.3 31.6 %all_to_all.10.own_ref = bf16[16,464,128]{2,1,0:T(8,128)(2,1)S(1)} all-to-all(bf16[16,464,128]{2,1,0:T(8,128)(2,1)} %shard_map.102), channel_id=1, replica_groups={{0,16,32,48,64,80,96,112,128,144,160,176,192,208,224,240},{1,17,33,49,6..., dimensions={0} | all-to-all | bytes 3801088 | tf_op jit(solution)/shard_map/all_to_all | solution.py:385
  34.8 0.0 copy-start
  34.9 0.0 copy-start.1
  34.9 0.1 shard_map.103
  34.9 0.1 collective-permute-start
  35.0 0.4 fusion.ord_ref
  35.4 0.7 copy-done
  36.1 0.3 copy-done.1
  36.4 2.5 %shard_map.104 = (bf16[1024,256]{1,0:T(8,128)(2,1)S(1)}, bf16[1024,128]{1,0:T(8,128)(2,1)S(1)}, bf16[1024,128]{1,0:T(8,128)(2,1)S(1)}, bf16[1024,128]{1,0:T(8,12...) custom-call(s32[16]{0:T(128)S(1)} %fusion.ord_ref, ...), custom_call_target="tpu_custom_call" | custom-call | tf_op jit(solution)/shard_map/pallas_call | solution.py:166
  38.9 0.0 collective-permute-done.oth_ref
  38.9 5.4 %shard_map.105 = (bf16[16,128,128]{2,1,0:T(8,128)(2,1)S(1)}, bf16[16,192,128]{2,1,0:T(8,128)(2,1)S(1)}, bf16[16,64,128]{2,1,0:T(8,128)(2,1)S(1)}, bf16[16,64,128]{2,1,0:T(8,128)(2,1)S(1)}) custom-call(s32[16]{0:T(128)S(1)} %fusion.ord_ref, bf16[16,320,128]{2,1,0:T(8,128)(2,1)S(1)} %collective-permute-done.oth_ref, bf16[512,1024]{1,0:T(8,128)(2,1)S(1)} %copy-done, ...), custom_call_target="tpu_custom_call" | custom-call | tf_op jit(solution)/shard_map/pallas_call | solution.py:260
  44.3 0.1 collective-permute-start.1
  44.4 2.3 %collective-permute-done.1.met_ref = bf16[16,192,128]{2,1,0:T(8,128)(2,1)S(1)} collective-permute-done((bf16[16,192,128]{2,1,0:T(8,128)(2,1)S(1)}, bf16[16,192,128]{2,1,0:T(8,128)(2,1)S(1)}, u32[]{:S(2)}, u32[]{:S(2)}) %collective-permute-start.1) | collective-permute-done | bytes 786464 | tf_op jit(solution)/shard_map/ppermute | solution.py:399
  46.7 0.6 shard_map.106
  47.2 20.6 %all_to_all.11.r_ref = bf16[16,288,128]{2,1,0:T(8,128)(2,1)S(1)} all-to-all(bf16[16,288,128]{2,1,0:T(8,128)(2,1)S(1)} %shard_map.106), channel_id=1, replica_groups={{0,16,32,48,64,80,96,112,128,144,160,176,192,208,224,240},{1,17,33,49,6..., dimensions={0} | all-to-all | bytes 2359296 | tf_op jit(solution)/shard_map/all_to_all | solution.py:385
  67.8 0.7 shard_map.108
  68.5 0.6 collective-permute-start.2
  69.2 2.4 %collective-permute-start.3 = (bf16[144,128]{1,0:T(8,128)(2,1)S(1)}, bf16[144,128]{1,0:T(8,128)(2,1)S(1)}, u32[]{:S(2)}, u32[]{:S(2)}) collective-permute-start(bf16[144,128]{1,0:T(8,128)(2,1)S(1)} %get-tuple-element.44), channel_id=1, source_target_pairs={{0,8},{1,9},{2,10},{3,11},{4,12},{5,13},{6,14},{7,15},{8,0},{9,1},... | collective-permute-start | bytes 110600 | tf_op jit(solution)/shard_map/ppermute | solution.py:388
  71.6 0.5 collective-permute-start.4
  72.1 0.5 collective-permute-done.2.b_ref
  72.6 2.0 %collective-permute-done.3.c_ref = bf16[144,128]{1,0:T(8,128)(2,1)S(1)} collective-permute-done((bf16[144,128]{1,0:T(8,128)(2,1)S(1)}, bf16[144,128]{1,0:T(8,128)(2,1)S(1)}, u32[]{:S(2)}, u32[]{:S(2)}) %collective-permute-start.3) | collective-permute-done | bytes 36896 | tf_op jit(solution)/shard_map/ppermute | solution.py:388
  74.6 0.9 collective-permute-done.4.d_ref
  75.6 5.5 %collective-permute-start.7 = (bf16[144,128]{1,0:T(8,128)(2,1)S(1)}, bf16[144,128]{1,0:T(8,128)(2,1)S(1)}, u32[]{:S(2)}, u32[]{:S(2)}) collective-permute-start(bf16[144,128]{1,0:T(8,128)(2,1)S(1)} %shard_map.109.a_ref), channel_id=1, source_target_pairs={{0,3},{1,2},{2,1},{3,0},{4,7},{5,6},{6,5},{7,4},{8,11},{9,10},{10,... | collective-permute-start | bytes 110600 | tf_op jit(solution)/shard_map/ppermute | solution.py:391
  81.0 1.4 %collective-permute-start.6 = (bf16[144,128]{1,0:T(8,128)(2,1)S(1)}, bf16[144,128]{1,0:T(8,128)(2,1)S(1)}, u32[]{:S(2)}, u32[]{:S(2)}) collective-permute-start(bf16[144,128]{1,0:T(8,128)(2,1)S(1)} %shard_map.109.a_ref), channel_id=1, source_target_pairs={{0,2},{1,3},{2,0},{3,1},{4,6},{5,7},{6,4},{7,5},{8,10},{9,11},{10,... | collective-permute-start | bytes 110600 | tf_op jit(solution)/shard_map/ppermute | solution.py:391
  82.5 1.0 %collective-permute-start.5 = (bf16[144,128]{1,0:T(8,128)(2,1)S(1)}, bf16[144,128]{1,0:T(8,128)(2,1)S(1)}, u32[]{:S(2)}, u32[]{:S(2)}) collective-permute-start(bf16[144,128]{1,0:T(8,128)(2,1)S(1)} %shard_map.109.a_ref), channel_id=1, source_target_pairs={{0,1},{1,0},{2,3},{3,2},{4,5},{5,4},{6,7},{7,6},{8,9},{9,8},{10,11... | collective-permute-start | bytes 110600 | tf_op jit(solution)/shard_map/ppermute | solution.py:391
  83.5 0.0 collective-permute-done.7.d_ref
  83.5 5.4 %collective-permute-done.6.c_ref = bf16[144,128]{1,0:T(8,128)(2,1)S(1)} collective-permute-done((bf16[144,128]{1,0:T(8,128)(2,1)S(1)}, bf16[144,128]{1,0:T(8,128)(2,1)S(1)}, u32[]{:S(2)}, u32[]{:S(2)}) %collective-permute-start.6) | collective-permute-done | bytes 36896 | tf_op jit(solution)/shard_map/ppermute | solution.py:391
  88.9 0.0 collective-permute-done.5.b_ref
  88.9 1.3 %collective-permute-start.10 = (bf16[144,128]{1,0:T(8,128)(2,1)S(1)}, bf16[144,128]{1,0:T(8,128)(2,1)S(1)}, u32[]{:S(2)}, u32[]{:S(2)}) collective-permute-start(bf16[144,128]{1,0:T(8,128)(2,1)S(1)} %shard_map.110.a_ref), channel_id=1, source_target_pairs={{0,12},{1,13},{2,14},{3,15},{4,8},{5,9},{6,10},{7,11},{8,4},{9,5},... | collective-permute-start | bytes 110600 | tf_op jit(solution)/shard_map/ppermute | solution.py:388
  90.3 3.8 %collective-permute-start.9 = (bf16[144,128]{1,0:T(8,128)(2,1)S(1)}, bf16[144,128]{1,0:T(8,128)(2,1)S(1)}, u32[]{:S(2)}, u32[]{:S(2)}) collective-permute-start(bf16[144,128]{1,0:T(8,128)(2,1)S(1)} %shard_map.110.a_ref), channel_id=1, source_target_pairs={{0,8},{1,9},{2,10},{3,11},{4,12},{5,13},{6,14},{7,15},{8,0},{9,1},... | collective-permute-start | bytes 110600 | tf_op jit(solution)/shard_map/ppermute | solution.py:388
  94.1 0.0 collective-permute-start.8
  94.1 0.9 shard_map.107
  95.0 0.0 collective-permute-done.10.d_ref
  95.0 1.0 %collective-permute-done.9.c_ref = bf16[144,128]{1,0:T(8,128)(2,1)S(1)} collective-permute-done((bf16[144,128]{1,0:T(8,128)(2,1)S(1)}, bf16[144,128]{1,0:T(8,128)(2,1)S(1)}, u32[]{:S(2)}, u32[]{:S(2)}) %collective-permute-start.9) | collective-permute-done | bytes 36896 | tf_op jit(solution)/shard_map/ppermute | solution.py:388
  96.0 2.0 %collective-permute-done.8.b_ref = bf16[144,128]{1,0:T(8,128)(2,1)S(1)} collective-permute-done((bf16[144,128]{1,0:T(8,128)(2,1)S(1)}, bf16[144,128]{1,0:T(8,128)(2,1)S(1)}, u32[]{:S(2)}, u32[]{:S(2)}) %collective-permute-start.8) | collective-permute-done | bytes 36896 | tf_op jit(solution)/shard_map/ppermute | solution.py:388
  98.1 0.7 shard_map.111
  (2 shorter events, 0.0 us)
Async XLA Ops:
  34.8 1.2 %copy-start = (bf16[512,1024]{1,0:T(8,128)(2,1)S(1)}, bf16[512,1024]{1,0:T(8,128)(2,1)}, u32[]{:S(2)}) copy-start(bf16[512,1024]{1,0:T(8,128)(2,1)} %uk_ref.5) | copy-start | bytes 3145732
  34.9 1.5 %copy-start.1 = (bf16[512,1024]{1,0:T(8,128)(2,1)S(1)}, bf16[512,1024]{1,0:T(8,128)(2,1)}, u32[]{:S(2)}) copy-start(bf16[512,1024]{1,0:T(8,128)(2,1)} %uv_ref.5) | copy-start | bytes 3145732
  34.9 3.9 %collective-permute-start = (bf16[16,320,128]{2,1,0:T(8,128)(2,1)S(1)}, bf16[16,320,128]{2,1,0:T(8,128)(2,1)S(1)}, u32[]{:S(2)}, u32[]{:S(2)}) collective-permute-start(bf16[16,320,128]{2,1,0:T(8,128)(2,1)S(1)} %shard_map.103), channel_id=1, source_target_pairs={{0,16},{16,0},{32,48},{48,32},{64,80},{80,64},{96,112},{112,96},{1... | collective-permute-start | bytes 3932168 | tf_op jit(solution)/shard_map/ppermute | solution.py:395
  44.3 2.4 %collective-permute-start.1 = (bf16[16,192,128]{2,1,0:T(8,128)(2,1)S(1)}, bf16[16,192,128]{2,1,0:T(8,128)(2,1)S(1)}, u32[]{:S(2)}, u32[]{:S(2)}) collective-permute-start(bf16[16,192,128]{2,1,0:T(8,128)(2,1)S(1)} %get-tuple-element.38), channel_id=1, source_target_pairs={{0,16},{16,0},{32,48},{48,32},{64,80},{80,64},{96,112},{112,96},{1... | collective-permute-start | bytes 2359304 | tf_op jit(solution)/shard_map/ppermute | solution.py:399
  68.5 4.0 %collective-permute-start.2 = (bf16[144,128]{1,0:T(8,128)(2,1)S(1)}, bf16[144,128]{1,0:T(8,128)(2,1)S(1)}, u32[]{:S(2)}, u32[]{:S(2)}) collective-permute-start(bf16[144,128]{1,0:T(8,128)(2,1)S(1)} %get-tuple-element.43), channel_id=1, source_target_pairs={{0,4},{1,5},{2,6},{3,7},{4,0},{5,1},{6,2},{7,3},{8,12},{9,13},{10,... | collective-permute-start | bytes 110600 | tf_op jit(solution)/shard_map/ppermute | solution.py:388
  69.2 5.5 %collective-permute-start.3 = (bf16[144,128]{1,0:T(8,128)(2,1)S(1)}, bf16[144,128]{1,0:T(8,128)(2,1)S(1)}, u32[]{:S(2)}, u32[]{:S(2)}) collective-permute-start(bf16[144,128]{1,0:T(8,128)(2,1)S(1)} %get-tuple-element.44), channel_id=1, source_target_pairs={{0,8},{1,9},{2,10},{3,11},{4,12},{5,13},{6,14},{7,15},{8,0},{9,1},... | collective-permute-start | bytes 110600 | tf_op jit(solution)/shard_map/ppermute | solution.py:388
  71.6 4.0 %collective-permute-start.4 = (bf16[144,128]{1,0:T(8,128)(2,1)S(1)}, bf16[144,128]{1,0:T(8,128)(2,1)S(1)}, u32[]{:S(2)}, u32[]{:S(2)}) collective-permute-start(bf16[144,128]{1,0:T(8,128)(2,1)S(1)} %get-tuple-element.45), channel_id=1, source_target_pairs={{0,12},{1,13},{2,14},{3,15},{4,8},{5,9},{6,10},{7,11},{8,4},{9,5},... | collective-permute-start | bytes 110600 | tf_op jit(solution)/shard_map/ppermute | solution.py:388
  75.6 8.0 %collective-permute-start.7 = (bf16[144,128]{1,0:T(8,128)(2,1)S(1)}, bf16[144,128]{1,0:T(8,128)(2,1)S(1)}, u32[]{:S(2)}, u32[]{:S(2)}) collective-permute-start(bf16[144,128]{1,0:T(8,128)(2,1)S(1)} %shard_map.109.a_ref), channel_id=1, source_target_pairs={{0,3},{1,2},{2,1},{3,0},{4,7},{5,6},{6,5},{7,4},{8,11},{9,10},{10,... | collective-permute-start | bytes 110600 | tf_op jit(solution)/shard_map/ppermute | solution.py:391
  81.0 7.9 %collective-permute-start.6 = (bf16[144,128]{1,0:T(8,128)(2,1)S(1)}, bf16[144,128]{1,0:T(8,128)(2,1)S(1)}, u32[]{:S(2)}, u32[]{:S(2)}) collective-permute-start(bf16[144,128]{1,0:T(8,128)(2,1)S(1)} %shard_map.109.a_ref), channel_id=1, source_target_pairs={{0,2},{1,3},{2,0},{3,1},{4,6},{5,7},{6,4},{7,5},{8,10},{9,11},{10,... | collective-permute-start | bytes 110600 | tf_op jit(solution)/shard_map/ppermute | solution.py:391
  82.5 6.4 %collective-permute-start.5 = (bf16[144,128]{1,0:T(8,128)(2,1)S(1)}, bf16[144,128]{1,0:T(8,128)(2,1)S(1)}, u32[]{:S(2)}, u32[]{:S(2)}) collective-permute-start(bf16[144,128]{1,0:T(8,128)(2,1)S(1)} %shard_map.109.a_ref), channel_id=1, source_target_pairs={{0,1},{1,0},{2,3},{3,2},{4,5},{5,4},{6,7},{7,6},{8,9},{9,8},{10,11... | collective-permute-start | bytes 110600 | tf_op jit(solution)/shard_map/ppermute | solution.py:391
  88.9 6.1 %collective-permute-start.10 = (bf16[144,128]{1,0:T(8,128)(2,1)S(1)}, bf16[144,128]{1,0:T(8,128)(2,1)S(1)}, u32[]{:S(2)}, u32[]{:S(2)}) collective-permute-start(bf16[144,128]{1,0:T(8,128)(2,1)S(1)} %shard_map.110.a_ref), channel_id=1, source_target_pairs={{0,12},{1,13},{2,14},{3,15},{4,8},{5,9},{6,10},{7,11},{8,4},{9,5},... | collective-permute-start | bytes 110600 | tf_op jit(solution)/shard_map/ppermute | solution.py:388
  90.3 5.8 %collective-permute-start.9 = (bf16[144,128]{1,0:T(8,128)(2,1)S(1)}, bf16[144,128]{1,0:T(8,128)(2,1)S(1)}, u32[]{:S(2)}, u32[]{:S(2)}) collective-permute-start(bf16[144,128]{1,0:T(8,128)(2,1)S(1)} %shard_map.110.a_ref), channel_id=1, source_target_pairs={{0,8},{1,9},{2,10},{3,11},{4,12},{5,13},{6,14},{7,15},{8,0},{9,1},... | collective-permute-start | bytes 110600 | tf_op jit(solution)/shard_map/ppermute | solution.py:388
  94.1 4.0 %collective-permute-start.8 = (bf16[144,128]{1,0:T(8,128)(2,1)S(1)}, bf16[144,128]{1,0:T(8,128)(2,1)S(1)}, u32[]{:S(2)}, u32[]{:S(2)}) collective-permute-start(bf16[144,128]{1,0:T(8,128)(2,1)S(1)} %shard_map.110.a_ref), channel_id=1, source_target_pairs={{0,4},{1,5},{2,6},{3,7},{4,0},{5,1},{6,2},{7,3},{8,12},{9,13},{10,... | collective-permute-start | bytes 110600 | tf_op jit(solution)/shard_map/ppermute | solution.py:388
